TPU v7x, 32 devices: a whole 2x2x4 slice. The times are simulated.
32 devices in a mesh: grp: 2 (over y), ctx: 4 (over x, core), head: 4 (over z).
Axes of the slice: x: 2, y: 2, z: 4, core: 2. Of those that a mesh axis runs over, the one named last changes fastest.
Arguments:
- prompt_hidden: bfloat16 [4, 1024, 4096], P('grp', 'ctx', 'head'), parts along dimension 0, may hold values from -3 to 3
- qkv_weight: bfloat16 [3, 4096, 4096], P(None, 'ctx', 'head'), may hold values from -0.09375 to 0.09375
- out_weight: bfloat16 [4096, 4096], P('head', 'ctx'), may hold values from -0.9375 to 0.9375
- embed_table: bfloat16 [32768, 4096], P('ctx', 'head'), may hold values from -60 to 60
- response_ids: int32 [4, 256], P(None, 'grp'), parts along dimension 1, may hold values from 0 to 32767
- assignment: int32 [256], P('grp'), parts along dimension 0, may hold values from 0 to 1
Outputs:
- final_hidden: bfloat16 [4, 256, 4096], P(None, ('grp', 'ctx'), 'head'), parts along dimension 1
There are 2 independent parts, one for each index of `grp`. A program takes and returns all parts, laid end to end along the dimension named above; an argument that names none is the same for every part. Nothing has to cross between parts.
All inputs are finite; a program needn't handle non-finite values.
Results may differ from a plain program's by a relative error of at most 0.023.
Values may be sent and summed in bfloat16 or wider, within the bound.
No kernel may reach another device: no remote copies, remote signals or barrier semaphores. Data moves between devices by JAX's collectives and lax.ppermute only.
A program may use at most 128 MiB of HBM per device.

v0:
```python
import jax
import jax.numpy as jnp
from jax import lax
from jax.sharding import PartitionSpec as P

DH = 128


def rms_rows(values):
    return values * lax.rsqrt(jnp.mean(values * values, axis=-1, keepdims=True) + 1e-06)


def on_device(prompt_hidden, qkv_weight, out_weight, embed_table, response_ids, assignment):
    local_cols = prompt_hidden.shape[2]
    prompt_rows = prompt_hidden.shape[1]
    head_size = DH
    local_heads = local_cols // head_size
    steps = response_ids.shape[0]
    resp_local = response_ids.shape[1] // lax.axis_size("ctx")
    ctx_index = lax.axis_index("ctx")
    full_rows = lax.all_gather(qkv_weight, "ctx", axis=1, tiled=True)
    kv_weight = jnp.concatenate([full_rows[1], full_rows[2]], axis=1)
    piece = lax.all_gather(prompt_hidden, "head", axis=2, tiled=True)
    flat_piece = piece.reshape(2 * prompt_rows, piece.shape[2])
    kv_local = jnp.dot(flat_piece, kv_weight, preferred_element_type=jnp.float32)
    kv_local = kv_local.astype(jnp.bfloat16).reshape(2, prompt_rows, 2, local_heads, head_size)
    partial_state = jnp.einsum(
        "pthd,pthe->phde", kv_local[:, :, 0], kv_local[:, :, 1], preferred_element_type=jnp.float32
    )
    state = lax.psum(partial_state.astype(jnp.bfloat16), "ctx").astype(jnp.float32)
    vocab_rows = embed_table.shape[0]
    offset_ids = response_ids - ctx_index * vocab_rows
    inside = (offset_ids >= 0) & (offset_ids < vocab_rows)
    looked = jnp.take(embed_table, jnp.clip(offset_ids, 0, vocab_rows - 1), axis=0)
    looked = jnp.where(inside[:, :, None], looked.astype(jnp.float32), 0.0)
    embedded_mine = lax.psum_scatter(
        looked.astype(jnp.bfloat16), "ctx", scatter_dimension=1, tiled=True
    )
    embedded = lax.all_gather(embedded_mine, "head", axis=2, tiled=True)
    normed = rms_rows(embedded.astype(jnp.float32)).astype(jnp.bfloat16)
    projected_qkv = jnp.einsum(
        "trd,kde->trke", normed, full_rows, preferred_element_type=jnp.float32
    ).astype(jnp.bfloat16)
    projected_qkv = projected_qkv.reshape(steps, resp_local, 3, local_heads, head_size)
    query = projected_qkv[:, :, 0]
    key = projected_qkv[:, :, 1]
    value = projected_qkv[:, :, 2]
    my_prompt = lax.dynamic_slice_in_dim(assignment, ctx_index * resp_local, resp_local, 0)
    query_f = query.astype(jnp.float32)
    both = jnp.einsum("trhd,phde->ptrhe", query_f, state, precision=lax.Precision.HIGHEST)
    chosen = jnp.where((my_prompt == 0)[None, :, None, None], both[0], both[1])
    scores = jnp.einsum("trhd,srhd->rhts", query, key, preferred_element_type=jnp.float32)
    later = jnp.arange(steps)[:, None] >= jnp.arange(steps)[None, :]
    scores = jnp.where(later[None, None], scores, 0.0).astype(jnp.bfloat16)
    local = jnp.einsum("rhts,srhd->trhd", scores, value, preferred_element_type=jnp.float32)
    head_out = rms_rows(chosen + local).astype(jnp.bfloat16).reshape(steps, resp_local, local_cols)
    terms = jnp.einsum(
        "trd,de->tre",
        head_out,
        lax.all_gather(out_weight, "ctx", axis=1, tiled=True),
        preferred_element_type=jnp.float32,
    )
    width = terms.shape[2]
    mine = lax.psum_scatter(
        terms.astype(jnp.bfloat16), "head", scatter_dimension=2, tiled=True
    ).astype(jnp.float32)
    mixed = embedded_mine.astype(jnp.float32) + mine
    squares = lax.psum(jnp.sum(mixed * mixed, axis=-1), "head")
    result = mixed * lax.rsqrt(squares[:, :, None] / width + 1e-06)
    return result.astype(jnp.bfloat16)


def solution(mesh):
    return jax.shard_map(
        on_device,
        mesh=mesh,
        in_specs=(
            P("grp", "ctx", "head"),
            P(None, "ctx", "head"),
            P("head", "ctx"),
            P("ctx", "head"),
            P(None, "grp"),
            P("grp"),
        ),
        out_specs=P(None, ("grp", "ctx"), "head"),
        check_vma=False,
    )
```

profile of v0, /device:TPU:0, one launch (start us, length us, event | category | flops | bytes accessed | tf_op | source)
XLA Modules:
  0.0 461.6 jit_solution(4606842393122182999)
XLA Ops:
  6.5 0.0 reduce-scatter.3.cloned.1.call-start
  6.5 0.7 compare_and_fusion.1
  7.2 0.7 fusion.41
  7.9 10.7 %gather_fusion = bf16[512,1024]{1,0:T(8,128)(2,1)S(1)} fusion(bf16[8192,1024]{1,0:T(8,128)(2,1)} %param.9, s32[1024]{0:T(1024)S(1)} %pad_clamp_fusion), kind=kCustom, calls=%fused_computation | custom fusion | bytes 2099200 | tf_op jit(solution)/shard_map/jit(_take)/gather | solution.py:34
  18.6 1.4 select_convert_fusion
  20.0 0.0 reduce-scatter.3.cloned.1.call-update
  20.0 0.0 all-gather.5.cloned.1.call-start
  20.0 0.7 all-gather.5.cloned.1.call-update
  20.7 0.0 all-gather.7.cloned.1.call-start
  20.8 0.7 all-gather.7.cloned.1.call-update
  21.5 0.0 all-gather.9.cloned.1.call-start
  21.5 26.2 %reduce-scatter.3.cloned.1.call-done = bf16[4,32,1024]{2,1,0:T(8,128)(2,1)} async-done(((bf16[4,128,1024]{2,1,0:T(8,128)(2,1)}), bf16[4,32,1024]{2,1,0:T(8,128)(2,1)}) %reduce-scatter.3.cloned.1.call-update) | async-done | bytes 262160 | tf_op jit(solution)/shard_map/reduce_scatter | solution.py:36
  47.7 0.0 all-gather.9.cloned.1.call-update
  47.8 0.2 all-reduce.2.cloned.1.call-start
  48.0 156.3 %all-gather.5.cloned.1.call-done = bf16[3,4096,1024]{2,1,0:T(8,128)(2,1)} async-done(((bf16[3,1024,1024]{2,1,0:T(8,128)(2,1)}), bf16[3,4096,1024]{2,1,0:T(8,128)(2,1)}) %all-gather.5.cloned.1.call-update) | async-done | bytes 25165840 | tf_op jit(solution)/shard_map/all_gather | solution.py:21
  204.2 11.8 %slice_bitcast_fusion.1 = (bf16[4096,1024]{1,0:T(8,128)(2,1)}, bf16[4096,1024]{1,0:T(8,128)(2,1)}) fusion(bf16[3,4096,1024]{2,1,0:T(8,128)(2,1)} %all-gather.5.cloned.1.call-done), kind=kLoop, calls=%fused_computation.8 | loop fusion | bytes 33554432 | tf_op jit(solution)/shard_map/squeeze | solution.py:22
  216.1 70.6 %all-gather.7.cloned.1.call-done = bf16[2,256,4096]{2,1,0:T(8,128)(2,1)} async-done(((bf16[2,256,1024]{2,1,0:T(8,128)(2,1)}), bf16[2,256,4096]{2,1,0:T(8,128)(2,1)}) %all-gather.7.cloned.1.call-update) | async-done | bytes 4194320 | tf_op jit(solution)/shard_map/all_gather | solution.py:23
  286.7 17.3 %fusion.14 = bf16[512,2048]{0,1:T(8,128)(2,1)} fusion(bf16[512,4096]{1,0:T(8,128)(2,1)} %bitcast.86, bf16[4096,1024]{1,0:T(8,128)(2,1)} %get-tuple-element.8, bf16[4096,1024]{1,0:T(8,128)(2,1)} %get-tuple-element.7), kind=kOutput, calls=%fused_computation.13 | convolution fusion | flops 8624537600 | bytes 23068672 | tf_op jit(solution)/shard_map/dot_general | solution.py:25
  304.0 0.0 copy-start.1
  304.0 2.6 reshape.52
  306.6 1.5 slice_bitcast_fusion.3
  308.1 1.3 convolution_convert_fusion
  309.3 0.0 all-reduce.2.cloned.1.call-update
  309.4 0.0 all-gather.11.cloned.1.call-start
  309.4 0.5 all-gather.11.cloned.1.call-update
  310.0 0.3 reduce-scatter.5.cloned.1.call-start
  310.2 0.0 copy-done.1
  310.2 0.1 dynamic-slice_compare_fusion
  310.3 4.4 all-gather.9.cloned.1.call-done
  314.7 1.5 fusion.17
  316.2 12.1 %fusion.19 = bf16[4,32,3,1024]{3,1,2,0:T(8,128)(2,1)S(1)} fusion(bf16[3,4096,1024]{2,1,0:T(8,128)(2,1)} %all-gather.5.cloned.1.call-done, bf16[4,32,4096]{2,1,0:T(8,128)(2,1)} %all-gather.9.cloned.1.call-done, f32[4,32]{1,0:T(4,128)S(1)} %add_rsqrt_fusion.2), kind=kOutput, calls=%fused_computation.19 | convolution fusion | flops 3223191552 | bytes 27001344 | tf_op jit(solution)/shard_map/trd,kde->trke/dot_general | solution.py:41
  328.3 0.2 copy.28
  328.5 0.2 fusion.45
  328.6 0.7 fusion.23
  329.4 0.0 copy-start
  329.4 20.3 %all-reduce.2.cloned.1.call-done = bf16[2,8,128,128]{3,2,0,1:T(8,128)(2,1)} async-done(((bf16[2,8,128,128]{3,2,0,1:T(8,128)(2,1)}), bf16[2,8,128,128]{3,2,0,1:T(8,128)(2,1)}) %all-reduce.2.cloned.1.call-update) | async-done | bytes 524304 | tf_op jit(solution)/shard_map/psum | solution.py:30
  349.7 1.3 convolution_bitcast_fusion
  351.1 0.4 multiply_reduce_fusion.1
  351.5 58.0 %all-gather.11.cloned.1.call-done = bf16[1024,4096]{1,0:T(8,128)(2,1)} async-done(((bf16[1024,1024]{1,0:T(8,128)(2,1)}), bf16[1024,4096]{1,0:T(8,128)(2,1)}) %all-gather.11.cloned.1.call-update) | async-done | bytes 8388624 | tf_op jit(solution)/shard_map/all_gather | solution.py:60
  409.5 5.7 %fusion.8 = bf16[4,32,4096]{2,1,0:T(8,128)(2,1)} fusion(bf16[1024,4096]{1,0:T(8,128)(2,1)} %all-gather.11.cloned.1.call-done, f32[4,32,8,128]{3,1,0,2:T(8,128)S(1)} %get-tuple-element.6, f32[4,32,8]{1,0,2:T(4,128)S(1)} %add_rsqrt_fusion), kind=kOutput, calls=%fused_computation.11 | convolution fusion | flops 1074528256 | bytes 9965568 | tf_op jit(solution)/shard_map/trd,de->tre/dot_general | solution.py:57
  415.2 0.0 reduce-scatter.5.cloned.1.call-update
  415.2 27.3 %reduce-scatter.5.cloned.1.call-done = bf16[4,32,1024]{2,1,0:T(8,128)(2,1)} async-done(((bf16[4,32,4096]{2,1,0:T(8,128)(2,1)}), bf16[4,32,1024]{2,1,0:T(8,128)(2,1)}) %reduce-scatter.5.cloned.1.call-update) | async-done | bytes 262160 | tf_op jit(solution)/shard_map/reduce_scatter | solution.py:64
  442.5 0.0 copy-done
  442.5 1.1 multiply_reduce_fusion
  443.6 9.4 %psum.15 = f32[4,32]{1,0:T(4,128)S(1)} all-reduce(f32[4,32]{1,0:T(4,128)S(1)} %multiply_reduce_fusion), channel_id=1, replica_groups=mesh['grp'=2,'ctx'=4,'head'=4] {'head'}, use_global_device_ids=true, to_apply=%region_6.7 | all-reduce | flops 128 | bytes 1024 | tf_op jit(solution)/shard_map/psum | solution.py:68
  453.0 1.8 multiply_convert_fusion
  (5 shorter events, 0.0 us)
Async XLA Ops:
  6.5 41.2 %reduce-scatter.3.cloned.1.call-start = ((), (), s32[]{:S(2)}) async-start(), calls=%async_computation.2 | async-start | bytes 1310720 | tf_op jit(solution)/shard_map/reduce_scatter | solution.py:36
  20.0 184.2 %all-gather.5.cloned.1.call-start = ((), (), s32[]{:S(2)}) async-start(), calls=%async_computation.3 | async-start | bytes 31457280 | tf_op jit(solution)/shard_map/all_gather | solution.py:21
  20.7 265.9 %all-gather.7.cloned.1.call-start = ((), (), s32[]{:S(2)}) async-start(), calls=%async_computation.4 | async-start | bytes 5242880 | tf_op jit(solution)/shard_map/all_gather | solution.py:23
  21.5 293.2 %all-gather.9.cloned.1.call-start = ((), (), s32[]{:S(2)}) async-start(), calls=%async_computation.6 | async-start | bytes 1310720 | tf_op jit(solution)/shard_map/all_gather | solution.py:39
  47.8 302.0 %all-reduce.2.cloned.1.call-start = ((), (), s32[]{:S(2)}) async-start(), calls=%async_computation.5 | async-start | bytes 1048576 | tf_op jit(solution)/shard_map/psum | solution.py:30
  304.0 6.2 %copy-start.1 = (s32[128]{0:T(128)S(1)}, s32[128]{0:T(128)}, u32[]{:S(2)}) copy-start(s32[128]{0:T(128)} %param.11) | copy-start | bytes 1540
  309.4 100.2 %all-gather.11.cloned.1.call-start = ((), (), s32[]{:S(2)}) async-start(), calls=%async_computation.7 | async-start | bytes 10485760 | tf_op jit(solution)/shard_map/all_gather | solution.py:60
  310.0 132.6 %reduce-scatter.5.cloned.1.call-start = ((), (), s32[]{:S(2)}) async-start(), calls=%async_computation.8 | async-start | bytes 1310720 | tf_op jit(solution)/shard_map/reduce_scatter | solution.py:64
  329.4 113.1 %copy-start = (bf16[4,32,1024]{2,1,0:T(8,128)(2,1)S(1)}, bf16[4,32,1024]{2,1,0:T(8,128)(2,1)}, u32[]{:S(2)}) copy-start(bf16[4,32,1024]{2,1,0:T(8,128)(2,1)} %reduce-scatter.3.cloned.1.call-done) | copy-start | bytes 786436
Sparse Core Ops, SparseCore 0:
  20.1 27.5 reduce-scatter.2
  49.4 154.8 all-gather.4
  205.9 80.7 all-gather.6
  288.2 26.4 all-gather.8
  317.0 32.6 all-reduce.1
  351.2 58.2 all-gather.10
  415.3 27.1 reduce-scatter.4
where the time goes:
time: 462 us
  waiting for transfers between devices  365 us (79%)
  matrix products  38.4 us (8%)
  local copies, waits for them, and re-layouts  26.9 us (6%)
  between operations  13.6 us (3%)
  blocking collectives  9.39 us (2%)
  other arithmetic  7.7 us (2%)
    all_gather x1, waiting for transfers between devices, on_device(): full_rows = lax.all_gather(qkv_weight, 'ctx', axis=1, tiled=True)  156 us
    all_gather x1, waiting for transfers between devices, on_device(): piece = lax.all_gather(prompt_hidden, 'head', axis=2, tiled=True)  70.6 us
    all_gather x1, waiting for transfers between devices, on_device(): lax.all_gather(out_weight, 'ctx', axis=1, tiled=True)  58 us
    reduce_scatter x1, waiting for transfers between devices, on_device(): lax.psum_scatter(terms.astype(jnp.bfloat16), 'head', scatter_dimension=2,...  27.3 us
    reduce_scatter x1, waiting for transfers between devices, on_device(): lax.psum_scatter(looked.astype(jnp.bfloat16), 'ctx', scatter_dimension=1,...  26.2 us
    psum x1, waiting for transfers between devices, on_device(): lax.psum(partial_state.astype(jnp.bfloat16), 'ctx').astype(jnp.float32)  20.3 us
    dot_general x1, matrix products, on_device(): jnp.dot(flat_piece, kv_weight, preferred_element_type=jnp.float32)  17.3 us
    dot_general x1, matrix products, on_device(): jnp.einsum('trd,kde->trke', normed, full_rows, preferred_element_type=jnp...  12.1 us
  transfers between devices with their start and end apart: 7, of which 7 were waited for; matrix products, arithmetic and copies ran while one was open for 11% of the time, Pallas kernels for 0%

commit v1 on v0

--- a/solution.py
+++ b/solution.py
@@ -1,16 +1,23 @@
+import functools
+
 import jax
 import jax.numpy as jnp
 from jax import lax
+from jax.experimental import pallas as pl
+from jax.experimental.pallas import tpu as pltpu
 from jax.sharding import PartitionSpec as P
 
 DH = 128
+F32 = jnp.float32
+BF16 = jnp.bfloat16
+VMEM_LIMIT = 48 * 1024 * 1024
 
 
 def rms_rows(values):
     return values * lax.rsqrt(jnp.mean(values * values, axis=-1, keepdims=True) + 1e-06)
 
 
-def on_device(prompt_hidden, qkv_weight, out_weight, embed_table, response_ids, assignment):
+def gathered_plan(prompt_hidden, qkv_weight, out_weight, embed_table, response_ids, assignment):
     local_cols = prompt_hidden.shape[2]
     prompt_rows = prompt_hidden.shape[1]
     head_size = DH
@@ -70,6 +77,400 @@
     return result.astype(jnp.bfloat16)
 
 
+def permute(array, axis, pairs):
+    return lax.ppermute(array, axis, pairs)
+
+
+def xor_pairs(count, mask):
+    return [(i, i ^ mask) for i in range(count)]
+
+
+def shift_pairs(count, by):
+    return [(i, (i + by) % count) for i in range(count)]
+
+
+def fetch_rows(meta, blocks, held, sems, parts):
+    depth = held.shape[2]
+    copies = []
+    for part in range(parts):
+        for k in range(len(blocks) // parts):
+            block = blocks[part * (len(blocks) // parts) + k]
+            rows = block.shape[0]
+            for s in range(2):
+                copies.append(
+                    pltpu.make_async_copy(
+                        block.at[:, pl.ds(s * depth, depth)],
+                        held.at[2 * meta[k] + s, pl.ds(part * rows, rows), :],
+                        sems.at[len(copies)],
+                    )
+                )
+    for copy in copies:
+        copy.start()
+    for copy in copies:
+        copy.wait()
+
+
+def weight_slices(own, sib, crossed, depth):
+    parts = [own[pl.ds(0, depth), :], own[pl.ds(depth, depth), :]]
+    parts += [sib[pl.ds(0, depth), :], sib[pl.ds(depth, depth), :]]
+    return parts + [ref[...] for ref in crossed]
+
+
+def slot_dot(meta, first, held, parts):
+    total = None
+    for i, part in enumerate(parts):
+        term = jnp.dot(held[meta[first + i]], part, preferred_element_type=F32)
+        total = term if total is None else total + term
+    return total
+
+
+def state_kernel(nblocks, meta, *refs):
+    blocks, refs = refs[:nblocks], refs[nblocks:]
+    key_own, value_own, key_sib, value_sib = refs[:4]
+    key_far, value_far = refs[4:8], refs[8:12]
+    out, rounded, held, sems = refs[12:]
+    depth = held.shape[2]
+
+    @pl.when(pl.program_id(0) == 0)
+    def _():
+        fetch_rows(meta, blocks, held, sems, 2)
+
+    first = nblocks // 2
+    keys = slot_dot(meta, first, held, weight_slices(key_own.at[0], key_sib.at[0], key_far, depth)).astype(BF16)
+    values = slot_dot(meta, first, held, weight_slices(value_own.at[0], value_sib.at[0], value_far, depth)).astype(BF16)
+    for head in range(out.shape[0]):
+        cols = slice(head * DH, (head + 1) * DH)
+        state = lax.dot_general(
+            keys[:, cols], values[:, cols], (((0,), (0,)), ((), ())), preferred_element_type=F32
+        )
+        out[head] = state
+        rounded[head] = state.astype(BF16)
+
+
+def project_kernel(nblocks, steps, meta, *refs):
+    blocks, refs = refs[:nblocks], refs[nblocks:]
+    own, sib = refs[:3], refs[3:6]
+    far = refs[6:10], refs[10:14], refs[14:18]
+    query_out, local_out, held, sems = refs[18:]
+    slots, rows, depth = held.shape
+
+    @pl.when(pl.program_id(0) == 0)
+    def _():
+        fetch_rows(meta, blocks, held, sems, 2)
+        squares = jnp.zeros((rows, 1), F32)
+        for i in range(slots):
+            part = held[i].astype(F32)
+            squares += jnp.sum(part * part, axis=-1, keepdims=True)
+        scale = lax.rsqrt(squares / (slots * depth) + 1e-06)
+        for i in range(slots):
+            held[i] = (held[i].astype(F32) * scale).astype(BF16)
+
+    first = nblocks // 2
+    query, key, value = (
+        slot_dot(meta, first, held, weight_slices(own[i].at[0], sib[i].at[0], far[i], depth)).astype(BF16)
+        for i in range(3)
+    )
+    query_out[...] = query
+    query, key, value = query.astype(F32), key.astype(F32), value.astype(F32)
+    each = rows // 2 // steps
+    for part in range(2):
+        for s in range(steps):
+            at_s = slice((part * steps + s) * each, (part * steps + s + 1) * each)
+            for head in range(query.shape[1] // DH):
+                cols = slice(head * DH, (head + 1) * DH)
+                total = None
+                for u in range(s + 1):
+                    at_u = slice((part * steps + u) * each, (part * steps + u + 1) * each)
+                    score = jnp.sum(query[at_s, cols] * key[at_u, cols], axis=-1, keepdims=True)
+                    term = score.astype(BF16).astype(F32) * value[at_u, cols]
+                    total = term if total is None else total + term
+                local_out[at_s, cols] = total
+
+
+def attend_kernel(query, local, chosen, state0, state1, other0, other1, out):
+    second = chosen[...] != 0
+    for head in range(state0.shape[0]):
+        cols = slice(head * DH, (head + 1) * DH)
+        q = query[:, cols]
+        both = []
+        for mine, other in ((state0, other0), (state1, other1)):
+            state = mine[head] + other[head].astype(F32)
+            high = state.astype(BF16)
+            low = (state - high.astype(F32)).astype(BF16)
+            both.append(
+                jnp.dot(q, high, preferred_element_type=F32) + jnp.dot(q, low, preferred_element_type=F32)
+            )
+        attended = jnp.where(second, both[1], both[0]) + local[:, cols]
+        out[:, cols] = rms_rows(attended).astype(BF16)
+
+
+def output_kernel(npieces, meta, heads_own, heads_sib, *refs):
+    pieces, refs = refs[:npieces], refs[npieces:]
+    outs, refs = refs[:4], refs[4:]
+    held, terms, sems = refs
+    rows, width = held.shape[1:]
+    core = meta[4]
+    copies = []
+    copies.append([pltpu.make_async_copy(pieces[0], held.at[0], sems.at[0])])
+    copies.append([pltpu.make_async_copy(pieces[1], held.at[1], sems.at[1])])
+    for j in (2, 3):
+        pair = []
+        for s in range(2):
+            i = 2 + (j - 2) * 2 + s
+            at = pl.multiple_of(meta[5 + s] * (rows // 2), rows // 2)
+            pair.append(pltpu.make_async_copy(pieces[i], held.at[j, pl.ds(at, rows // 2), :], sems.at[i]))
+        copies.append(pair)
+    for pair in copies:
+        for copy in pair:
+            copy.start()
+    half = rows // 2
+    own_at = pl.multiple_of(core * half, half)
+    sib_at = pl.multiple_of((1 - core) * half, half)
+    for j in range(4):
+        for copy in copies[j]:
+            copy.wait()
+        term = jnp.dot(heads_own[...], held[j, pl.ds(own_at, half), :], preferred_element_type=F32)
+        term += jnp.dot(heads_sib[...], held[j, pl.ds(sib_at, half), :], preferred_element_type=F32)
+        terms[meta[j]] = term
+    for k in range(4):
+        outs[k][...] = terms[k].astype(outs[k].dtype)
+
+
+def anywhere(count):
+    return [pl.BlockSpec(memory_space=pl.ANY)] * count
+
+
+def permuted_plan(prompt_hidden, qkv_weight, out_weight, embed_table, response_ids, assignment):
+    grp, ctx, head = lax.axis_index("grp"), lax.axis_index("ctx"), lax.axis_index("head")
+    nctx, nhead = lax.axis_size("ctx"), lax.axis_size("head")
+    core, chip = ctx % 2, ctx // 2
+    to_sib, to_far, to_diag = xor_pairs(nctx, 1), xor_pairs(nctx, 2), xor_pairs(nctx, 3)
+    over_grp = xor_pairs(2, 1)
+    ring = shift_pairs(nhead, 1)
+    prompts, prompt_rows, block = prompt_hidden.shape
+    depth = block // 2
+    cols = qkv_weight.shape[2] // 2
+    steps = response_ids.shape[0]
+    resp_local = response_ids.shape[1] // nctx
+    rows_local = steps * resp_local
+
+    def half_slice(k, col_half):
+        return lax.dynamic_slice(qkv_weight, (k, grp * depth, col_half * cols), (1, depth, cols))[0]
+
+    order = [(k, mask) for k in (1, 2) for mask in (2, 3)]
+    sent = lax.optimization_barrier(
+        tuple(half_slice(k, core if mask == 2 else 1 - core) for k, mask in order)
+    )
+    crossed = {}
+    for (k, mask), part in zip(order, sent):
+        got = permute(part, "ctx", to_far if mask == 2 else to_diag)
+        crossed[k, mask] = (got, permute(got, "grp", over_grp))
+    sib_weight = permute(
+        lax.dynamic_slice(qkv_weight, (0, 0, (1 - core) * cols), (3, block, cols)), "ctx", to_sib
+    )
+
+    own_blocks, sib_blocks = [], []
+    for p in range(prompts):
+        moving = prompt_hidden[p]
+        own, sib = [moving], [permute(moving, "ctx", to_sib)]
+        for _ in range(nhead - 1):
+            moving = permute(moving, "head", ring)
+            own.append(moving)
+            sib.append(permute(moving, "ctx", to_sib))
+        own_blocks.append(own)
+        sib_blocks.append(sib)
+
+    vocab_rows = embed_table.shape[0]
+    offset_ids = response_ids - ctx * vocab_rows
+    inside = (offset_ids >= 0) & (offset_ids < vocab_rows)
+    looked = jnp.take(embed_table, jnp.clip(offset_ids, 0, vocab_rows - 1), axis=0)
+    looked = jnp.where(inside[:, :, None], looked, jnp.zeros((), BF16))
+    looked = looked.reshape(steps, nctx // 2, 2, resp_local, block)
+    kept = lax.dynamic_index_in_dim(looked, core, 2, keepdims=False)
+    given = lax.dynamic_index_in_dim(looked, 1 - core, 2, keepdims=False)
+    kept = kept + permute(given, "ctx", to_sib)
+    mine = lax.dynamic_index_in_dim(kept, chip, 1, keepdims=False)
+    given = lax.dynamic_index_in_dim(kept, 1 - chip, 1, keepdims=False)
+    embedded = (mine + permute(given, "ctx", to_far)).reshape(rows_local, block)
+    moving = embedded
+    own_rows, sib_rows = [moving], [permute(moving, "ctx", to_sib)]
+    for _ in range(nhead - 1):
+        moving = permute(moving, "head", ring)
+        own_rows.append(moving)
+        sib_rows.append(permute(moving, "ctx", to_sib))
+
+    for mask in (2, 3):
+        part = half_slice(0, core if mask == 2 else 1 - core)
+        part, _ = lax.optimization_barrier((part, given))
+        got = permute(part, "ctx", to_far if mask == 2 else to_diag)
+        crossed[0, mask] = (got, permute(got, "grp", over_grp))
+    out_sib = permute(out_weight, "ctx", to_sib)
+    part = lax.dynamic_slice(out_weight, (grp * depth, 0), (depth, out_weight.shape[1]))
+    part, _ = lax.optimization_barrier((part, crossed[2, 3][0]))
+    got = permute(part, "ctx", to_far)
+    out_far = (got, permute(got, "grp", over_grp))
+    out_diag = tuple(permute(piece, "ctx", to_sib) for piece in out_far)
+
+    slots = [(head - k) % nhead for k in range(nhead)]
+    for j in range(nctx):
+        if j < 2:
+            slots += [2 * (ctx ^ j), 2 * (ctx ^ j) + 1]
+        else:
+            slots += [2 * (ctx ^ j) + grp, 2 * (ctx ^ j) + 1 - grp]
+    meta = jnp.stack(slots + [core]).astype(jnp.int32)
+    at_core = len(slots)
+    wide = 2 * DH
+    nsteps = cols // wide
+
+    def own_spec(k):
+        return pl.BlockSpec((1, block, wide), lambda n, m: (k, 0, m[at_core] * nsteps + n))
+
+    def sib_spec(k):
+        return pl.BlockSpec((1, block, wide), lambda n, m: (k, 0, n))
+
+    far_spec = pl.BlockSpec((depth, wide), lambda n, m: (0, n))
+    far_of = lambda k: [*crossed[k, 2], *crossed[k, 3]]
+    nblocks = 2 * nhead
+    heads_here = cols // DH
+    tokens = 2 * prompt_rows
+
+    states, rounded = [], []
+    for p in range(prompts):
+        state_spec = pl.BlockSpec((2, DH, DH), lambda n, m: (n, 0, 0))
+        state, low = pl.pallas_call(
+            functools.partial(state_kernel, nblocks),
+            out_shape=(
+                jax.ShapeDtypeStruct((heads_here, DH, DH), F32),
+                jax.ShapeDtypeStruct((heads_here, DH, DH), BF16),
+            ),
+            grid_spec=pltpu.PrefetchScalarGridSpec(
+                num_scalar_prefetch=1,
+                grid=(nsteps,),
+                in_specs=anywhere(nblocks)
+                + [own_spec(1), own_spec(2), sib_spec(1), sib_spec(2)]
+                + [far_spec] * 8,
+                out_specs=(state_spec, state_spec),
+                scratch_shapes=[
+                    pltpu.VMEM((2 * nhead, tokens, depth), BF16),
+                    pltpu.SemaphoreType.DMA((2 * nblocks,)),
+                ],
+            ),
+            compiler_params=pltpu.CompilerParams(vmem_limit_bytes=VMEM_LIMIT),
+            cost_estimate=pl.CostEstimate(
+                flops=4 * tokens * nhead * block * cols, bytes_accessed=12 * 1024 * 1024, transcendentals=0
+            ),
+            name="prompt_state",
+        )(
+            meta,
+            *own_blocks[p],
+            *sib_blocks[p],
+            qkv_weight,
+            qkv_weight,
+            sib_weight,
+            sib_weight,
+            *far_of(1),
+            *far_of(2),
+        )
+        states.append(state)
+        rounded.append(permute(low, "ctx", to_far))
+
+    chip_rows = 2 * rows_local
+    row_spec = pl.BlockSpec((chip_rows, wide), lambda n, m: (0, n))
+    query, local = pl.pallas_call(
+        functools.partial(project_kernel, nblocks, steps),
+        out_shape=(
+            jax.ShapeDtypeStruct((chip_rows, cols), BF16),
+            jax.ShapeDtypeStruct((chip_rows, cols), F32),
+        ),
+        grid_spec=pltpu.PrefetchScalarGridSpec(
+            num_scalar_prefetch=1,
+            grid=(nsteps,),
+            in_specs=anywhere(nblocks)
+            + [own_spec(0), own_spec(1), own_spec(2), sib_spec(0), sib_spec(1), sib_spec(2)]
+            + [far_spec] * 12,
+            out_specs=(row_spec, row_spec),
+            scratch_shapes=[
+                pltpu.VMEM((2 * nhead, chip_rows, depth), BF16),
+                pltpu.SemaphoreType.DMA((2 * nblocks,)),
+            ],
+        ),
+        compiler_params=pltpu.CompilerParams(vmem_limit_bytes=VMEM_LIMIT),
+        cost_estimate=pl.CostEstimate(
+            flops=6 * chip_rows * nhead * block * cols, bytes_accessed=14 * 1024 * 1024, transcendentals=0
+        ),
+        name="response_rows",
+    )(
+        meta,
+        *own_rows,
+        *sib_rows,
+        *([qkv_weight] * 3),
+        *([sib_weight] * 3),
+        *far_of(0),
+        *far_of(1),
+        *far_of(2),
+    )
+
+    which = [
+        jnp.tile(lax.dynamic_slice_in_dim(assignment, owner * resp_local, resp_local, 0), steps)
+        for owner in (ctx, ctx ^ 1)
+    ]
+    heads_out = pl.pallas_call(
+        attend_kernel,
+        out_shape=jax.ShapeDtypeStruct((chip_rows, cols), BF16),
+        compiler_params=pltpu.CompilerParams(vmem_limit_bytes=VMEM_LIMIT),
+        name="attend",
+    )(query, local, jnp.concatenate(which)[:, None], *states, *rounded)
+
+    heads_own = heads_out[:rows_local]
+    heads_sib = permute(heads_out[rows_local:], "ctx", to_sib)
+
+    away = [((ctx ^ j) - head) % nhead for j in range(nctx)]
+    out_meta = jnp.stack(away + [core, grp, 1 - grp]).astype(jnp.int32)
+    width = out_weight.shape[1]
+    whole = pl.BlockSpec((rows_local, cols), lambda i, m: (0, 0))
+    term_spec = pl.BlockSpec((rows_local, width), lambda i, m: (0, 0))
+    terms = pl.pallas_call(
+        functools.partial(output_kernel, 6),
+        out_shape=(jax.ShapeDtypeStruct((rows_local, width), F32),)
+        + (jax.ShapeDtypeStruct((rows_local, width), BF16),) * 3,
+        grid_spec=pltpu.PrefetchScalarGridSpec(
+            num_scalar_prefetch=1,
+            grid=(1,),
+            in_specs=[whole, whole] + anywhere(6),
+            out_specs=(term_spec,) * 4,
+            scratch_shapes=[
+                pltpu.VMEM((nctx, block, width), BF16),
+                pltpu.VMEM((nctx, rows_local, width), F32),
+                pltpu.SemaphoreType.DMA((6,)),
+            ],
+        ),
+        compiler_params=pltpu.CompilerParams(vmem_limit_bytes=VMEM_LIMIT),
+        name="output_terms",
+    )(out_meta, heads_own, heads_sib, out_weight, out_sib, *out_far, *out_diag)
+    mixed = embedded.astype(F32) + terms[0]
+    for k in range(1, nhead):
+        mixed = mixed + permute(terms[k], "head", shift_pairs(nhead, k)).astype(F32)
+    squares = lax.psum(jnp.sum(mixed * mixed, axis=-1, keepdims=True), "head")
+    result = mixed * lax.rsqrt(squares / (nhead * width) + 1e-06)
+    return result.astype(BF16).reshape(steps, resp_local, width)
+
+
+def on_device(prompt_hidden, qkv_weight, out_weight, embed_table, response_ids, assignment):
+    nctx, nhead = lax.axis_size("ctx"), lax.axis_size("head")
+    local_heads = qkv_weight.shape[2] // DH
+    fits = (
+        lax.axis_size("grp") == 2
+        and nctx == 4
+        and nhead == 4
+        and prompt_hidden.shape[0] == 2
+        and local_heads % 4 == 0
+        and prompt_hidden.shape[1] % 16 == 0
+        and (response_ids.shape[1] // nctx) % 16 == 0
+    )
+    plan = permuted_plan if fits else gathered_plan
+    return plan(prompt_hidden, qkv_weight, out_weight, embed_table, response_ids, assignment)
+
+
 def solution(mesh):
     return jax.shard_map(
         on_device,

time: 462 us -> 269 us (0.58)
  waiting for transfers between devices: 365 us -> 142 us
  starting transfers between devices: 0.64 us -> 41.3 us
  matrix products: 38.4 us -> 0 us
  Pallas kernels: 0 us -> 34.5 us
  between operations: 13.6 us -> 0.49 us
  local copies, waits for them, and re-layouts: 26.9 us -> 31.6 us
    all_gather x4 -> x0, waiting for transfers between devices: 289 us -> none  [the longest x1 156 us: on_device(): full_rows = lax.all_gather(qkv_weight, 'ctx', axis=1, tiled=True)]
    ppermute x0 -> x47, waiting for transfers between devices: none -> 142 us  [permute(): return lax.ppermute(array, axis, pairs)]
    reduce_scatter x2 -> x0, waiting for transfers between devices: 53.5 us -> none  [the longest x1 27.3 us: on_device(): lax.psum_scatter(terms.astype(jnp.bfloat16), 'head', scatter_dimension=2,...]
    ppermute x0 -> x47, starting transfers between devices: none -> 41.3 us  [permute(): return lax.ppermute(array, axis, pairs)]
    dot_general x6 -> x0, matrix products: 38.4 us -> none  [the longest x1 17.3 us: on_device(): jnp.dot(flat_piece, kv_weight, preferred_element_type=jnp.float32)]
    pallas_call x0 -> x5, Pallas kernels: none -> 34.5 us  [the longest x2 19.5 us: permuted_plan(): pl.pallas_call(functools.partial(state_kernel, nblocks), out_shape=(jax.S...]
    psum x1 -> x0, waiting for transfers between devices: 20.3 us -> none  [on_device(): lax.psum(partial_state.astype(jnp.bfloat16), 'ctx').astype(jnp.float32)]
    unnamed x5 -> x56, local copies, waits for them, and re-layouts: 0.18 us -> 8.51 us
  transfers between devices with their start and end apart: 7 -> 47, of which waited for: 7 -> 19; matrix products, arithmetic and copies ran while one was open for 11% -> 9% of each run, Pallas kernels for 0% -> 11%
where the time goes in v1:
time: 269 us; the launch traced here: 268 us
  waiting for transfers between devices  142 us (53%)
  starting transfers between devices  41.3 us (15%)
  Pallas kernels  34.5 us (13%)
  local copies, waits for them, and re-layouts  31.6 us (12%)
  blocking collectives  13.8 us (5%)
  other arithmetic  4.58 us (2%)
    ppermute x47, waiting for transfers between devices, permute(): return lax.ppermute(array, axis, pairs)  142 us
    ppermute x47, starting transfers between devices, permute(): return lax.ppermute(array, axis, pairs)  41.3 us
    pallas_call x2, Pallas kernels, permuted_plan(): pl.pallas_call(functools.partial(state_kernel, nblocks), out_shape=(jax.S...  19.5 us
    psum x1, blocking collectives, permuted_plan(): squares = lax.psum(jnp.sum(mixed * mixed, axis=-1, keepdims=True), 'head')  13.8 us
    gather x1, local copies, waits for them, and re-layouts, permuted_plan(): jnp.take(embed_table, jnp.clip(offset_ids, 0, vocab_rows - 1), axis=0)  10.7 us
    pallas_call x1, Pallas kernels, permuted_plan(): pl.pallas_call(functools.partial(project_kernel, nblocks, steps), out_sha...  10.1 us
    unnamed x56, local copies, waits for them, and re-layouts  8.51 us
  transfers between devices with their start and end apart: 47, of which 19 were waited for; matrix products, arithmetic and copies ran while one was open for 9% of the time, Pallas kernels for 11%

profile of v1, /device:TPU:0, one launch (start us, length us, event | category | flops | bytes accessed | tf_op | source)
XLA Modules:
  0.0 268.3 jit_solution(4682353371892094999)
XLA Ops:
  0.0 3.4 %dynamic-slice_bitcast_fusion = (bf16[512,512]{1,0:T(8,128)(2,1)}, bf16[512,512]{1,0:T(8,128)(2,1)}, bf16[512,512]{1,0:T(8,128)(2,1)S(1)}, bf16[512,512]{1,0:T(8...) fusion(bf16[3,1024,1024]{2,1,0:T(8,128)(2,1)} %refs_9_.5, s32[]{:T(128)S(6)} %select_n.116, ...), kind=kLoop, calls=%fused_computation.9 | loop fusion | bytes 6291468 | tf_op jit(solution)/shard_map/squeeze | solution.py:258
  3.4 2.9 %collective-permute-start.14 = (bf16[512,512]{1,0:T(8,128)(2,1)}, bf16[512,512]{1,0:T(8,128)(2,1)S(1)}, u32[]{:S(2)}, u32[]{:S(2)}) collective-permute-start(bf16[512,512]{1,0:T(8,128)(2,1)} %get-tuple-element.24), channel_id=1, source_target_pairs={{0,8},{4,12},{8,0},{12,4},{1,9},{5,13},{9,1},{13,5},{2,10},{6,14},... | collective-permute-start | bytes 1572872 | tf_op jit(solution)/shard_map/ppermute | solution.py:81
  6.3 1.2 collective-permute-start.18
  8.3 10.7 %gather_fusion = bf16[512,1024]{1,0:T(8,128)(2,1)S(1)} fusion(bf16[8192,1024]{1,0:T(8,128)(2,1)} %param.9, s32[1024]{0:T(1024)S(1)} %pad_clamp_fusion), kind=kCustom, calls=%fused_computation | custom fusion | bytes 2099200 | tf_op jit(solution)/shard_map/jit(_take)/gather | solution.py:286
  19.0 1.2 fusion
  20.2 1.9 dynamic-slice_bitcast_fusion.6
  22.5 1.3 slice_bitcast_fusion
  23.8 1.6 collective-permute-start.29
  25.4 4.7 %collective-permute-done.16.refs_20_.refs_14_ = bf16[512,512]{1,0:T(8,128)(2,1)S(1)} collective-permute-done((bf16[512,512]{1,0:T(8,128)(2,1)S(1)}, bf16[512,512]{1,0:T(8,128)(2,1)S(1)}, u32[]{:S(2)}, u32[]{:S(2)}) %collective-permute-start.16) | collective-permute-done | bytes 524320 | tf_op jit(solution)/shard_map/ppermute | solution.py:81
  30.7 11.0 %collective-permute-done.18.refs_22_.refs_16_ = bf16[512,512]{1,0:T(8,128)(2,1)S(1)} collective-permute-done((bf16[512,512]{1,0:T(8,128)(2,1)}, bf16[512,512]{1,0:T(8,128)(2,1)S(1)}, u32[]{:S(2)}, u32[]{:S(2)}) %collective-permute-start.18) | collective-permute-done | bytes 524320 | tf_op jit(solution)/shard_map/ppermute | solution.py:81
  41.8 2.1 collective-permute-start.22
  43.9 3.8 %constant_dynamic-slice_fusion.1 = bf16[3,1024,512]{2,1,0:T(8,128)(2,1)} fusion(bf16[3,1024,1024]{2,1,0:T(8,128)(2,1)} %refs_9_.5, s32[]{:T(128)S(6)} %select_n.115), kind=kLoop, calls=%fused_computation.21 | loop fusion | bytes 6291460 | tf_op jit(solution)/shard_map/dynamic_slice | solution.py:269
  47.7 3.8 %collective-permute-done.20.refs_24_.refs_18_ = bf16[512,512]{1,0:T(8,128)(2,1)} collective-permute-done((bf16[512,512]{1,0:T(8,128)(2,1)}, bf16[512,512]{1,0:T(8,128)(2,1)}, u32[]{:S(2)}, u32[]{:S(2)}) %collective-permute-start.20) | collective-permute-done | bytes 524320 | tf_op jit(solution)/shard_map/ppermute | solution.py:81
  52.4 1.8 collective-permute-start.15
  54.2 1.1 bitcast_add_fusion
  55.9 1.6 collective-permute-start.1
  58.4 1.5 collective-permute-start.19
  59.9 4.3 %collective-permute-done.1 = bf16[4,32,1024]{2,1,0:T(8,128)(2,1)S(1)} collective-permute-done((bf16[4,32,1024]{2,1,0:T(8,128)(2,1)S(1)}, bf16[4,32,1024]{2,1,0:T(8,128)(2,1)S(1)}, u32[]{:S(2)}, u32[]{:S(2)}) %collective-permute-start.1) | collective-permute-done | bytes 262176 | tf_op jit(solution)/shard_map/ppermute | solution.py:81
  64.2 1.7 collective-permute-start.21
  65.9 1.2 collective-permute-done.15.refs_19_.refs_13_
  67.2 1.8 collective-permute-start.30
  69.0 9.4 %collective-permute-done.17.refs_21_.refs_15_ = bf16[512,512]{1,0:T(8,128)(2,1)S(1)} collective-permute-done((bf16[512,512]{1,0:T(8,128)(2,1)S(1)}, bf16[512,512]{1,0:T(8,128)(2,1)S(1)}, u32[]{:S(2)}, u32[]{:S(2)}) %collective-permute-start.17) | collective-permute-done | bytes 524320 | tf_op jit(solution)/shard_map/ppermute | solution.py:81
  78.4 11.2 %collective-permute-done.19.refs_23_.refs_17_ = bf16[512,512]{1,0:T(8,128)(2,1)S(1)} collective-permute-done((bf16[512,512]{1,0:T(8,128)(2,1)}, bf16[512,512]{1,0:T(8,128)(2,1)S(1)}, u32[]{:S(2)}, u32[]{:S(2)}) %collective-permute-start.19) | collective-permute-done | bytes 524320 | tf_op jit(solution)/shard_map/ppermute | solution.py:81
  89.6 1.8 collective-permute-start.23
  91.5 8.6 %collective-permute-done.21.refs_25_.refs_19_ = bf16[512,512]{1,0:T(8,128)(2,1)S(1)} collective-permute-done((bf16[512,512]{1,0:T(8,128)(2,1)}, bf16[512,512]{1,0:T(8,128)(2,1)S(1)}, u32[]{:S(2)}, u32[]{:S(2)}) %collective-permute-start.21) | collective-permute-done | bytes 524320 | tf_op jit(solution)/shard_map/ppermute | solution.py:81
  100.0 1.8 collective-permute-start.10
  104.2 1.4 collective-permute-start.2
  105.9 1.3 constant_dynamic-slice_fusion
  107.2 7.9 %collective-permute-done.10.refs_14_ = bf16[512,512]{1,0:T(8,128)(2,1)S(1)} collective-permute-done((bf16[512,512]{1,0:T(8,128)(2,1)}, bf16[512,512]{1,0:T(8,128)(2,1)S(1)}, u32[]{:S(2)}, u32[]{:S(2)}) %collective-permute-start.10) | collective-permute-done | bytes 524320 | tf_op jit(solution)/shard_map/ppermute | solution.py:81
  115.1 1.7 collective-permute-start.40
  116.8 8.9 %collective-permute-done.12.refs_16_ = bf16[512,512]{1,0:T(8,128)(2,1)} collective-permute-done((bf16[512,512]{1,0:T(8,128)(2,1)}, bf16[512,512]{1,0:T(8,128)(2,1)}, u32[]{:S(2)}, u32[]{:S(2)}) %collective-permute-start.12) | collective-permute-done | bytes 524320 | tf_op jit(solution)/shard_map/ppermute | solution.py:81
  125.6 1.7 collective-permute-start.31
  127.3 1.6 collective-permute-start.3
  130.4 17.6 %collective-permute-done.3.refs_2_ = bf16[128,1024]{1,0:T(8,128)(2,1)} collective-permute-done((bf16[128,1024]{1,0:T(8,128)(2,1)S(1)}, bf16[128,1024]{1,0:T(8,128)(2,1)}, u32[]{:S(2)}, u32[]{:S(2)}) %collective-permute-start.3) | collective-permute-done | bytes 262176 | tf_op jit(solution)/shard_map/ppermute | solution.py:81
  151.0 1.5 collective-permute-start.11
  152.5 12.7 %collective-permute-done.24.refs_3_ = bf16[256,1024]{1,0:T(8,128)(2,1)} collective-permute-done((bf16[256,1024]{1,0:T(8,128)(2,1)}, bf16[256,1024]{1,0:T(8,128)(2,1)}, u32[]{:S(2)}, u32[]{:S(2)}) %collective-permute-start.24) | collective-permute-done | bytes 524320 | tf_op jit(solution)/shard_map/ppermute | solution.py:81
  165.2 1.5 collective-permute-start.41
  172.3 9.7 %prompt_state.3 = (f32[4,128,128]{2,1,0:T(8,128)S(1)}, bf16[4,128,128]{2,1,0:T(8,128)(2,1)S(1)}) custom-call(s32[13]{0:T(128)S(1)} %stack.84.meta, bf16[256,1024]{1,0:T(8,128)(2,1)S(1)} %get-tuple-element.45.refs_0_, bf16[256,1024]{1,0:T(8,128)(2,1)} %collective-permute-done.29.refs_1_, bf16[256,1024]{1,0:T(8,128)(2,1)} %collective-permute-done.30.refs_2_, ...), custom_call_target="tpu_custom_call" | custom-call | flops 4294967296 | bytes 12582912 | tf_op jit(solution)/shard_map/prompt_state/pallas_call | solution.py:340
  182.0 20.4 %collective-permute-done.13.refs_17_ = bf16[512,512]{1,0:T(8,128)(2,1)} collective-permute-done((bf16[512,512]{1,0:T(8,128)(2,1)}, bf16[512,512]{1,0:T(8,128)(2,1)}, u32[]{:S(2)}, u32[]{:S(2)}) %collective-permute-start.13) | collective-permute-done | bytes 524320 | tf_op jit(solution)/shard_map/ppermute | solution.py:81
  203.4 9.9 %prompt_state.2 = (f32[4,128,128]{2,1,0:T(8,128)S(1)}, bf16[4,128,128]{2,1,0:T(8,128)(2,1)S(1)}) custom-call(s32[13]{0:T(128)S(1)} %stack.84.meta, bf16[256,1024]{1,0:T(8,128)(2,1)S(1)} %get-tuple-element.46.refs_0_, bf16[256,1024]{1,0:T(8,128)(2,1)} %collective-permute-done.22.refs_1_, bf16[256,1024]{1,0:T(8,128)(2,1)} %collective-permute-done.23.refs_2_, ...), custom_call_target="tpu_custom_call" | custom-call | flops 4294967296 | bytes 12582912 | tf_op jit(solution)/shard_map/prompt_state/pallas_call | solution.py:340
  213.3 1.6 collective-permute-start.37
  215.4 10.1 %response_rows.1 = (bf16[256,512]{1,0:T(8,128)(2,1)S(1)}, f32[256,512]{1,0:T(8,128)S(1)}) custom-call(s32[13]{0:T(128)S(1)} %stack.84.meta, bf16[128,1024]{1,0:T(8,128)(2,1)S(1)} %bitcast.59, bf16[128,1024]{1,0:T(8,128)(2,1)S(1)} %copy-done.14, bf16[128,1024]{1,0:T(8,128)(2,1)} %collective-permute-done.3.refs_2_, ...), custom_call_target="tpu_custom_call" | custom-call | flops 3221225472 | bytes 14680064 | tf_op jit(solution)/shard_map/response_rows/pallas_call | solution.py:379
  226.3 1.2 collective-permute-done.38.heads_sib
  227.5 4.4 %output_terms.1 = (f32[128,1024]{1,0:T(8,128)S(1)}, bf16[128,1024]{1,0:T(8,128)(2,1)S(1)}, bf16[128,1024]{1,0:T(8,128)(2,1)S(1)}, bf16[128,1024]{1,0:T(8,128)(2,1)S(1)}) custom-call(s32[7]{0:T(128)S(1)} %stack.71.meta, bf16[128,512]{1,0:T(8,128)(2,1)S(1)} %get-tuple-element.48.heads_own, bf16[128,512]{1,0:T(8,128)(2,1)S(1)} %collective-permute-done.38.heads_sib, ...), custom_call_target="tpu_custom_call" | custom-call | tf_op jit(solution)/shard_map/output_terms/pallas_call | solution.py:432
  232.4 3.3 %collective-permute-start.46 = (bf16[128,1024]{1,0:T(8,128)(2,1)S(1)}, bf16[128,1024]{1,0:T(8,128)(2,1)S(1)}, u32[]{:S(2)}, u32[]{:S(2)}) collective-permute-start(bf16[128,1024]{1,0:T(8,128)(2,1)S(1)} %get-tuple-element.38), channel_id=1, source_target_pairs={{0,3},{1,0},{2,1},{3,2},{4,7},{5,4},{6,5},{7,6},{8,11},{9,8},{10,9... | collective-permute-start | bytes 786440 | tf_op jit(solution)/shard_map/ppermute | solution.py:81
  235.8 7.3 %collective-permute-done.44 = bf16[128,1024]{1,0:T(8,128)(2,1)S(1)} collective-permute-done((bf16[128,1024]{1,0:T(8,128)(2,1)S(1)}, bf16[128,1024]{1,0:T(8,128)(2,1)S(1)}, u32[]{:S(2)}, u32[]{:S(2)}) %collective-permute-start.44) | collective-permute-done | bytes 262176 | tf_op jit(solution)/shard_map/ppermute | solution.py:81
  243.0 10.3 %collective-permute-done.45 = bf16[128,1024]{1,0:T(8,128)(2,1)S(1)} collective-permute-done((bf16[128,1024]{1,0:T(8,128)(2,1)S(1)}, bf16[128,1024]{1,0:T(8,128)(2,1)S(1)}, u32[]{:S(2)}, u32[]{:S(2)}) %collective-permute-start.45) | collective-permute-done | bytes 262176 | tf_op jit(solution)/shard_map/ppermute | solution.py:81
  253.6 13.8 %psum.7 = f32[128,1]{0,1:T(1,128)S(1)} all-reduce(f32[128,1]{0,1:T(1,128)S(1)} %bitcast.62), channel_id=1, replica_groups=mesh['grp'=2,'ctx'=4,'head'=4] {'head'}, use_global_device_ids=true, to_apply=%region_1.2 | all-reduce | flops 128 | bytes 1024 | tf_op jit(solution)/shard_map/psum | solution.py:453
  (138 shorter events, 20.7 us)
Async XLA Ops:
  3.4 20.4 %collective-permute-start.14 = (bf16[512,512]{1,0:T(8,128)(2,1)}, bf16[512,512]{1,0:T(8,128)(2,1)S(1)}, u32[]{:S(2)}, u32[]{:S(2)}) collective-permute-start(bf16[512,512]{1,0:T(8,128)(2,1)} %get-tuple-element.24), channel_id=1, source_target_pairs={{0,8},{4,12},{8,0},{12,4},{1,9},{5,13},{9,1},{13,5},{2,10},{6,14},... | collective-permute-start | bytes 1572872 | tf_op jit(solution)/shard_map/ppermute | solution.py:81
  6.3 23.8 %collective-permute-start.16 = (bf16[512,512]{1,0:T(8,128)(2,1)S(1)}, bf16[512,512]{1,0:T(8,128)(2,1)S(1)}, u32[]{:S(2)}, u32[]{:S(2)}) collective-permute-start(bf16[512,512]{1,0:T(8,128)(2,1)S(1)} %get-tuple-element.25), channel_id=1, source_target_pairs={{0,12},{4,8},{8,4},{12,0},{1,13},{5,9},{9,5},{13,1},{2,14},{6,10},... | collective-permute-start | bytes 1572872 | tf_op jit(solution)/shard_map/ppermute | solution.py:81
  6.3 35.4 %collective-permute-start.18 = (bf16[512,512]{1,0:T(8,128)(2,1)}, bf16[512,512]{1,0:T(8,128)(2,1)S(1)}, u32[]{:S(2)}, u32[]{:S(2)}) collective-permute-start(bf16[512,512]{1,0:T(8,128)(2,1)} %get-tuple-element.26), channel_id=1, source_target_pairs={{0,8},{4,12},{8,0},{12,4},{1,9},{5,13},{9,1},{13,5},{2,10},{6,14},... | collective-permute-start | bytes 1572872 | tf_op jit(solution)/shard_map/ppermute | solution.py:81
  7.5 44.0 %collective-permute-start.20 = (bf16[512,512]{1,0:T(8,128)(2,1)}, bf16[512,512]{1,0:T(8,128)(2,1)}, u32[]{:S(2)}, u32[]{:S(2)}) collective-permute-start(bf16[512,512]{1,0:T(8,128)(2,1)} %get-tuple-element.27), channel_id=1, source_target_pairs={{0,12},{4,8},{8,4},{12,0},{1,13},{5,9},{9,5},{13,1},{2,14},{6,10},... | collective-permute-start | bytes 1572872 | tf_op jit(solution)/shard_map/ppermute | solution.py:81
  22.1 30.3 %collective-permute-start = (bf16[4,2,32,1024]{3,2,1,0:T(8,128)(2,1)}, bf16[4,2,32,1024]{3,2,1,0:T(8,128)(2,1)}, u32[]{:S(2)}, u32[]{:S(2)}) collective-permute-start(bf16[4,2,32,1024]{3,2,1,0:T(8,128)(2,1)} %dynamic-slice_bitcast_fusion.6), channel_id=1, source_target_pairs={{0,4},{4,0},{8,12},{12,8},{1,5},{5,1},{9,13},{13,9},{2,6},{6,2},{1... | collective-permute-start | bytes 1572872 | tf_op jit(solution)/shard_map/ppermute | solution.py:81
  23.8 31.5 %collective-permute-start.29 = (bf16[256,1024]{1,0:T(8,128)(2,1)S(1)}, bf16[256,1024]{1,0:T(8,128)(2,1)}, u32[]{:S(2)}, u32[]{:S(2)}) collective-permute-start(bf16[256,1024]{1,0:T(8,128)(2,1)S(1)} %get-tuple-element.45.refs_0_), channel_id=1, source_target_pairs={{0,1},{1,2},{2,3},{3,0},{4,5},{5,6},{6,7},{7,4},{8,9},{9,10},{10,1... | collective-permute-start | bytes 1572872 | tf_op jit(solution)/shard_map/ppermute | solution.py:81
  30.1 173.3 %copy-start = (bf16[512,512]{1,0:T(8,128)(2,1)}, bf16[512,512]{1,0:T(8,128)(2,1)S(1)}, u32[]{:S(2)}) copy-start(bf16[512,512]{1,0:T(8,128)(2,1)S(1)} %collective-permute-done.16.refs_20_.refs_14_) | copy-start | bytes 1572868
  30.1 25.3 %collective-permute-start.32 = (bf16[256,1024]{1,0:T(8,128)(2,1)S(1)}, bf16[256,1024]{1,0:T(8,128)(2,1)S(1)}, u32[]{:S(2)}, u32[]{:S(2)}) collective-permute-start(bf16[256,1024]{1,0:T(8,128)(2,1)S(1)} %get-tuple-element.45.refs_0_), channel_id=1, source_target_pairs={{0,4},{4,0},{8,12},{12,8},{1,5},{5,1},{9,13},{13,9},{2,6},{6,2},{1... | collective-permute-start | bytes 1572872 | tf_op jit(solution)/shard_map/ppermute | solution.py:81
  41.8 14.2 %collective-permute-start.22 = (bf16[256,1024]{1,0:T(8,128)(2,1)S(1)}, bf16[256,1024]{1,0:T(8,128)(2,1)}, u32[]{:S(2)}, u32[]{:S(2)}) collective-permute-start(bf16[256,1024]{1,0:T(8,128)(2,1)S(1)} %get-tuple-element.46.refs_0_), channel_id=1, source_target_pairs={{0,1},{1,2},{2,3},{3,0},{4,5},{5,6},{6,7},{7,4},{8,9},{9,10},{10,1... | collective-permute-start | bytes 1572872 | tf_op jit(solution)/shard_map/ppermute | solution.py:81
  51.5 6.0 %collective-permute-start.25 = (bf16[256,1024]{1,0:T(8,128)(2,1)S(1)}, bf16[256,1024]{1,0:T(8,128)(2,1)S(1)}, u32[]{:S(2)}, u32[]{:S(2)}) collective-permute-start(bf16[256,1024]{1,0:T(8,128)(2,1)S(1)} %get-tuple-element.46.refs_0_), channel_id=1, source_target_pairs={{0,4},{4,0},{8,12},{12,8},{1,5},{5,1},{9,13},{13,9},{2,6},{6,2},{1... | collective-permute-start | bytes 1572872 | tf_op jit(solution)/shard_map/ppermute | solution.py:81
  52.4 14.8 %collective-permute-start.15 = (bf16[512,512]{1,0:T(8,128)(2,1)S(1)}, bf16[512,512]{1,0:T(8,128)(2,1)S(1)}, u32[]{:S(2)}, u32[]{:S(2)}) collective-permute-start(bf16[512,512]{1,0:T(8,128)(2,1)S(1)} %collective-permute-done.14.refs_18_.refs_12_), channel_id=1, source_target_pairs={{0,16},{16,0},{1,17},{17,1},{2,18},{18,2},{3,19},{19,3},{4,20},{20... | collective-permute-start | bytes 1572872 | tf_op jit(solution)/shard_map/ppermute | solution.py:81
  55.3 113.6 %collective-permute-start.9 = (bf16[3,1024,512]{2,1,0:T(8,128)(2,1)}, bf16[3,1024,512]{2,1,0:T(8,128)(2,1)}, u32[]{:S(2)}, u32[]{:S(2)}) collective-permute-start(bf16[3,1024,512]{2,1,0:T(8,128)(2,1)} %constant_dynamic-slice_fusion.1), channel_id=1, source_target_pairs={{0,4},{4,0},{8,12},{12,8},{1,5},{5,1},{9,13},{13,9},{2,6},{6,2},{1... | collective-permute-start | bytes 9437192 | tf_op jit(solution)/shard_map/ppermute | solution.py:81
  55.4 23.0 %collective-permute-start.17 = (bf16[512,512]{1,0:T(8,128)(2,1)S(1)}, bf16[512,512]{1,0:T(8,128)(2,1)S(1)}, u32[]{:S(2)}, u32[]{:S(2)}) collective-permute-start(bf16[512,512]{1,0:T(8,128)(2,1)S(1)} %collective-permute-done.16.refs_20_.refs_14_), channel_id=1, source_target_pairs={{0,16},{16,0},{1,17},{17,1},{2,18},{18,2},{3,19},{19,3},{4,20},{20... | collective-permute-start | bytes 1572872 | tf_op jit(solution)/shard_map/ppermute | solution.py:81
  55.9 8.2 %collective-permute-start.1 = (bf16[4,32,1024]{2,1,0:T(8,128)(2,1)S(1)}, bf16[4,32,1024]{2,1,0:T(8,128)(2,1)S(1)}, u32[]{:S(2)}, u32[]{:S(2)}) collective-permute-start(bf16[4,32,1024]{2,1,0:T(8,128)(2,1)S(1)} %dynamic-slice_bitcast_fusion.7), channel_id=1, source_target_pairs={{0,8},{4,12},{8,0},{12,4},{1,9},{5,13},{9,1},{13,5},{2,10},{6,14},... | collective-permute-start | bytes 786440 | tf_op jit(solution)/shard_map/ppermute | solution.py:81
  58.4 31.3 %collective-permute-start.19 = (bf16[512,512]{1,0:T(8,128)(2,1)}, bf16[512,512]{1,0:T(8,128)(2,1)S(1)}, u32[]{:S(2)}, u32[]{:S(2)}) collective-permute-start(bf16[512,512]{1,0:T(8,128)(2,1)} %copy-done.19), channel_id=1, source_target_pairs={{0,16},{16,0},{1,17},{17,1},{2,18},{18,2},{3,19},{19,3},{4,20},{20... | collective-permute-start | bytes 1572872 | tf_op jit(solution)/shard_map/ppermute | solution.py:81
  64.2 35.8 %collective-permute-start.21 = (bf16[512,512]{1,0:T(8,128)(2,1)}, bf16[512,512]{1,0:T(8,128)(2,1)S(1)}, u32[]{:S(2)}, u32[]{:S(2)}) collective-permute-start(bf16[512,512]{1,0:T(8,128)(2,1)} %collective-permute-done.20.refs_24_.refs_18_), channel_id=1, source_target_pairs={{0,16},{16,0},{1,17},{17,1},{2,18},{18,2},{3,19},{19,3},{4,20},{20... | collective-permute-start | bytes 1572872 | tf_op jit(solution)/shard_map/ppermute | solution.py:81
  67.2 32.9 %collective-permute-start.30 = (bf16[256,1024]{1,0:T(8,128)(2,1)}, bf16[256,1024]{1,0:T(8,128)(2,1)}, u32[]{:S(2)}, u32[]{:S(2)}) collective-permute-start(bf16[256,1024]{1,0:T(8,128)(2,1)} %collective-permute-done.29.refs_1_), channel_id=1, source_target_pairs={{0,1},{1,2},{2,3},{3,0},{4,5},{5,6},{6,7},{7,4},{8,9},{9,10},{10,1... | collective-permute-start | bytes 1572872 | tf_op jit(solution)/shard_map/ppermute | solution.py:81
  78.4 23.4 %collective-permute-start.33 = (bf16[256,1024]{1,0:T(8,128)(2,1)}, bf16[256,1024]{1,0:T(8,128)(2,1)S(1)}, u32[]{:S(2)}, u32[]{:S(2)}) collective-permute-start(bf16[256,1024]{1,0:T(8,128)(2,1)} %collective-permute-done.29.refs_1_), channel_id=1, source_target_pairs={{0,4},{4,0},{8,12},{12,8},{1,5},{5,1},{9,13},{13,9},{2,6},{6,2},{1... | collective-permute-start | bytes 1572872 | tf_op jit(solution)/shard_map/ppermute | solution.py:81
  89.6 14.6 %collective-permute-start.23 = (bf16[256,1024]{1,0:T(8,128)(2,1)}, bf16[256,1024]{1,0:T(8,128)(2,1)}, u32[]{:S(2)}, u32[]{:S(2)}) collective-permute-start(bf16[256,1024]{1,0:T(8,128)(2,1)} %collective-permute-done.22.refs_1_), channel_id=1, source_target_pairs={{0,1},{1,2},{2,3},{3,0},{4,5},{5,6},{6,7},{7,4},{8,9},{9,10},{10,1... | collective-permute-start | bytes 1572872 | tf_op jit(solution)/shard_map/ppermute | solution.py:81
  100.0 5.6 %collective-permute-start.26 = (bf16[256,1024]{1,0:T(8,128)(2,1)}, bf16[256,1024]{1,0:T(8,128)(2,1)}, u32[]{:S(2)}, u32[]{:S(2)}) collective-permute-start(bf16[256,1024]{1,0:T(8,128)(2,1)} %collective-permute-done.22.refs_1_), channel_id=1, source_target_pairs={{0,4},{4,0},{8,12},{12,8},{1,5},{5,1},{9,13},{13,9},{2,6},{6,2},{1... | collective-permute-start | bytes 1572872 | tf_op jit(solution)/shard_map/ppermute | solution.py:81
  100.0 15.0 %collective-permute-start.10 = (bf16[512,512]{1,0:T(8,128)(2,1)}, bf16[512,512]{1,0:T(8,128)(2,1)S(1)}, u32[]{:S(2)}, u32[]{:S(2)}) collective-permute-start(bf16[512,512]{1,0:T(8,128)(2,1)} %get-tuple-element.22), channel_id=1, source_target_pairs={{0,8},{4,12},{8,0},{12,4},{1,9},{5,13},{9,1},{13,5},{2,10},{6,14},... | collective-permute-start | bytes 1572872 | tf_op jit(solution)/shard_map/ppermute | solution.py:81
  102.7 23.0 %collective-permute-start.12 = (bf16[512,512]{1,0:T(8,128)(2,1)}, bf16[512,512]{1,0:T(8,128)(2,1)}, u32[]{:S(2)}, u32[]{:S(2)}) collective-permute-start(bf16[512,512]{1,0:T(8,128)(2,1)} %get-tuple-element.23), channel_id=1, source_target_pairs={{0,12},{4,8},{8,4},{12,0},{1,13},{5,9},{9,5},{13,1},{2,14},{6,10},... | collective-permute-start | bytes 1572872 | tf_op jit(solution)/shard_map/ppermute | solution.py:81
  104.2 23.0 %collective-permute-start.2 = (bf16[128,1024]{1,0:T(8,128)(2,1)S(1)}, bf16[128,1024]{1,0:T(8,128)(2,1)S(1)}, u32[]{:S(2)}, u32[]{:S(2)}) collective-permute-start(bf16[128,1024]{1,0:T(8,128)(2,1)S(1)} %bitcast.57), channel_id=1, source_target_pairs={{0,1},{1,2},{2,3},{3,0},{4,5},{5,6},{6,7},{7,4},{8,9},{9,10},{10,1... | collective-permute-start | bytes 786440 | tf_op jit(solution)/shard_map/ppermute | solution.py:81
  105.7 23.2 %collective-permute-start.5 = (bf16[128,1024]{1,0:T(8,128)(2,1)S(1)}, bf16[128,1024]{1,0:T(8,128)(2,1)S(1)}, u32[]{:S(2)}, u32[]{:S(2)}) collective-permute-start(bf16[128,1024]{1,0:T(8,128)(2,1)S(1)} %bitcast.58), channel_id=1, source_target_pairs={{0,4},{4,0},{8,12},{12,8},{1,5},{5,1},{9,13},{13,9},{2,6},{6,2},{1... | collective-permute-start | bytes 786440 | tf_op jit(solution)/shard_map/ppermute | solution.py:81
  115.1 50.2 %collective-permute-start.40 = (bf16[512,1024]{1,0:T(8,128)(2,1)S(1)}, bf16[512,1024]{1,0:T(8,128)(2,1)}, u32[]{:S(2)}, u32[]{:S(2)}) collective-permute-start(bf16[512,1024]{1,0:T(8,128)(2,1)S(1)} %constant_dynamic-slice_fusion), channel_id=1, source_target_pairs={{0,8},{4,12},{8,0},{12,4},{1,9},{5,13},{9,1},{13,5},{2,10},{6,14},... | collective-permute-start | bytes 3145736 | tf_op jit(solution)/shard_map/ppermute | solution.py:81
  125.6 23.2 %collective-permute-start.31 = (bf16[256,1024]{1,0:T(8,128)(2,1)}, bf16[256,1024]{1,0:T(8,128)(2,1)}, u32[]{:S(2)}, u32[]{:S(2)}) collective-permute-start(bf16[256,1024]{1,0:T(8,128)(2,1)} %collective-permute-done.30.refs_2_), channel_id=1, source_target_pairs={{0,1},{1,2},{2,3},{3,0},{4,5},{5,6},{6,7},{7,4},{8,9},{9,10},{10,1... | collective-permute-start | bytes 1572872 | tf_op jit(solution)/shard_map/ppermute | solution.py:81
  127.3 20.8 %collective-permute-start.3 = (bf16[128,1024]{1,0:T(8,128)(2,1)S(1)}, bf16[128,1024]{1,0:T(8,128)(2,1)}, u32[]{:S(2)}, u32[]{:S(2)}) collective-permute-start(bf16[128,1024]{1,0:T(8,128)(2,1)S(1)} %collective-permute-done.2.refs_1_), channel_id=1, source_target_pairs={{0,1},{1,2},{2,3},{3,0},{4,5},{5,6},{6,7},{7,4},{8,9},{9,10},{10,1... | collective-permute-start | bytes 786440 | tf_op jit(solution)/shard_map/ppermute | solution.py:81
  129.6 18.5 %collective-permute-start.6 = (bf16[128,1024]{1,0:T(8,128)(2,1)S(1)}, bf16[128,1024]{1,0:T(8,128)(2,1)S(1)}, u32[]{:S(2)}, u32[]{:S(2)}) collective-permute-start(bf16[128,1024]{1,0:T(8,128)(2,1)S(1)} %collective-permute-done.2.refs_1_), channel_id=1, source_target_pairs={{0,4},{4,0},{8,12},{12,8},{1,5},{5,1},{9,13},{13,9},{2,6},{6,2},{1... | collective-permute-start | bytes 786440 | tf_op jit(solution)/shard_map/ppermute | solution.py:81
  148.1 2.1 collective-permute-start.34
  148.8 16.4 %collective-permute-start.24 = (bf16[256,1024]{1,0:T(8,128)(2,1)}, bf16[256,1024]{1,0:T(8,128)(2,1)}, u32[]{:S(2)}, u32[]{:S(2)}) collective-permute-start(bf16[256,1024]{1,0:T(8,128)(2,1)} %collective-permute-done.23.refs_2_), channel_id=1, source_target_pairs={{0,1},{1,2},{2,3},{3,0},{4,5},{5,6},{6,7},{7,4},{8,9},{9,10},{10,1... | collective-permute-start | bytes 1572872 | tf_op jit(solution)/shard_map/ppermute | solution.py:81
  148.8 18.0 %collective-permute-start.27 = (bf16[256,1024]{1,0:T(8,128)(2,1)}, bf16[256,1024]{1,0:T(8,128)(2,1)S(1)}, u32[]{:S(2)}, u32[]{:S(2)}) collective-permute-start(bf16[256,1024]{1,0:T(8,128)(2,1)} %collective-permute-done.23.refs_2_), channel_id=1, source_target_pairs={{0,4},{4,0},{8,12},{12,8},{1,5},{5,1},{9,13},{13,9},{2,6},{6,2},{1... | collective-permute-start | bytes 1572872 | tf_op jit(solution)/shard_map/ppermute | solution.py:81
  151.0 16.8 %collective-permute-start.11 = (bf16[512,512]{1,0:T(8,128)(2,1)S(1)}, bf16[512,512]{1,0:T(8,128)(2,1)}, u32[]{:S(2)}, u32[]{:S(2)}) collective-permute-start(bf16[512,512]{1,0:T(8,128)(2,1)S(1)} %collective-permute-done.10.refs_14_), channel_id=1, source_target_pairs={{0,16},{16,0},{1,17},{17,1},{2,18},{18,2},{3,19},{19,3},{4,20},{20... | collective-permute-start | bytes 1572872 | tf_op jit(solution)/shard_map/ppermute | solution.py:81
  165.2 3.1 %collective-permute-start.35 = (bf16[256,1024]{1,0:T(8,128)(2,1)}, bf16[256,1024]{1,0:T(8,128)(2,1)}, u32[]{:S(2)}, u32[]{:S(2)}) collective-permute-start(bf16[256,1024]{1,0:T(8,128)(2,1)} %collective-permute-done.31.refs_3_), channel_id=1, source_target_pairs={{0,4},{4,0},{8,12},{12,8},{1,5},{5,1},{9,13},{13,9},{2,6},{6,2},{1... | collective-permute-start | bytes 1572872 | tf_op jit(solution)/shard_map/ppermute | solution.py:81
  165.2 37.7 %collective-permute-start.41 = (bf16[512,1024]{1,0:T(8,128)(2,1)}, bf16[512,1024]{1,0:T(8,128)(2,1)}, u32[]{:S(2)}, u32[]{:S(2)}) collective-permute-start(bf16[512,1024]{1,0:T(8,128)(2,1)} %collective-permute-done.40.refs_2_), channel_id=1, source_target_pairs={{0,16},{16,0},{1,17},{17,1},{2,18},{18,2},{3,19},{19,3},{4,20},{20... | collective-permute-start | bytes 3145736 | tf_op jit(solution)/shard_map/ppermute | solution.py:81
  167.6 58.7 %collective-permute-start.39 = (bf16[1024,1024]{1,0:T(8,128)(2,1)}, bf16[1024,1024]{1,0:T(8,128)(2,1)}, u32[]{:S(2)}, u32[]{:S(2)}) collective-permute-start(bf16[1024,1024]{1,0:T(8,128)(2,1)} %refs_0_.1), channel_id=1, source_target_pairs={{0,4},{4,0},{8,12},{12,8},{1,5},{5,1},{9,13},{13,9},{2,6},{6,2},{1... | collective-permute-start | bytes 6291464 | tf_op jit(solution)/shard_map/ppermute | solution.py:81
  167.8 34.6 %collective-permute-start.13 = (bf16[512,512]{1,0:T(8,128)(2,1)}, bf16[512,512]{1,0:T(8,128)(2,1)}, u32[]{:S(2)}, u32[]{:S(2)}) collective-permute-start(bf16[512,512]{1,0:T(8,128)(2,1)} %collective-permute-done.12.refs_16_), channel_id=1, source_target_pairs={{0,16},{16,0},{1,17},{17,1},{2,18},{18,2},{3,19},{19,3},{4,20},{20... | collective-permute-start | bytes 1572872 | tf_op jit(solution)/shard_map/ppermute | solution.py:81
  168.3 34.6 %collective-permute-start.28 = (bf16[256,1024]{1,0:T(8,128)(2,1)}, bf16[256,1024]{1,0:T(8,128)(2,1)}, u32[]{:S(2)}, u32[]{:S(2)}) collective-permute-start(bf16[256,1024]{1,0:T(8,128)(2,1)} %collective-permute-done.24.refs_3_), channel_id=1, source_target_pairs={{0,4},{4,0},{8,12},{12,8},{1,5},{5,1},{9,13},{13,9},{2,6},{6,2},{1... | collective-permute-start | bytes 1572872 | tf_op jit(solution)/shard_map/ppermute | solution.py:81
  168.9 33.5 %collective-permute-start.4 = (bf16[128,1024]{1,0:T(8,128)(2,1)}, bf16[128,1024]{1,0:T(8,128)(2,1)S(1)}, u32[]{:S(2)}, u32[]{:S(2)}) collective-permute-start(bf16[128,1024]{1,0:T(8,128)(2,1)} %collective-permute-done.3.refs_2_), channel_id=1, source_target_pairs={{0,1},{1,2},{2,3},{3,0},{4,5},{5,6},{6,7},{7,4},{8,9},{9,10},{10,1... | collective-permute-start | bytes 786440 | tf_op jit(solution)/shard_map/ppermute | solution.py:81
  202.4 10.9 %collective-permute-start.7 = (bf16[128,1024]{1,0:T(8,128)(2,1)}, bf16[128,1024]{1,0:T(8,128)(2,1)S(1)}, u32[]{:S(2)}, u32[]{:S(2)}) collective-permute-start(bf16[128,1024]{1,0:T(8,128)(2,1)} %collective-permute-done.3.refs_2_), channel_id=1, source_target_pairs={{0,4},{4,0},{8,12},{12,8},{1,5},{5,1},{9,13},{13,9},{2,6},{6,2},{1... | collective-permute-start | bytes 786440 | tf_op jit(solution)/shard_map/ppermute | solution.py:81
  202.4 23.9 %collective-permute-start.42 = (bf16[512,1024]{1,0:T(8,128)(2,1)}, bf16[512,1024]{1,0:T(8,128)(2,1)S(1)}, u32[]{:S(2)}, u32[]{:S(2)}) collective-permute-start(bf16[512,1024]{1,0:T(8,128)(2,1)} %collective-permute-done.40.refs_2_), channel_id=1, source_target_pairs={{0,4},{4,0},{8,12},{12,8},{1,5},{5,1},{9,13},{13,9},{2,6},{6,2},{1... | collective-permute-start | bytes 3145736 | tf_op jit(solution)/shard_map/ppermute | solution.py:81
  202.9 12.0 %collective-permute-start.8 = (bf16[128,1024]{1,0:T(8,128)(2,1)S(1)}, bf16[128,1024]{1,0:T(8,128)(2,1)S(1)}, u32[]{:S(2)}, u32[]{:S(2)}) collective-permute-start(bf16[128,1024]{1,0:T(8,128)(2,1)S(1)} %collective-permute-done.4.refs_3_), channel_id=1, source_target_pairs={{0,4},{4,0},{8,12},{12,8},{1,5},{5,1},{9,13},{13,9},{2,6},{6,2},{1... | collective-permute-start | bytes 786440 | tf_op jit(solution)/shard_map/ppermute | solution.py:81
  203.0 24.5 %collective-permute-start.43 = (bf16[512,1024]{1,0:T(8,128)(2,1)}, bf16[512,1024]{1,0:T(8,128)(2,1)}, u32[]{:S(2)}, u32[]{:S(2)}) collective-permute-start(bf16[512,1024]{1,0:T(8,128)(2,1)} %collective-permute-done.41.refs_3_), channel_id=1, source_target_pairs={{0,4},{4,0},{8,12},{12,8},{1,5},{5,1},{9,13},{13,9},{2,6},{6,2},{1... | collective-permute-start | bytes 3145736 | tf_op jit(solution)/shard_map/ppermute | solution.py:81
  213.3 12.2 %collective-permute-start.37 = (bf16[4,128,128]{2,1,0:T(8,128)(2,1)S(1)}, bf16[4,128,128]{2,1,0:T(8,128)(2,1)S(1)}, u32[]{:S(2)}, u32[]{:S(2)}) collective-permute-start(bf16[4,128,128]{2,1,0:T(8,128)(2,1)S(1)} %get-tuple-element.33), channel_id=1, source_target_pairs={{0,8},{4,12},{8,0},{12,4},{1,9},{5,13},{9,1},{13,5},{2,10},{6,14},... | collective-permute-start | bytes 393224 | tf_op jit(solution)/shard_map/ppermute | solution.py:81
  214.8 10.6 %collective-permute-start.36 = (bf16[4,128,128]{2,1,0:T(8,128)(2,1)S(1)}, bf16[4,128,128]{2,1,0:T(8,128)(2,1)S(1)}, u32[]{:S(2)}, u32[]{:S(2)}) collective-permute-start(bf16[4,128,128]{2,1,0:T(8,128)(2,1)S(1)} %get-tuple-element.32), channel_id=1, source_target_pairs={{0,8},{4,12},{8,0},{12,4},{1,9},{5,13},{9,1},{13,5},{2,10},{6,14},... | collective-permute-start | bytes 393224 | tf_op jit(solution)/shard_map/ppermute | solution.py:81
  226.0 1.4 collective-permute-start.38
  231.9 11.1 %collective-permute-start.44 = (bf16[128,1024]{1,0:T(8,128)(2,1)S(1)}, bf16[128,1024]{1,0:T(8,128)(2,1)S(1)}, u32[]{:S(2)}, u32[]{:S(2)}) collective-permute-start(bf16[128,1024]{1,0:T(8,128)(2,1)S(1)} %get-tuple-element.36), channel_id=1, source_target_pairs={{0,1},{1,2},{2,3},{3,0},{4,5},{5,6},{6,7},{7,4},{8,9},{9,10},{10,1... | collective-permute-start | bytes 786440 | tf_op jit(solution)/shard_map/ppermute | solution.py:81
  231.9 21.4 %collective-permute-start.45 = (bf16[128,1024]{1,0:T(8,128)(2,1)S(1)}, bf16[128,1024]{1,0:T(8,128)(2,1)S(1)}, u32[]{:S(2)}, u32[]{:S(2)}) collective-permute-start(bf16[128,1024]{1,0:T(8,128)(2,1)S(1)} %get-tuple-element.37), channel_id=1, source_target_pairs={{0,2},{1,3},{2,0},{3,1},{4,6},{5,7},{6,4},{7,5},{8,10},{9,11},{10,... | collective-permute-start | bytes 786440 | tf_op jit(solution)/shard_map/ppermute | solution.py:81
  232.4 20.9 %collective-permute-start.46 = (bf16[128,1024]{1,0:T(8,128)(2,1)S(1)}, bf16[128,1024]{1,0:T(8,128)(2,1)S(1)}, u32[]{:S(2)}, u32[]{:S(2)}) collective-permute-start(bf16[128,1024]{1,0:T(8,128)(2,1)S(1)} %get-tuple-element.38), channel_id=1, source_target_pairs={{0,3},{1,0},{2,1},{3,2},{4,7},{5,4},{6,5},{7,6},{8,11},{9,8},{10,9... | collective-permute-start | bytes 786440 | tf_op jit(solution)/shard_map/ppermute | solution.py:81
  (27 other events, 536.1 us)

commit v2 on v0

--- a/solution.py
+++ b/solution.py
@@ -1,16 +1,24 @@
+import functools
+
 import jax
 import jax.numpy as jnp
 from jax import lax
+from jax.experimental import pallas as pl
+from jax.experimental.pallas import tpu as pltpu
 from jax.sharding import PartitionSpec as P
 
 DH = 128
+F32 = jnp.float32
+BF16 = jnp.bfloat16
+VMEM_LIMIT = 56 * 1024 * 1024
+VMEM_SMALL = 16 * 1024 * 1024
 
 
 def rms_rows(values):
     return values * lax.rsqrt(jnp.mean(values * values, axis=-1, keepdims=True) + 1e-06)
 
 
-def on_device(prompt_hidden, qkv_weight, out_weight, embed_table, response_ids, assignment):
+def gathered_plan(prompt_hidden, qkv_weight, out_weight, embed_table, response_ids, assignment):
     local_cols = prompt_hidden.shape[2]
     prompt_rows = prompt_hidden.shape[1]
     head_size = DH
@@ -70,6 +78,479 @@
     return result.astype(jnp.bfloat16)
 
 
+def permute(array, axis, pairs):
+    return lax.ppermute(array, axis, pairs)
+
+
+def xor_pairs(count, mask):
+    return [(i, i ^ mask) for i in range(count)]
+
+
+def shift_pairs(count, by):
+    return [(i, (i + by) % count) for i in range(count)]
+
+
+def fetch_rows(meta, blocks, parts, held, sems):
+    count = len(blocks) // parts
+    block = held.shape[1] // count
+    copies = []
+    for part in range(parts):
+        for k in range(count):
+            rows = blocks[part * count + k].shape[0]
+            at = pl.multiple_of(meta[k] * block, block)
+            copies.append(
+                pltpu.make_async_copy(
+                    blocks[part * count + k],
+                    held.at[pl.ds(part * rows, rows), pl.ds(at, block)],
+                    sems.at[len(copies)],
+                )
+            )
+    for copy in copies:
+        copy.start()
+    for copy in copies:
+        copy.wait()
+
+
+def held_dot(held, weights):
+    total, at = None, 0
+    for weight in weights:
+        term = jnp.dot(held[:, at : at + weight.shape[0]], weight, preferred_element_type=F32)
+        total = term if total is None else total + term
+        at += weight.shape[0]
+    return total
+
+
+def state_kernel(nblocks, meta, *refs):
+    blocks, refs = refs[:nblocks], refs[nblocks:]
+    key_own, value_own, key_sib, value_sib = refs[:4]
+    key_far, value_far = refs[4:6], refs[6:8]
+    out, rounded, held, sems = refs[8:]
+    prompts = out.shape[0]
+    half = nblocks // 2
+
+    @pl.when(pl.program_id(0) == 0)
+    def _():
+        parts = [blocks[s * half + k].at[p] for p in range(prompts) for s in range(2) for k in range(half)]
+        fetch_rows(meta, parts, 2 * prompts, held, sems)
+
+    keys = [key_own[0], key_sib[0]] + [ref[...] for ref in key_far]
+    values = [value_own[0], value_sib[0]] + [ref[...] for ref in value_far]
+    parts = [jnp.concatenate(pair, axis=1) for pair in zip(keys, values)]
+    both = held_dot(held, parts).astype(BF16)
+    tokens = both.shape[0] // prompts
+    for p in range(prompts):
+        rows = both[p * tokens : (p + 1) * tokens]
+        state = lax.dot_general(
+            rows[:, :DH], rows[:, DH:], (((0,), (0,)), ((), ())), preferred_element_type=F32
+        )
+        out[p, 0] = state
+        rounded[p, 0] = state.astype(BF16)
+
+
+def project_kernel(nhead, steps, meta, mine, other, *refs):
+    own, sib = refs[:3], refs[3:6]
+    far = refs[6:8], refs[8:10], refs[10:12]
+    query_out, local_out, residual, held, sems = refs[12:]
+    rows, features = held.shape
+    depth = features // (2 * nhead)
+
+    @pl.when(pl.program_id(0) == 0)
+    def _():
+        fetch_rows(meta, [ref.at[k] for ref in (mine, other) for k in range(nhead)], 2, held, sems)
+        share = residual.shape[0]
+        at = pl.multiple_of(meta[nhead] * share, share)
+        residual[...] = held[pl.ds(at, share), :]
+        squares = jnp.zeros((rows, 1), F32)
+        for i in range(0, features, depth):
+            part = held[:, i : i + depth].astype(F32)
+            squares += jnp.sum(part * part, axis=-1, keepdims=True)
+        scale = lax.rsqrt(squares / features + 1e-06)
+        for i in range(0, features, depth):
+            held[:, i : i + depth] = (held[:, i : i + depth].astype(F32) * scale).astype(BF16)
+
+    query, key, value = (
+        held_dot(held, [own[i][0], sib[i][0]] + [ref[...] for ref in far[i]]).astype(BF16) for i in range(3)
+    )
+    query_out[...] = query
+    query, key, value = query.astype(F32), key.astype(F32), value.astype(F32)
+    each = rows // 2 // steps
+    for part in range(2):
+        for s in range(steps):
+            at_s = slice((part * steps + s) * each, (part * steps + s + 1) * each)
+            for head in range(query.shape[1] // DH):
+                cols = slice(head * DH, (head + 1) * DH)
+                total = None
+                for u in range(s + 1):
+                    at_u = slice((part * steps + u) * each, (part * steps + u + 1) * each)
+                    score = jnp.sum(query[at_s, cols] * key[at_u, cols], axis=-1, keepdims=True)
+                    term = score.astype(BF16).astype(F32) * value[at_u, cols]
+                    total = term if total is None else total + term
+                local_out[at_s, cols] = total
+
+
+def attend_kernel(query, local, chosen, states, others, out, given):
+    second = chosen[...] != 0
+    rows = out.shape[0]
+    for head in range(states.shape[1]):
+        cols = slice(head * DH, (head + 1) * DH)
+        q = query[:, cols]
+        both = []
+        for p in range(2):
+            state = states[p, head] + others[p, head].astype(F32)
+            high = state.astype(BF16)
+            low = (state - high.astype(F32)).astype(BF16)
+            both.append(
+                jnp.dot(q, high, preferred_element_type=F32) + jnp.dot(q, low, preferred_element_type=F32)
+            )
+        attended = jnp.where(second, both[1], both[0]) + local[:, cols]
+        normed = rms_rows(attended).astype(BF16)
+        out[:, cols] = normed[:rows]
+        given[:, cols] = normed[rows:]
+
+
+def share_out(meta, terms, outs):
+    for k, out in enumerate(outs):
+        share = out.shape[0]
+        at = pl.multiple_of(meta[k] * share, share)
+        out[...] = terms[pl.ds(at, share), :].astype(out.dtype)
+
+
+def near_kernel(meta, heads_own, heads_sib, own, sib, *refs):
+    outs, terms = refs[:-1], refs[-1]
+    core = meta[len(outs)]
+    half, width = heads_own.shape[1], own.shape[1]
+    own_at = pl.multiple_of(core * half, half)
+    sib_at = pl.multiple_of((1 - core) * half, half)
+    for j, weight in enumerate((own, sib)):
+        term = jnp.dot(heads_own[...], weight[pl.ds(own_at, half), :], preferred_element_type=F32)
+        term += jnp.dot(heads_sib[...], weight[pl.ds(sib_at, half), :], preferred_element_type=F32)
+        terms[:, j * width : (j + 1) * width] = term
+    share_out(meta, terms, outs)
+
+
+def far_kernel(meta, heads_own, heads_sib, far_x, far_y, diag_x, diag_y, *refs):
+    outs, heads, terms = refs[:-2], refs[-2], refs[-1]
+    core, group = meta[len(outs)], meta[len(outs) + 1]
+    heads[core] = heads_own[...]
+    heads[1 - core] = heads_sib[...]
+    width = far_x.shape[1]
+    for i, (first, second) in enumerate(((far_x, far_y), (diag_x, diag_y))):
+        term = jnp.dot(heads[group], first[...], preferred_element_type=F32)
+        term += jnp.dot(heads[1 - group], second[...], preferred_element_type=F32)
+        at = pl.multiple_of((i ^ group) * width, width)
+        terms[:, pl.ds(at, width)] = term
+    share_out(meta, terms, outs)
+
+
+def norm_kernel(nhead, meta, residual, *refs):
+    near, far, outs, mixed = refs[:nhead], refs[nhead : 2 * nhead], refs[2 * nhead : 3 * nhead], refs[-1]
+    part = near[0].shape[1]
+    squares = 0.0
+    for i, group in enumerate((near, far)):
+        total = residual[:, i * part : (i + 1) * part].astype(F32)
+        for ref in group:
+            total = total + ref[...].astype(F32)
+        squares = squares + jnp.sum(total * total, axis=-1, keepdims=True)
+        width = outs[0].shape[1]
+        for j in range(part // width):
+            mixed[i * (part // width) + j] = total[:, j * width : (j + 1) * width]
+    scale = lax.rsqrt(squares / (2 * part) + 1e-06)
+    for k, out in enumerate(outs):
+        out[...] = (mixed[meta[k]] * scale).astype(out.dtype)
+
+
+def place_kernel(meta, *refs):
+    out = refs[-1]
+    for k, piece in enumerate(refs[:-1]):
+        share = piece.shape[0]
+        out[pl.ds(pl.multiple_of(meta[k] * share, share), share), :] = piece[...]
+
+
+def anywhere(count):
+    return [pl.BlockSpec(memory_space=pltpu.HBM)] * count
+
+
+def in_vmem(count):
+    return [pl.BlockSpec(memory_space=pltpu.VMEM)] * count
+
+
+def small_call(kernel, name, meta, operands, outs, scratch=(), flops=0, limit=VMEM_SMALL):
+    return pl.pallas_call(
+        kernel,
+        out_shape=outs,
+        grid_spec=pltpu.PrefetchScalarGridSpec(
+            num_scalar_prefetch=1,
+            grid=(),
+            in_specs=in_vmem(len(operands)),
+            out_specs=tuple(in_vmem(len(outs))) if isinstance(outs, tuple) else in_vmem(1)[0],
+            scratch_shapes=list(scratch),
+        ),
+        compiler_params=pltpu.CompilerParams(vmem_limit_bytes=limit),
+        cost_estimate=pl.CostEstimate(flops=flops, bytes_accessed=4 * 1024 * 1024, transcendentals=0),
+        name=name,
+    )(meta, *operands)
+
+
+def permuted_plan(prompt_hidden, qkv_weight, out_weight, embed_table, response_ids, assignment):
+    grp, ctx, head = lax.axis_index("grp"), lax.axis_index("ctx"), lax.axis_index("head")
+    nctx, nhead = lax.axis_size("ctx"), lax.axis_size("head")
+    core, chip = ctx % 2, ctx // 2
+    to_sib, to_far = xor_pairs(nctx, 1), xor_pairs(nctx, 2)
+    fetch = [(g * nctx + c, g * nctx + (c ^ (2 + g))) for g in range(2) for c in range(nctx)]
+    ring = shift_pairs(nhead, 1)
+    prompts, prompt_rows, block = prompt_hidden.shape
+    depth = block // 2
+    cols = qkv_weight.shape[2] // 2
+    steps = response_ids.shape[0]
+    resp_local = response_ids.shape[1] // nctx
+    rows_local = steps * resp_local
+
+    sib = lambda array: permute(array, "ctx", to_sib)
+    up = lambda array: permute(array, "head", ring)
+    swap = lambda array: permute(array, "grp", xor_pairs(2, 1))
+
+    def lookup(ids):
+        offset_ids = ids - ctx * embed_table.shape[0]
+        return jnp.take(embed_table, jnp.clip(offset_ids, 0, embed_table.shape[0] - 1), axis=0)
+
+    def by_core(looked):
+        vocab_rows = embed_table.shape[0]
+        offset_ids = response_ids - ctx * vocab_rows
+        inside = (offset_ids >= 0) & (offset_ids < vocab_rows)
+        looked = jnp.where(inside[:, :, None], looked, jnp.zeros((), BF16))
+        looked = looked.reshape(steps, nctx // 2, 2, resp_local, block)
+        kept = lax.dynamic_index_in_dim(looked, core, 2, keepdims=False)
+        given = lax.dynamic_index_in_dim(looked, 1 - core, 2, keepdims=False)
+
+        def halves(received):
+            total = kept + received
+            mine = lax.dynamic_index_in_dim(total, chip, 1, keepdims=False)
+            given = lax.dynamic_index_in_dim(total, 1 - chip, 1, keepdims=False)
+            return mine.reshape(rows_local, block), given.reshape(rows_local, block)
+
+        return given, halves
+
+    width = out_weight.shape[1]
+    tie = lax.optimization_barrier
+
+    def fetched(k, weight):
+        return lax.dynamic_slice(weight, (k, 0, (core ^ grp) * cols), (1, block, cols))[0]
+
+    def cross(array):
+        return permute(array, ("grp", "ctx"), fetch)
+
+    first_half, later_weight = tie((fetched(1, qkv_weight), qkv_weight))
+    keys_x = cross(first_half)
+    tokens = [prompt_hidden, up(prompt_hidden)]
+    sib_tokens = [sib(prompt_hidden)]
+    looked = lookup(response_ids)
+
+    keys_x, tokens, sib_tokens, looked, next_half, later_weight = tie(
+        (keys_x, tokens, sib_tokens, looked, fetched(2, later_weight), later_weight)
+    )
+    values_x = cross(next_half)
+    keys_y = swap(keys_x)
+    tokens.append(up(tokens[1]))
+    sib_tokens.append(sib(tokens[1]))
+    given, halves_of = by_core(looked)
+    mine, given = halves_of(sib(given))
+    sib_weight = sib(lax.dynamic_slice(later_weight, (0, 0, (1 - core) * cols), (3, block, cols)))
+
+    values_x, keys_y, tokens, sib_tokens, mine, given, next_half, sib_weight = tie(
+        (values_x, keys_y, tokens, sib_tokens, mine, given, fetched(0, later_weight), sib_weight)
+    )
+    query_x = cross(next_half)
+    given = permute(given, "ctx", to_far)
+    values_y = swap(values_x)
+    tokens.append(up(tokens[2]))
+    sib_tokens.append(sib(tokens[2]))
+    embedded = mine + given
+    out_half = lax.dynamic_slice(out_weight, (grp * depth, 0), (depth, width))
+
+    query_x, values_y, tokens, sib_tokens, embedded, out_half = tie(
+        (query_x, values_y, tokens, sib_tokens, embedded, out_half)
+    )
+    out_x = permute(out_half, "ctx", to_far)
+    query_y = swap(query_x)
+    e = [embedded] + [permute(embedded, "head", shift_pairs(nhead, k)) for k in range(1, nhead)]
+    sib_tokens.append(sib(tokens[3]))
+
+    places = []
+    for k in range(nhead):
+        place = ctx ^ ((head - k) % nhead)
+        places.append(jnp.where(place < 2, place, place ^ grp))
+    meta = jnp.stack(places + [head, core, grp]).astype(jnp.int32)
+    at_core = nhead + 1
+
+    def own_spec(k, wide):
+        return pl.BlockSpec((1, block, wide), lambda n, m: (k, 0, m[at_core] * (cols // wide) + n))
+
+    def sib_spec(k, wide):
+        return pl.BlockSpec((1, block, wide), lambda n, m: (k, 0, n))
+
+    def far_spec(wide):
+        return pl.BlockSpec((block, wide), lambda n, m: (0, n))
+
+    crossed = ((query_x, query_y), (keys_x, keys_y), (values_x, values_y))
+    far_of = lambda k: crossed[k]
+    nblocks = 2 * nhead
+    heads_here = cols // DH
+    chip_tokens = 2 * prompts * prompt_rows
+
+    state_spec = pl.BlockSpec((prompts, 1, DH, DH), lambda n, m: (0, n, 0, 0))
+    states, rounded = pl.pallas_call(
+        functools.partial(state_kernel, nblocks),
+        out_shape=(
+            jax.ShapeDtypeStruct((prompts, heads_here, DH, DH), F32),
+            jax.ShapeDtypeStruct((prompts, heads_here, DH, DH), BF16),
+        ),
+        grid_spec=pltpu.PrefetchScalarGridSpec(
+            num_scalar_prefetch=1,
+            grid=(heads_here,),
+            in_specs=anywhere(nblocks)
+            + [own_spec(1, DH), own_spec(2, DH), sib_spec(1, DH), sib_spec(2, DH)]
+            + [far_spec(DH)] * 4,
+            out_specs=(state_spec, state_spec),
+            scratch_shapes=[
+                pltpu.VMEM((chip_tokens, nhead * block), BF16),
+                pltpu.SemaphoreType.DMA((prompts * nblocks,)),
+            ],
+        ),
+        compiler_params=pltpu.CompilerParams(vmem_limit_bytes=VMEM_LIMIT),
+        cost_estimate=pl.CostEstimate(
+            flops=4 * chip_tokens * nhead * block * cols, bytes_accessed=16 * 1024 * 1024, transcendentals=0
+        ),
+        name="prompt_state",
+    )(
+        meta,
+        *tokens,
+        *sib_tokens,
+        qkv_weight,
+        qkv_weight,
+        sib_weight,
+        sib_weight,
+        *far_of(1),
+        *far_of(2),
+    )
+
+    states, rounded, out_x, query_y, query_x, e, out_own = tie(
+        (states, rounded, out_x, query_y, query_x, e, out_weight)
+    )
+    out_y = swap(out_x)
+    others = permute(rounded, "ctx", to_far)
+    e = jnp.stack(e)
+    sib_e = sib(e)
+
+    chip_rows = 2 * rows_local
+    share = rows_local // nhead
+    wide = 2 * DH
+    row_spec = pl.BlockSpec((chip_rows, wide), lambda n, m: (0, n))
+    query, local, residual = pl.pallas_call(
+        functools.partial(project_kernel, nhead, steps),
+        out_shape=(
+            jax.ShapeDtypeStruct((chip_rows, cols), BF16),
+            jax.ShapeDtypeStruct((chip_rows, cols), F32),
+            jax.ShapeDtypeStruct((share, nhead * block), BF16),
+        ),
+        grid_spec=pltpu.PrefetchScalarGridSpec(
+            num_scalar_prefetch=1,
+            grid=(cols // wide,),
+            in_specs=anywhere(2)
+            + [own_spec(k, wide) for k in range(3)]
+            + [sib_spec(k, wide) for k in range(3)]
+            + [far_spec(wide)] * 6,
+            out_specs=(row_spec, row_spec, pl.BlockSpec((share, nhead * block), lambda n, m: (0, 0))),
+            scratch_shapes=[
+                pltpu.VMEM((chip_rows, nhead * block), BF16),
+                pltpu.SemaphoreType.DMA((nblocks,)),
+            ],
+        ),
+        compiler_params=pltpu.CompilerParams(vmem_limit_bytes=VMEM_LIMIT),
+        cost_estimate=pl.CostEstimate(
+            flops=6 * chip_rows * nhead * block * cols, bytes_accessed=14 * 1024 * 1024, transcendentals=0
+        ),
+        name="response_rows",
+    )(
+        meta,
+        e,
+        sib_e,
+        *([qkv_weight] * 3),
+        *([sib_weight] * 3),
+        *far_of(0),
+        *far_of(1),
+        *far_of(2),
+    )
+
+    which = [
+        jnp.tile(lax.dynamic_slice_in_dim(assignment, owner * resp_local, resp_local, 0), steps)
+        for owner in (ctx, ctx ^ 1)
+    ]
+    heads_own, heads_sib = pl.pallas_call(
+        attend_kernel,
+        out_shape=(jax.ShapeDtypeStruct((rows_local, cols), BF16),) * 2,
+        compiler_params=pltpu.CompilerParams(vmem_limit_bytes=VMEM_SMALL),
+        name="attend",
+    )(query, local, jnp.concatenate(which)[:, None], states, others)
+    heads_sib = sib(heads_sib)
+    out_sib = sib(out_own)
+
+    ahead = [(head + k) % nhead for k in range(nhead)]
+    out_meta = jnp.stack(ahead + [core, grp]).astype(jnp.int32)
+
+    def spread(kernel, name, heads, operands, scratch):
+        outs = (jax.ShapeDtypeStruct((share, 2 * width), F32),)
+        outs += (jax.ShapeDtypeStruct((share, 2 * width), BF16),) * (nhead - 1)
+        scratch = [*scratch, pltpu.VMEM((rows_local, 2 * width), F32)]
+        flops = 4 * rows_local * block * width
+        terms = small_call(kernel, name, out_meta, (*heads, *operands), outs, scratch, flops, VMEM_LIMIT)
+        moved = {k: permute(terms[k], "head", shift_pairs(nhead, k)) for k in (2, 3, 1)}
+        return [terms[0]] + [moved[k] for k in range(1, nhead)]
+
+    near = spread(near_kernel, "near_terms", (heads_own, heads_sib), (out_weight, out_sib), [])
+    heads_own, heads_sib, out_y = tie((heads_own, heads_sib, out_y, near[0]))[:3]
+    diag_x = sib(out_x)
+    far = spread(
+        far_kernel,
+        "far_terms",
+        (heads_own, heads_sib),
+        (out_x, out_y, diag_x, sib(out_y)),
+        [pltpu.VMEM((2, rows_local, cols), BF16)],
+    )
+    norm_meta = [ctx ^ f for f in ahead]
+    norm_meta = jnp.stack([jnp.where(j < 2, j, j ^ grp) for j in norm_meta]).astype(jnp.int32)
+    normed = small_call(
+        functools.partial(norm_kernel, nhead),
+        "final_norm",
+        norm_meta,
+        (residual, *near, *far),
+        (jax.ShapeDtypeStruct((share, width), BF16),) * nhead,
+        [pltpu.VMEM((nhead, share, width), F32)],
+    )
+    pieces = [normed[0]] + [permute(normed[k], "head", shift_pairs(nhead, k)) for k in range(1, nhead)]
+    behind = jnp.stack([(head - k) % nhead for k in range(nhead)]).astype(jnp.int32)
+    result = small_call(
+        place_kernel, "place", behind, pieces, jax.ShapeDtypeStruct((rows_local, width), BF16)
+    )
+    return result.reshape(steps, resp_local, width)
+
+
+def on_device(prompt_hidden, qkv_weight, out_weight, embed_table, response_ids, assignment):
+    nctx, nhead = lax.axis_size("ctx"), lax.axis_size("head")
+    local_heads = qkv_weight.shape[2] // DH
+    fits = (
+        lax.axis_size("grp") == 2
+        and nctx == 4
+        and nhead == 4
+        and prompt_hidden.shape[0] == 2
+        and local_heads % 4 == 0
+        and prompt_hidden.shape[1] % 16 == 0
+        and (response_ids.shape[1] // nctx) % (16 * nhead // response_ids.shape[0]) == 0
+        and (response_ids.shape[1] // nctx) % 16 == 0
+    )
+    plan = permuted_plan if fits else gathered_plan
+    return plan(prompt_hidden, qkv_weight, out_weight, embed_table, response_ids, assignment)
+
+
 def solution(mesh):
     return jax.shard_map(
         on_device,

time: 462 us -> 198 us (0.43)
  waiting for transfers between devices: 365 us -> 78.2 us
  Pallas kernels: 0 us -> 40.7 us
  matrix products: 38.4 us -> 0 us
  starting transfers between devices: 0.64 us -> 37.3 us
  between operations: 13.6 us -> 0.23 us
  blocking collectives: 9.39 us -> 0 us
  local copies, waits for them, and re-layouts: 26.9 us -> 33.9 us
    all_gather x4 -> x0, waiting for transfers between devices: 289 us -> none  [the longest x1 156 us: on_device(): full_rows = lax.all_gather(qkv_weight, 'ctx', axis=1, tiled=True)]
    ppermute x0 -> x36, waiting for transfers between devices: none -> 78.2 us  [permute(): return lax.ppermute(array, axis, pairs)]
    reduce_scatter x2 -> x0, waiting for transfers between devices: 53.5 us -> none  [the longest x1 27.3 us: on_device(): lax.psum_scatter(terms.astype(jnp.bfloat16), 'head', scatter_dimension=2,...]
    pallas_call x0 -> x7, Pallas kernels: none -> 40.7 us  [the longest x1 17.3 us: permuted_plan(): pl.pallas_call(functools.partial(state_kernel, nblocks), out_shape=(jax.S...]
    dot_general x6 -> x0, matrix products: 38.4 us -> none  [the longest x1 17.3 us: on_device(): jnp.dot(flat_piece, kv_weight, preferred_element_type=jnp.float32)]
    ppermute x0 -> x36, starting transfers between devices: none -> 37.3 us  [permute(): return lax.ppermute(array, axis, pairs)]
    psum x1 -> x0, waiting for transfers between devices: 20.3 us -> none  [on_device(): lax.psum(partial_state.astype(jnp.bfloat16), 'ctx').astype(jnp.float32)]
    psum x1 -> x0, blocking collectives: 9.39 us -> none  [on_device(): squares = lax.psum(jnp.sum(mixed * mixed, axis=-1), 'head')]
  transfers between devices with their start and end apart: 7 -> 36, of which waited for: 7 -> 17; matrix products, arithmetic and copies ran while one was open for 11% -> 14% of each run, Pallas kernels for 0% -> 20%
where the time goes in v2:
time: 198 us; the launch traced here: 197 us
  waiting for transfers between devices  78.2 us (39%)
  Pallas kernels  40.7 us (21%)
  starting transfers between devices  37.3 us (19%)
  local copies, waits for them, and re-layouts  33.9 us (17%)
  other arithmetic  6.5 us (3%)
    ppermute x36, waiting for transfers between devices, permute(): return lax.ppermute(array, axis, pairs)  78.2 us
    ppermute x36, starting transfers between devices, permute(): return lax.ppermute(array, axis, pairs)  37.3 us
    pallas_call x1, Pallas kernels, permuted_plan(): pl.pallas_call(functools.partial(state_kernel, nblocks), out_shape=(jax.S...  17.3 us
    pallas_call x1, Pallas kernels, permuted_plan(): pl.pallas_call(functools.partial(project_kernel, nhead, steps), out_shape...  11.7 us
    pallas_call x4, Pallas kernels, small_call(): pl.pallas_call(kernel, out_shape=outs, grid_spec=pltpu.PrefetchScalarGrid...  11.2 us
    gather x1, local copies, waits for them, and re-layouts, lookup(): jnp.take(embed_table, jnp.clip(offset_ids, 0, embed_table.shape[0] - 1),...  10.7 us
    unnamed x35, local copies, waits for them, and re-layouts  8.03 us
    squeeze x3, local copies, waits for them, and re-layouts, fetched(): lax.dynamic_slice(weight, (k, 0, (core ^ grp) * cols), (1, block, cols))[0]  5.85 us
  transfers between devices with their start and end apart: 36, of which 17 were waited for; matrix products, arithmetic and copies ran while one was open for 14% of the time, Pallas kernels for 20%

profile of v2, /device:TPU:0, one launch (start us, length us, event | category | flops | bytes accessed | tf_op | source)
XLA Modules:
  0.0 196.9 jit_solution(2829810853796201797)
XLA Ops:
  0.0 1.3 dynamic-slice_bitcast_fusion.2
  1.3 3.0 %collective-permute-start = (bf16[1024,512]{1,0:T(8,128)(2,1)S(1)}, bf16[1024,512]{1,0:T(8,128)(2,1)S(1)}, u32[]{:S(2)}, u32[]{:S(2)}) collective-permute-start(bf16[1024,512]{1,0:T(8,128)(2,1)S(1)} %dynamic-slice_bitcast_fusion.2), channel_id=1, source_target_pairs={{0,8},{4,12},{8,0},{12,4},{16,28},{20,24},{24,20},{28,16},{1,9},{5... | collective-permute-start | bytes 3145736 | tf_op jit(solution)/shard_map/ppermute | solution.py:82
  4.3 1.6 collective-permute-start.1
  6.6 10.7 %gather_fusion = bf16[512,1024]{1,0:T(8,128)(2,1)S(1)} fusion(bf16[8192,1024]{1,0:T(8,128)(2,1)} %param.9, s32[1024]{0:T(1024)S(1)} %pad_clamp_fusion), kind=kCustom, calls=%fused_computation | custom fusion | bytes 2099200 | tf_op jit(solution)/shard_map/jit(_take)/gather | solution.py:314
  17.3 2.3 %dynamic-slice_bitcast_fusion.1 = bf16[1024,512]{1,0:T(8,128)(2,1)} fusion(bf16[3,1024,1024]{2,1,0:T(8,128)(2,1)} %refs_2_.1, s32[]{:T(128)S(6)} %select_n.130), kind=kLoop, calls=%fused_computation.3 | loop fusion | bytes 2097156 | tf_op jit(solution)/shard_map/squeeze | solution.py:337
  19.6 1.2 broadcast_select_fusion.1
  20.7 6.8 %collective-permute-done.refs_12_.refs_8_ = bf16[1024,512]{1,0:T(8,128)(2,1)S(1)} collective-permute-done((bf16[1024,512]{1,0:T(8,128)(2,1)S(1)}, bf16[1024,512]{1,0:T(8,128)(2,1)S(1)}, u32[]{:S(2)}, u32[]{:S(2)}) %collective-permute-start) | collective-permute-done | bytes 1048608 | tf_op jit(solution)/shard_map/ppermute | solution.py:82
  27.5 3.6 %collective-permute-done.1.refs_1_ = bf16[2,256,1024]{2,1,0:T(8,128)(2,1)} collective-permute-done((bf16[2,256,1024]{2,1,0:T(8,128)(2,1)}, bf16[2,256,1024]{2,1,0:T(8,128)(2,1)}, u32[]{:S(2)}, u32[]{:S(2)}) %collective-permute-start.1) | collective-permute-done | bytes 1048608 | tf_op jit(solution)/shard_map/ppermute | solution.py:82
  31.1 3.7 %constant_dynamic-slice_fusion.1 = bf16[3,1024,512]{2,1,0:T(8,128)(2,1)} fusion(bf16[3,1024,1024]{2,1,0:T(8,128)(2,1)} %refs_2_.1, s32[]{:T(128)S(6)} %select_n.139), kind=kLoop, calls=%fused_computation.13 | loop fusion | bytes 6291460 | tf_op jit(solution)/shard_map/dynamic_slice | solution.py:357
  34.8 1.4 broadcast_select_fusion
  36.2 0.9 constant_dynamic-slice_fusion.5
  38.3 1.8 collective-permute-start.4
  40.3 1.0 collective-permute-done.7
  41.5 2.3 %dynamic-slice_bitcast_fusion = bf16[1024,512]{1,0:T(8,128)(2,1)} fusion(bf16[3,1024,1024]{2,1,0:T(8,128)(2,1)} %refs_2_.1, s32[]{:T(128)S(6)} %select_n.130), kind=kLoop, calls=%fused_computation.2 | loop fusion | bytes 2097156 | tf_op jit(solution)/shard_map/squeeze | solution.py:337
  43.8 1.3 fusion
  45.8 17.4 %collective-permute-done.3.refs_14_.refs_10_ = bf16[1024,512]{1,0:T(8,128)(2,1)} collective-permute-done((bf16[1024,512]{1,0:T(8,128)(2,1)}, bf16[1024,512]{1,0:T(8,128)(2,1)}, u32[]{:S(2)}, u32[]{:S(2)}) %collective-permute-start.3) | collective-permute-done | bytes 1048608 | tf_op jit(solution)/shard_map/ppermute | solution.py:82
  64.1 3.3 %collective-permute-done.5.refs_2_ = bf16[2,256,1024]{2,1,0:T(8,128)(2,1)} collective-permute-done((bf16[2,256,1024]{2,1,0:T(8,128)(2,1)}, bf16[2,256,1024]{2,1,0:T(8,128)(2,1)}, u32[]{:S(2)}, u32[]{:S(2)}) %collective-permute-start.5) | collective-permute-done | bytes 1048608 | tf_op jit(solution)/shard_map/ppermute | solution.py:82
  67.7 1.5 collective-permute-start.9
  69.8 2.3 %constant_dynamic-slice_fusion = bf16[512,1024]{1,0:T(8,128)(2,1)} fusion(bf16[1024,1024]{1,0:T(8,128)(2,1)} %own.1, s32[]{:T(128)S(6)} %select_n.140), kind=kLoop, calls=%fused_computation.12 | loop fusion | bytes 2097156 | tf_op jit(solution)/shard_map/dynamic_slice | solution.py:368
  72.1 27.1 %collective-permute-done.13 = bf16[128,1024]{1,0:T(8,128)(2,1)} collective-permute-done((bf16[128,1024]{1,0:T(8,128)(2,1)}, bf16[128,1024]{1,0:T(8,128)(2,1)}, u32[]{:S(2)}, u32[]{:S(2)}) %collective-permute-start.13) | collective-permute-done | bytes 262176 | tf_op jit(solution)/shard_map/ppermute | solution.py:82
  99.2 1.7 add.110
  101.1 1.6 collective-permute-start.15
  102.6 1.6 collective-permute-start.16
  104.9 4.4 %collective-permute-start.18 = (bf16[128,1024]{1,0:T(8,128)(2,1)}, bf16[128,1024]{1,0:T(8,128)(2,1)S(1)}, u32[]{:S(2)}, u32[]{:S(2)}) collective-permute-start(bf16[128,1024]{1,0:T(8,128)(2,1)} %add.110), channel_id=1, source_target_pairs={{0,2},{1,3},{2,0},{3,1},{4,6},{5,7},{6,4},{7,5},{8,10},{9,11},{10,... | collective-permute-start | bytes 786440 | tf_op jit(solution)/shard_map/ppermute | solution.py:82
  109.3 17.3 %prompt_state.1 = (f32[2,4,128,128]{3,2,1,0:T(8,128)}, bf16[2,4,128,128]{3,2,1,0:T(8,128)(2,1)}) custom-call(s32[7]{0:T(128)} %stack.98.meta, bf16[2,256,1024]{2,1,0:T(8,128)(2,1)} %refs_0_.1, bf16[2,256,1024]{2,1,0:T(8,128)(2,1)} %collective-permute-done.1.refs_1_, bf16[2,256,1024]{2,1,0:T(8,128)(2,1)} %collective-permute-done.5.refs_2_, ...), custom_call_target="tpu_custom_call" | custom-call | flops 8589934592 | bytes 16777216 | tf_op jit(solution)/shard_map/prompt_state/pallas_call | solution.py:401
  127.0 1.2 collective-permute-done.16.refs_7_
  128.9 1.6 collective-permute-start.27
  131.6 2.4 %collective-permute-done.20.other = bf16[4,128,1024]{2,1,0:T(8,128)(2,1)} collective-permute-done((bf16[4,128,1024]{2,1,0:T(8,128)(2,1)S(1)}, bf16[4,128,1024]{2,1,0:T(8,128)(2,1)}, u32[]{:S(2)}, u32[]{:S(2)}) %collective-permute-start.20) | collective-permute-done | bytes 1048608 | tf_op jit(solution)/shard_map/ppermute | solution.py:82
  134.0 11.7 %response_rows.1 = (bf16[256,512]{1,0:T(8,128)(2,1)}, f32[256,512]{1,0:T(8,128)}, bf16[32,4096]{1,0:T(8,128)(2,1)}) custom-call(s32[7]{0:T(128)} %stack.98.meta, bf16[4,128,1024]{2,1,0:T(8,128)(2,1)} %copy-done.8, bf16[4,128,1024]{2,1,0:T(8,128)(2,1)} %collective-permute-done.20.other, bf16[3,1024,1024]{2,1,0:T(8,128)(2,1)} %refs_2_.1, ...), custom_call_target="tpu_custom_call" | custom-call | flops 3221225472 | bytes 14680064 | tf_op jit(solution)/shard_map/response_rows/pallas_call | solution.py:448
  145.7 1.0 copy-done.2
  146.7 0.9 copy-done.6
  151.6 4.6 %near_terms.1 = (f32[32,2048]{1,0:T(8,128)}, bf16[32,2048]{1,0:T(8,128)(2,1)}, bf16[32,2048]{1,0:T(8,128)(2,1)}, bf16[32,2048]{1,0:T(8,128)(2,1)}) custom-call(s32[6]{0:T(128)} %stack.107.meta, bf16[128,512]{1,0:T(8,128)(2,1)} %copy-done, bf16[128,512]{1,0:T(8,128)(2,1)} %copy-done.14, bf16[1024,1024]{1,0:T(8,128)(2,1)} %own.1, bf16[1024,1024]{1,0:T(8,128)(2,1)} %copy-done.9), custom_call_target="tpu_custom_call" | custom-call | flops 536870912 | bytes 4194304 | tf_op jit(solution)/shard_map/near_terms/pallas_call | solution.py:278
  156.4 4.7 %collective-permute-start.24 = (bf16[32,2048]{1,0:T(8,128)(2,1)}, bf16[32,2048]{1,0:T(8,128)(2,1)S(1)}, u32[]{:S(2)}, u32[]{:S(2)}) collective-permute-start(bf16[32,2048]{1,0:T(8,128)(2,1)} %get-tuple-element.112), channel_id=1, source_target_pairs={{0,1},{1,2},{2,3},{3,0},{4,5},{5,6},{6,7},{7,4},{8,9},{9,10},{10,1... | collective-permute-start | bytes 393224 | tf_op jit(solution)/shard_map/ppermute | solution.py:82
  161.1 2.4 %collective-permute-start.26 = (bf16[32,2048]{1,0:T(8,128)(2,1)}, bf16[32,2048]{1,0:T(8,128)(2,1)S(1)}, u32[]{:S(2)}, u32[]{:S(2)}) collective-permute-start(bf16[32,2048]{1,0:T(8,128)(2,1)} %get-tuple-element.114), channel_id=1, source_target_pairs={{0,3},{1,0},{2,1},{3,2},{4,7},{5,4},{6,5},{7,6},{8,11},{9,8},{10,9... | collective-permute-start | bytes 393224 | tf_op jit(solution)/shard_map/ppermute | solution.py:82
  163.5 1.0 copy-done.11
  164.5 1.0 copy-done.12
  165.5 4.5 %far_terms.1 = (f32[32,2048]{1,0:T(8,128)}, bf16[32,2048]{1,0:T(8,128)(2,1)}, bf16[32,2048]{1,0:T(8,128)(2,1)}, bf16[32,2048]{1,0:T(8,128)(2,1)}) custom-call(s32[6]{0:T(128)} %stack.107.meta, bf16[128,512]{1,0:T(8,128)(2,1)} %copy-done, bf16[128,512]{1,0:T(8,128)(2,1)} %copy-done.14, bf16[512,1024]{1,0:T(8,128)(2,1)} %collective-permute-done.15.far_x, ...), custom_call_target="tpu_custom_call" | custom-call | flops 536870912 | bytes 4194304 | tf_op jit(solution)/shard_map/far_terms/pallas_call | solution.py:278
  170.0 2.6 %collective-permute-start.31 = (bf16[32,2048]{1,0:T(8,128)(2,1)}, bf16[32,2048]{1,0:T(8,128)(2,1)S(1)}, u32[]{:S(2)}, u32[]{:S(2)}) collective-permute-start(bf16[32,2048]{1,0:T(8,128)(2,1)} %get-tuple-element.121), channel_id=1, source_target_pairs={{0,2},{1,3},{2,0},{3,1},{4,6},{5,7},{6,4},{7,5},{8,10},{9,11},{10,... | collective-permute-start | bytes 393224 | tf_op jit(solution)/shard_map/ppermute | solution.py:82
  172.6 1.2 collective-permute-start.32
  173.9 4.5 %collective-permute-done.30.refs_5_ = bf16[32,2048]{1,0:T(8,128)(2,1)S(1)} collective-permute-done((bf16[32,2048]{1,0:T(8,128)(2,1)}, bf16[32,2048]{1,0:T(8,128)(2,1)S(1)}, u32[]{:S(2)}, u32[]{:S(2)}) %collective-permute-start.30) | collective-permute-done | bytes 131104 | tf_op jit(solution)/shard_map/ppermute | solution.py:82
  178.5 4.5 %collective-permute-done.31.refs_6_ = bf16[32,2048]{1,0:T(8,128)(2,1)S(1)} collective-permute-done((bf16[32,2048]{1,0:T(8,128)(2,1)}, bf16[32,2048]{1,0:T(8,128)(2,1)S(1)}, u32[]{:S(2)}, u32[]{:S(2)}) %collective-permute-start.31) | collective-permute-done | bytes 131104 | tf_op jit(solution)/shard_map/ppermute | solution.py:82
  183.0 0.9 copy-done.4
  183.9 0.9 copy-done.5
  185.7 2.4 %collective-permute-start.33 = (bf16[32,1024]{1,0:T(8,128)(2,1)S(1)}, bf16[32,1024]{1,0:T(8,128)(2,1)S(1)}, u32[]{:S(2)}, u32[]{:S(2)}) collective-permute-start(bf16[32,1024]{1,0:T(8,128)(2,1)S(1)} %get-tuple-element.124), channel_id=1, source_target_pairs={{0,1},{1,2},{2,3},{3,0},{4,5},{5,6},{6,7},{7,4},{8,9},{9,10},{10,1... | collective-permute-start | bytes 196616 | tf_op jit(solution)/shard_map/ppermute | solution.py:82
  188.1 2.6 %collective-permute-start.34 = (bf16[32,1024]{1,0:T(8,128)(2,1)S(1)}, bf16[32,1024]{1,0:T(8,128)(2,1)S(1)}, u32[]{:S(2)}, u32[]{:S(2)}) collective-permute-start(bf16[32,1024]{1,0:T(8,128)(2,1)S(1)} %get-tuple-element.125), channel_id=1, source_target_pairs={{0,2},{1,3},{2,0},{3,1},{4,6},{5,7},{6,4},{7,5},{8,10},{9,11},{10,... | collective-permute-start | bytes 196616 | tf_op jit(solution)/shard_map/ppermute | solution.py:82
  190.8 2.4 %collective-permute-done.33.refs_1_ = bf16[32,1024]{1,0:T(8,128)(2,1)S(1)} collective-permute-done((bf16[32,1024]{1,0:T(8,128)(2,1)S(1)}, bf16[32,1024]{1,0:T(8,128)(2,1)S(1)}, u32[]{:S(2)}, u32[]{:S(2)}) %collective-permute-start.33) | collective-permute-done | bytes 65568 | tf_op jit(solution)/shard_map/ppermute | solution.py:82
  193.2 1.9 collective-permute-done.34.refs_2_
  195.6 1.3 place.1
  (93 shorter events, 13.2 us)
Async XLA Ops:
  1.3 18.2 %copy-start.15 = (s32[4,128]{1,0:T(4,128)S(1)}, s32[4,128]{1,0:T(4,128)}, u32[]{:S(2)}) copy-start(s32[4,128]{1,0:T(4,128)} %param.10) | copy-start | bytes 6148
  1.3 26.2 %collective-permute-start = (bf16[1024,512]{1,0:T(8,128)(2,1)S(1)}, bf16[1024,512]{1,0:T(8,128)(2,1)S(1)}, u32[]{:S(2)}, u32[]{:S(2)}) collective-permute-start(bf16[1024,512]{1,0:T(8,128)(2,1)S(1)} %dynamic-slice_bitcast_fusion.2), channel_id=1, source_target_pairs={{0,8},{4,12},{8,0},{12,4},{16,28},{20,24},{24,20},{28,16},{1,9},{5... | collective-permute-start | bytes 3145736 | tf_op jit(solution)/shard_map/ppermute | solution.py:82
  4.3 26.8 %collective-permute-start.1 = (bf16[2,256,1024]{2,1,0:T(8,128)(2,1)}, bf16[2,256,1024]{2,1,0:T(8,128)(2,1)}, u32[]{:S(2)}, u32[]{:S(2)}) collective-permute-start(bf16[2,256,1024]{2,1,0:T(8,128)(2,1)} %refs_0_.1), channel_id=1, source_target_pairs={{0,1},{1,2},{2,3},{3,0},{4,5},{5,6},{6,7},{7,4},{8,9},{9,10},{10,1... | collective-permute-start | bytes 3145736 | tf_op jit(solution)/shard_map/ppermute | solution.py:82
  5.9 25.2 %collective-permute-start.2 = (bf16[2,256,1024]{2,1,0:T(8,128)(2,1)}, bf16[2,256,1024]{2,1,0:T(8,128)(2,1)}, u32[]{:S(2)}, u32[]{:S(2)}) collective-permute-start(bf16[2,256,1024]{2,1,0:T(8,128)(2,1)} %refs_0_.1), channel_id=1, source_target_pairs={{0,4},{4,0},{8,12},{12,8},{1,5},{5,1},{9,13},{13,9},{2,6},{6,2},{1... | collective-permute-start | bytes 3145736 | tf_op jit(solution)/shard_map/ppermute | solution.py:82
  27.5 3.6 %copy-start.10 = (bf16[1024,512]{1,0:T(8,128)(2,1)}, bf16[1024,512]{1,0:T(8,128)(2,1)S(1)}, u32[]{:S(2)}) copy-start(bf16[1024,512]{1,0:T(8,128)(2,1)S(1)} %collective-permute-done.refs_12_.refs_8_) | copy-start | bytes 3145732
  34.8 32.6 %collective-permute-start.8 = (bf16[3,1024,512]{2,1,0:T(8,128)(2,1)}, bf16[3,1024,512]{2,1,0:T(8,128)(2,1)S(1)}, u32[]{:S(2)}, u32[]{:S(2)}) collective-permute-start(bf16[3,1024,512]{2,1,0:T(8,128)(2,1)} %constant_dynamic-slice_fusion.1), channel_id=1, source_target_pairs={{0,4},{4,0},{8,12},{12,8},{1,5},{5,1},{9,13},{13,9},{2,6},{6,2},{1... | collective-permute-start | bytes 9437192 | tf_op jit(solution)/shard_map/ppermute | solution.py:82
  37.2 4.2 %collective-permute-start.7 = (bf16[4,2,32,1024]{3,2,0,1:T(8,128)(2,1)S(1)}, bf16[4,2,32,1024]{3,2,0,1:T(8,128)(2,1)}, u32[]{:S(2)}, u32[]{:S(2)}) collective-permute-start(bf16[4,2,32,1024]{3,2,0,1:T(8,128)(2,1)S(1)} %bitcast.46), channel_id=1, source_target_pairs={{0,4},{4,0},{8,12},{12,8},{1,5},{5,1},{9,13},{13,9},{2,6},{6,2},{1... | collective-permute-start | bytes 1572872 | tf_op jit(solution)/shard_map/ppermute | solution.py:82
  37.7 25.5 %collective-permute-start.3 = (bf16[1024,512]{1,0:T(8,128)(2,1)}, bf16[1024,512]{1,0:T(8,128)(2,1)}, u32[]{:S(2)}, u32[]{:S(2)}) collective-permute-start(bf16[1024,512]{1,0:T(8,128)(2,1)} %dynamic-slice_bitcast_fusion.1), channel_id=1, source_target_pairs={{0,8},{4,12},{8,0},{12,4},{16,28},{20,24},{24,20},{28,16},{1,9},{5... | collective-permute-start | bytes 3145736 | tf_op jit(solution)/shard_map/ppermute | solution.py:82
  38.3 25.8 %collective-permute-start.4 = (bf16[1024,512]{1,0:T(8,128)(2,1)}, bf16[1024,512]{1,0:T(8,128)(2,1)}, u32[]{:S(2)}, u32[]{:S(2)}) collective-permute-start(bf16[1024,512]{1,0:T(8,128)(2,1)} %copy-done.10), channel_id=1, source_target_pairs={{0,16},{16,0},{1,17},{17,1},{2,18},{18,2},{3,19},{19,3},{4,20},{20... | collective-permute-start | bytes 3145736 | tf_op jit(solution)/shard_map/ppermute | solution.py:82
  40.0 27.3 %collective-permute-start.5 = (bf16[2,256,1024]{2,1,0:T(8,128)(2,1)}, bf16[2,256,1024]{2,1,0:T(8,128)(2,1)}, u32[]{:S(2)}, u32[]{:S(2)}) collective-permute-start(bf16[2,256,1024]{2,1,0:T(8,128)(2,1)} %collective-permute-done.1.refs_1_), channel_id=1, source_target_pairs={{0,1},{1,2},{2,3},{3,0},{4,5},{5,6},{6,7},{7,4},{8,9},{9,10},{10,1... | collective-permute-start | bytes 3145736 | tf_op jit(solution)/shard_map/ppermute | solution.py:82
  41.4 26.0 %collective-permute-start.6 = (bf16[2,256,1024]{2,1,0:T(8,128)(2,1)}, bf16[2,256,1024]{2,1,0:T(8,128)(2,1)}, u32[]{:S(2)}, u32[]{:S(2)}) collective-permute-start(bf16[2,256,1024]{2,1,0:T(8,128)(2,1)} %collective-permute-done.1.refs_1_), channel_id=1, source_target_pairs={{0,4},{4,0},{8,12},{12,8},{1,5},{5,1},{9,13},{13,9},{2,6},{6,2},{1... | collective-permute-start | bytes 3145736 | tf_op jit(solution)/shard_map/ppermute | solution.py:82
  67.4 41.9 %copy-start.7 = (bf16[3,1024,512]{2,1,0:T(8,128)(2,1)}, bf16[3,1024,512]{2,1,0:T(8,128)(2,1)S(1)}, u32[]{:S(2)}) copy-start(bf16[3,1024,512]{2,1,0:T(8,128)(2,1)S(1)} %collective-permute-done.8.refs_10_.refs_11_.refs_3_.refs_4_.refs_5_) | copy-start | bytes 9437188
  67.4 33.6 %collective-permute-start.10 = (bf16[1024,512]{1,0:T(8,128)(2,1)}, bf16[1024,512]{1,0:T(8,128)(2,1)}, u32[]{:S(2)}, u32[]{:S(2)}) collective-permute-start(bf16[1024,512]{1,0:T(8,128)(2,1)} %collective-permute-done.3.refs_14_.refs_10_), channel_id=1, source_target_pairs={{0,16},{16,0},{1,17},{17,1},{2,18},{18,2},{3,19},{19,3},{4,20},{20... | collective-permute-start | bytes 3145736 | tf_op jit(solution)/shard_map/ppermute | solution.py:82
  67.7 33.2 %collective-permute-start.11 = (bf16[2,256,1024]{2,1,0:T(8,128)(2,1)}, bf16[2,256,1024]{2,1,0:T(8,128)(2,1)}, u32[]{:S(2)}, u32[]{:S(2)}) collective-permute-start(bf16[2,256,1024]{2,1,0:T(8,128)(2,1)} %collective-permute-done.5.refs_2_), channel_id=1, source_target_pairs={{0,1},{1,2},{2,3},{3,0},{4,5},{5,6},{6,7},{7,4},{8,9},{9,10},{10,1... | collective-permute-start | bytes 3145736 | tf_op jit(solution)/shard_map/ppermute | solution.py:82
  67.7 33.2 %collective-permute-start.12 = (bf16[2,256,1024]{2,1,0:T(8,128)(2,1)}, bf16[2,256,1024]{2,1,0:T(8,128)(2,1)}, u32[]{:S(2)}, u32[]{:S(2)}) collective-permute-start(bf16[2,256,1024]{2,1,0:T(8,128)(2,1)} %collective-permute-done.5.refs_2_), channel_id=1, source_target_pairs={{0,4},{4,0},{8,12},{12,8},{1,5},{5,1},{9,13},{13,9},{2,6},{6,2},{1... | collective-permute-start | bytes 3145736 | tf_op jit(solution)/shard_map/ppermute | solution.py:82
  67.7 33.2 %collective-permute-start.9 = (bf16[1024,512]{1,0:T(8,128)(2,1)}, bf16[1024,512]{1,0:T(8,128)(2,1)}, u32[]{:S(2)}, u32[]{:S(2)}) collective-permute-start(bf16[1024,512]{1,0:T(8,128)(2,1)} %dynamic-slice_bitcast_fusion), channel_id=1, source_target_pairs={{0,8},{4,12},{8,0},{12,4},{16,28},{20,24},{24,20},{28,16},{1,9},{5... | collective-permute-start | bytes 3145736 | tf_op jit(solution)/shard_map/ppermute | solution.py:82
  69.2 30.0 %collective-permute-start.13 = (bf16[128,1024]{1,0:T(8,128)(2,1)}, bf16[128,1024]{1,0:T(8,128)(2,1)}, u32[]{:S(2)}, u32[]{:S(2)}) collective-permute-start(bf16[128,1024]{1,0:T(8,128)(2,1)} %bitcast.22), channel_id=1, source_target_pairs={{0,8},{4,12},{8,0},{12,4},{1,9},{5,13},{9,1},{13,5},{2,10},{6,14},... | collective-permute-start | bytes 786440 | tf_op jit(solution)/shard_map/ppermute | solution.py:82
  101.0 8.3 %collective-permute-start.14 = (bf16[2,256,1024]{2,1,0:T(8,128)(2,1)}, bf16[2,256,1024]{2,1,0:T(8,128)(2,1)}, u32[]{:S(2)}, u32[]{:S(2)}) collective-permute-start(bf16[2,256,1024]{2,1,0:T(8,128)(2,1)} %collective-permute-done.11.refs_3_), channel_id=1, source_target_pairs={{0,4},{4,0},{8,12},{12,8},{1,5},{5,1},{9,13},{13,9},{2,6},{6,2},{1... | collective-permute-start | bytes 3145736 | tf_op jit(solution)/shard_map/ppermute | solution.py:82
  101.1 25.9 %collective-permute-start.15 = (bf16[512,1024]{1,0:T(8,128)(2,1)}, bf16[512,1024]{1,0:T(8,128)(2,1)}, u32[]{:S(2)}, u32[]{:S(2)}) collective-permute-start(bf16[512,1024]{1,0:T(8,128)(2,1)} %constant_dynamic-slice_fusion), channel_id=1, source_target_pairs={{0,8},{4,12},{8,0},{12,4},{1,9},{5,13},{9,1},{13,5},{2,10},{6,14},... | collective-permute-start | bytes 3145736 | tf_op jit(solution)/shard_map/ppermute | solution.py:82
  102.6 25.5 %collective-permute-start.16 = (bf16[1024,512]{1,0:T(8,128)(2,1)}, bf16[1024,512]{1,0:T(8,128)(2,1)}, u32[]{:S(2)}, u32[]{:S(2)}) collective-permute-start(bf16[1024,512]{1,0:T(8,128)(2,1)} %collective-permute-done.9.refs_6_), channel_id=1, source_target_pairs={{0,16},{16,0},{1,17},{17,1},{2,18},{18,2},{3,19},{19,3},{4,20},{20... | collective-permute-start | bytes 3145736 | tf_op jit(solution)/shard_map/ppermute | solution.py:82
  104.9 23.2 %copy-start.13 = (bf16[128,1024]{1,0:T(8,128)(2,1)S(1)}, bf16[128,1024]{1,0:T(8,128)(2,1)}, u32[]{:S(2)}) copy-start(bf16[128,1024]{1,0:T(8,128)(2,1)} %add.110) | copy-start | bytes 786436
  104.9 25.6 %copy-start.16 = (s32[128]{0:T(128)S(1)}, s32[128]{0:T(128)}, u32[]{:S(2)}) copy-start(s32[128]{0:T(128)} %param.11) | copy-start | bytes 1540
  104.9 21.7 %collective-permute-start.17 = (bf16[128,1024]{1,0:T(8,128)(2,1)}, bf16[128,1024]{1,0:T(8,128)(2,1)S(1)}, u32[]{:S(2)}, u32[]{:S(2)}) collective-permute-start(bf16[128,1024]{1,0:T(8,128)(2,1)} %add.110), channel_id=1, source_target_pairs={{0,1},{1,2},{2,3},{3,0},{4,5},{5,6},{6,7},{7,4},{8,9},{9,10},{10,1... | collective-permute-start | bytes 786440 | tf_op jit(solution)/shard_map/ppermute | solution.py:82
  104.9 21.8 %collective-permute-start.18 = (bf16[128,1024]{1,0:T(8,128)(2,1)}, bf16[128,1024]{1,0:T(8,128)(2,1)S(1)}, u32[]{:S(2)}, u32[]{:S(2)}) collective-permute-start(bf16[128,1024]{1,0:T(8,128)(2,1)} %add.110), channel_id=1, source_target_pairs={{0,2},{1,3},{2,0},{3,1},{4,6},{5,7},{6,4},{7,5},{8,10},{9,11},{10,... | collective-permute-start | bytes 786440 | tf_op jit(solution)/shard_map/ppermute | solution.py:82
  109.3 17.4 %collective-permute-start.19 = (bf16[128,1024]{1,0:T(8,128)(2,1)}, bf16[128,1024]{1,0:T(8,128)(2,1)S(1)}, u32[]{:S(2)}, u32[]{:S(2)}) collective-permute-start(bf16[128,1024]{1,0:T(8,128)(2,1)} %add.110), channel_id=1, source_target_pairs={{0,3},{1,0},{2,1},{3,2},{4,7},{5,4},{6,5},{7,6},{8,11},{9,8},{10,9... | collective-permute-start | bytes 786440 | tf_op jit(solution)/shard_map/ppermute | solution.py:82
  128.2 22.1 %collective-permute-start.23 = (bf16[1024,1024]{1,0:T(8,128)(2,1)}, bf16[1024,1024]{1,0:T(8,128)(2,1)S(1)}, u32[]{:S(2)}, u32[]{:S(2)}) collective-permute-start(bf16[1024,1024]{1,0:T(8,128)(2,1)} %own.1), channel_id=1, source_target_pairs={{0,4},{4,0},{8,12},{12,8},{1,5},{5,1},{9,13},{13,9},{2,6},{6,2},{1... | collective-permute-start | bytes 6291464 | tf_op jit(solution)/shard_map/ppermute | solution.py:82
  128.3 5.7 %copy-start.8 = (bf16[4,128,1024]{2,1,0:T(8,128)(2,1)}, bf16[4,128,1024]{2,1,0:T(8,128)(2,1)S(1)}, u32[]{:S(2)}) copy-start(bf16[4,128,1024]{2,1,0:T(8,128)(2,1)S(1)} %pad_maximum_fusion.mine) | copy-start | bytes 3145732
  128.3 5.6 %collective-permute-start.20 = (bf16[4,128,1024]{2,1,0:T(8,128)(2,1)S(1)}, bf16[4,128,1024]{2,1,0:T(8,128)(2,1)}, u32[]{:S(2)}, u32[]{:S(2)}) collective-permute-start(bf16[4,128,1024]{2,1,0:T(8,128)(2,1)S(1)} %pad_maximum_fusion.mine), channel_id=1, source_target_pairs={{0,4},{4,0},{8,12},{12,8},{1,5},{5,1},{9,13},{13,9},{2,6},{6,2},{1... | collective-permute-start | bytes 3145736 | tf_op jit(solution)/shard_map/ppermute | solution.py:82
  128.9 27.3 %collective-permute-start.27 = (bf16[512,1024]{1,0:T(8,128)(2,1)}, bf16[512,1024]{1,0:T(8,128)(2,1)}, u32[]{:S(2)}, u32[]{:S(2)}) collective-permute-start(bf16[512,1024]{1,0:T(8,128)(2,1)} %collective-permute-done.15.far_x), channel_id=1, source_target_pairs={{0,16},{16,0},{1,17},{17,1},{2,18},{18,2},{3,19},{19,3},{4,20},{20... | collective-permute-start | bytes 3145736 | tf_op jit(solution)/shard_map/ppermute | solution.py:82
  130.9 14.7 %copy-start.1 = (f32[2,4,128,128]{3,2,1,0:T(8,128)S(1)}, f32[2,4,128,128]{3,2,1,0:T(8,128)}, u32[]{:S(2)}) copy-start(f32[2,4,128,128]{3,2,1,0:T(8,128)} %get-tuple-element.106.states) | copy-start | bytes 1572868
  131.0 14.7 %collective-permute-start.21 = (bf16[2,4,128,128]{3,2,1,0:T(8,128)(2,1)}, bf16[2,4,128,128]{3,2,1,0:T(8,128)(2,1)S(1)}, u32[]{:S(2)}, u32[]{:S(2)}) collective-permute-start(bf16[2,4,128,128]{3,2,1,0:T(8,128)(2,1)} %get-tuple-element.107), channel_id=1, source_target_pairs={{0,8},{4,12},{8,0},{12,4},{1,9},{5,13},{9,1},{13,5},{2,10},{6,14},... | collective-permute-start | bytes 786440 | tf_op jit(solution)/shard_map/ppermute | solution.py:82
  145.7 1.0 copy-start.2
  147.7 35.3 %copy-start.3 = (bf16[32,4096]{1,0:T(8,128)(2,1)S(1)}, bf16[32,4096]{1,0:T(8,128)(2,1)}, u32[]{:S(2)}) copy-start(bf16[32,4096]{1,0:T(8,128)(2,1)} %get-tuple-element.103.residual) | copy-start | bytes 786436
  148.9 1.3 collective-permute-start.22
  149.6 13.8 %collective-permute-start.28 = (bf16[512,1024]{1,0:T(8,128)(2,1)}, bf16[512,1024]{1,0:T(8,128)(2,1)S(1)}, u32[]{:S(2)}, u32[]{:S(2)}) collective-permute-start(bf16[512,1024]{1,0:T(8,128)(2,1)} %collective-permute-done.15.far_x), channel_id=1, source_target_pairs={{0,4},{4,0},{8,12},{12,8},{1,5},{5,1},{9,13},{13,9},{2,6},{6,2},{1... | collective-permute-start | bytes 3145736 | tf_op jit(solution)/shard_map/ppermute | solution.py:82
  150.2 1.4 copy-start.9
  156.2 7.2 %collective-permute-start.29 = (bf16[512,1024]{1,0:T(8,128)(2,1)}, bf16[512,1024]{1,0:T(8,128)(2,1)S(1)}, u32[]{:S(2)}, u32[]{:S(2)}) collective-permute-start(bf16[512,1024]{1,0:T(8,128)(2,1)} %collective-permute-done.27.far_y), channel_id=1, source_target_pairs={{0,4},{4,0},{8,12},{12,8},{1,5},{5,1},{9,13},{13,9},{2,6},{6,2},{1... | collective-permute-start | bytes 3145736 | tf_op jit(solution)/shard_map/ppermute | solution.py:82
  156.4 16.2 %collective-permute-start.24 = (bf16[32,2048]{1,0:T(8,128)(2,1)}, bf16[32,2048]{1,0:T(8,128)(2,1)S(1)}, u32[]{:S(2)}, u32[]{:S(2)}) collective-permute-start(bf16[32,2048]{1,0:T(8,128)(2,1)} %get-tuple-element.112), channel_id=1, source_target_pairs={{0,1},{1,2},{2,3},{3,0},{4,5},{5,6},{6,7},{7,4},{8,9},{9,10},{10,1... | collective-permute-start | bytes 393224 | tf_op jit(solution)/shard_map/ppermute | solution.py:82
  161.1 12.8 %collective-permute-start.25 = (bf16[32,2048]{1,0:T(8,128)(2,1)}, bf16[32,2048]{1,0:T(8,128)(2,1)S(1)}, u32[]{:S(2)}, u32[]{:S(2)}) collective-permute-start(bf16[32,2048]{1,0:T(8,128)(2,1)} %get-tuple-element.113), channel_id=1, source_target_pairs={{0,2},{1,3},{2,0},{3,1},{4,6},{5,7},{6,4},{7,5},{8,10},{9,11},{10,... | collective-permute-start | bytes 393224 | tf_op jit(solution)/shard_map/ppermute | solution.py:82
  161.1 12.8 %collective-permute-start.26 = (bf16[32,2048]{1,0:T(8,128)(2,1)}, bf16[32,2048]{1,0:T(8,128)(2,1)S(1)}, u32[]{:S(2)}, u32[]{:S(2)}) collective-permute-start(bf16[32,2048]{1,0:T(8,128)(2,1)} %get-tuple-element.114), channel_id=1, source_target_pairs={{0,3},{1,0},{2,1},{3,2},{4,7},{5,4},{6,5},{7,6},{8,11},{9,8},{10,9... | collective-permute-start | bytes 393224 | tf_op jit(solution)/shard_map/ppermute | solution.py:82
  163.5 1.0 copy-start.11
  164.5 1.0 copy-start.12
  170.0 8.5 %collective-permute-start.30 = (bf16[32,2048]{1,0:T(8,128)(2,1)}, bf16[32,2048]{1,0:T(8,128)(2,1)S(1)}, u32[]{:S(2)}, u32[]{:S(2)}) collective-permute-start(bf16[32,2048]{1,0:T(8,128)(2,1)} %get-tuple-element.120), channel_id=1, source_target_pairs={{0,1},{1,2},{2,3},{3,0},{4,5},{5,6},{6,7},{7,4},{8,9},{9,10},{10,1... | collective-permute-start | bytes 393224 | tf_op jit(solution)/shard_map/ppermute | solution.py:82
  170.0 12.9 %collective-permute-start.31 = (bf16[32,2048]{1,0:T(8,128)(2,1)}, bf16[32,2048]{1,0:T(8,128)(2,1)S(1)}, u32[]{:S(2)}, u32[]{:S(2)}) collective-permute-start(bf16[32,2048]{1,0:T(8,128)(2,1)} %get-tuple-element.121), channel_id=1, source_target_pairs={{0,2},{1,3},{2,0},{3,1},{4,6},{5,7},{6,4},{7,5},{8,10},{9,11},{10,... | collective-permute-start | bytes 393224 | tf_op jit(solution)/shard_map/ppermute | solution.py:82
  172.6 10.3 %collective-permute-start.32 = (bf16[32,2048]{1,0:T(8,128)(2,1)}, bf16[32,2048]{1,0:T(8,128)(2,1)S(1)}, u32[]{:S(2)}, u32[]{:S(2)}) collective-permute-start(bf16[32,2048]{1,0:T(8,128)(2,1)} %get-tuple-element.122), channel_id=1, source_target_pairs={{0,3},{1,0},{2,1},{3,2},{4,7},{5,4},{6,5},{7,6},{8,11},{9,8},{10,9... | collective-permute-start | bytes 393224 | tf_op jit(solution)/shard_map/ppermute | solution.py:82
  185.7 7.5 %collective-permute-start.33 = (bf16[32,1024]{1,0:T(8,128)(2,1)S(1)}, bf16[32,1024]{1,0:T(8,128)(2,1)S(1)}, u32[]{:S(2)}, u32[]{:S(2)}) collective-permute-start(bf16[32,1024]{1,0:T(8,128)(2,1)S(1)} %get-tuple-element.124), channel_id=1, source_target_pairs={{0,1},{1,2},{2,3},{3,0},{4,5},{5,6},{6,7},{7,4},{8,9},{9,10},{10,1... | collective-permute-start | bytes 196616 | tf_op jit(solution)/shard_map/ppermute | solution.py:82
  188.1 6.9 %collective-permute-start.34 = (bf16[32,1024]{1,0:T(8,128)(2,1)S(1)}, bf16[32,1024]{1,0:T(8,128)(2,1)S(1)}, u32[]{:S(2)}, u32[]{:S(2)}) collective-permute-start(bf16[32,1024]{1,0:T(8,128)(2,1)S(1)} %get-tuple-element.125), channel_id=1, source_target_pairs={{0,2},{1,3},{2,0},{3,1},{4,6},{5,7},{6,4},{7,5},{8,10},{9,11},{10,... | collective-permute-start | bytes 196616 | tf_op jit(solution)/shard_map/ppermute | solution.py:82
  190.7 5.0 %collective-permute-start.35 = (bf16[32,1024]{1,0:T(8,128)(2,1)S(1)}, bf16[32,1024]{1,0:T(8,128)(2,1)S(1)}, u32[]{:S(2)}, u32[]{:S(2)}) collective-permute-start(bf16[32,1024]{1,0:T(8,128)(2,1)S(1)} %get-tuple-element.126), channel_id=1, source_target_pairs={{0,3},{1,0},{2,1},{3,2},{4,7},{5,4},{6,5},{7,6},{8,11},{9,8},{10,9... | collective-permute-start | bytes 196616 | tf_op jit(solution)/shard_map/ppermute | solution.py:82
  (5 other events, 4.2 us)

commit v3 on v2

--- a/solution.py
+++ b/solution.py
@@ -147,30 +147,40 @@
         rounded[p, 0] = state.astype(BF16)
 
 
-def project_kernel(nhead, steps, meta, mine, other, *refs):
+def project_kernel(nhead, steps, meta, *refs):
+    mine, other, refs = refs[:nhead], refs[nhead : 2 * nhead], refs[2 * nhead :]
     own, sib = refs[:3], refs[3:6]
     far = refs[6:8], refs[8:10], refs[10:12]
-    query_out, local_out, residual, held, sems = refs[12:]
-    rows, features = held.shape
-    depth = features // (2 * nhead)
+    query_out, local_out, residual, held = refs[12:]
+    rows, block = held.shape[1:]
+    features = nhead * block
 
     @pl.when(pl.program_id(0) == 0)
     def _():
-        fetch_rows(meta, [ref.at[k] for ref in (mine, other) for k in range(nhead)], 2, held, sems)
+        for k in range(nhead):
+            held[meta[k], : rows // 2] = mine[k][...]
+            held[meta[k], rows // 2 :] = other[k][...]
         share = residual.shape[0]
         at = pl.multiple_of(meta[nhead] * share, share)
-        residual[...] = held[pl.ds(at, share), :]
-        squares = jnp.zeros((rows, 1), F32)
-        for i in range(0, features, depth):
-            part = held[:, i : i + depth].astype(F32)
-            squares += jnp.sum(part * part, axis=-1, keepdims=True)
-        scale = lax.rsqrt(squares / features + 1e-06)
-        for i in range(0, features, depth):
-            held[:, i : i + depth] = (held[:, i : i + depth].astype(F32) * scale).astype(BF16)
-
-    query, key, value = (
-        held_dot(held, [own[i][0], sib[i][0]] + [ref[...] for ref in far[i]]).astype(BF16) for i in range(3)
-    )
+        for j in range(nhead):
+            residual[:, j * block : (j + 1) * block] = held[j, pl.ds(at, share), :]
+
+    blocks = [held[j] for j in range(nhead)]
+
+    squares = jnp.zeros((rows, 1), F32)
+    for part in blocks:
+        part = part.astype(F32)
+        squares += jnp.sum(part * part, axis=-1, keepdims=True)
+    scale = lax.rsqrt(squares / features + 1e-06)
+
+    def projected(i):
+        total = None
+        for part, weight in zip(blocks, (own[i][0], sib[i][0], far[i][0][...], far[i][1][...])):
+            term = jnp.dot(part, weight, preferred_element_type=F32)
+            total = term if total is None else total + term
+        return (total * scale).astype(BF16)
+
+    query, key, value = (projected(i) for i in range(3))
     query_out[...] = query
     query, key, value = query.astype(F32), key.astype(F32), value.astype(F32)
     each = rows // 2 // steps
@@ -339,42 +349,6 @@
     def cross(array):
         return permute(array, ("grp", "ctx"), fetch)
 
-    first_half, later_weight = tie((fetched(1, qkv_weight), qkv_weight))
-    keys_x = cross(first_half)
-    tokens = [prompt_hidden, up(prompt_hidden)]
-    sib_tokens = [sib(prompt_hidden)]
-    looked = lookup(response_ids)
-
-    keys_x, tokens, sib_tokens, looked, next_half, later_weight = tie(
-        (keys_x, tokens, sib_tokens, looked, fetched(2, later_weight), later_weight)
-    )
-    values_x = cross(next_half)
-    keys_y = swap(keys_x)
-    tokens.append(up(tokens[1]))
-    sib_tokens.append(sib(tokens[1]))
-    given, halves_of = by_core(looked)
-    mine, given = halves_of(sib(given))
-    sib_weight = sib(lax.dynamic_slice(later_weight, (0, 0, (1 - core) * cols), (3, block, cols)))
-
-    values_x, keys_y, tokens, sib_tokens, mine, given, next_half, sib_weight = tie(
-        (values_x, keys_y, tokens, sib_tokens, mine, given, fetched(0, later_weight), sib_weight)
-    )
-    query_x = cross(next_half)
-    given = permute(given, "ctx", to_far)
-    values_y = swap(values_x)
-    tokens.append(up(tokens[2]))
-    sib_tokens.append(sib(tokens[2]))
-    embedded = mine + given
-    out_half = lax.dynamic_slice(out_weight, (grp * depth, 0), (depth, width))
-
-    query_x, values_y, tokens, sib_tokens, embedded, out_half = tie(
-        (query_x, values_y, tokens, sib_tokens, embedded, out_half)
-    )
-    out_x = permute(out_half, "ctx", to_far)
-    query_y = swap(query_x)
-    e = [embedded] + [permute(embedded, "head", shift_pairs(nhead, k)) for k in range(1, nhead)]
-    sib_tokens.append(sib(tokens[3]))
-
     places = []
     for k in range(nhead):
         place = ctx ^ ((head - k) % nhead)
@@ -382,11 +356,60 @@
     meta = jnp.stack(places + [head, core, grp]).astype(jnp.int32)
     at_core = nhead + 1
 
+    ahead = [(head + k) % nhead for k in range(nhead)]
+    out_meta = jnp.stack(ahead + [core, grp]).astype(jnp.int32)
+    norm_meta = [ctx ^ f for f in ahead]
+    norm_meta = jnp.stack([jnp.where(j < 2, j, j ^ grp) for j in norm_meta]).astype(jnp.int32)
+    behind = jnp.stack([(head - k) % nhead for k in range(nhead)]).astype(jnp.int32)
+    which = [
+        jnp.tile(lax.dynamic_slice_in_dim(assignment, owner * resp_local, resp_local, 0), steps)
+        for owner in (ctx, ctx ^ 1)
+    ]
+    chosen = jnp.concatenate(which)[:, None]
+
+    first_half, later_weight, prompt_hidden = tie((fetched(1, qkv_weight), qkv_weight, prompt_hidden))
+    tokens = [prompt_hidden, up(prompt_hidden)]
+    keys_x = cross(first_half)
+    sib_tokens = [sib(prompt_hidden)]
+    sib_weight = sib(later_weight)
+    next_half, ids, later_weight = tie((fetched(2, later_weight), response_ids, later_weight))
+    given, halves_of = by_core(lookup(ids))
+
+    metas = (meta, out_meta, norm_meta, behind, chosen)
+    tokens, keys_x, sib_tokens, sib_weight, given, next_half, later_weight, metas = tie(
+        (tokens, keys_x, sib_tokens, sib_weight, given, next_half, later_weight, metas)
+    )
+    meta, out_meta, norm_meta, behind, chosen = metas
+    tokens.append(up(tokens[1]))
+    values_x = cross(next_half)
+    keys_y = swap(keys_x)
+    sib_tokens.append(sib(tokens[1]))
+    mine, given = halves_of(sib(given))
+    given = permute(given, "ctx", to_far)
+
+    tokens, values_x, keys_y, sib_tokens, mine, given, next_half = tie(
+        (tokens, values_x, keys_y, sib_tokens, mine, given, fetched(0, later_weight))
+    )
+    tokens.append(up(tokens[2]))
+    query_x = cross(next_half)
+    values_y = swap(values_x)
+    sib_tokens.append(sib(tokens[2]))
+    embedded = mine + given
+    sib_e = [sib(embedded)]
+    out_half = lax.dynamic_slice(out_weight, (grp * depth, 0), (depth, width))
+
+    tokens, query_x, values_y, sib_tokens, embedded, sib_e, out_half = tie(
+        (tokens, query_x, values_y, sib_tokens, embedded, sib_e, out_half)
+    )
+    out_x = permute(out_half, "ctx", to_far)
+    query_y = swap(query_x)
+    e = [embedded] + [permute(embedded, "head", shift_pairs(nhead, k)) for k in range(1, nhead)]
+    sib_tokens.append(sib(tokens[3]))
+
     def own_spec(k, wide):
         return pl.BlockSpec((1, block, wide), lambda n, m: (k, 0, m[at_core] * (cols // wide) + n))
 
-    def sib_spec(k, wide):
-        return pl.BlockSpec((1, block, wide), lambda n, m: (k, 0, n))
+    sib_spec = own_spec
 
     def far_spec(wide):
         return pl.BlockSpec((block, wide), lambda n, m: (0, n))
@@ -433,13 +456,12 @@
         *far_of(2),
     )
 
-    states, rounded, out_x, query_y, query_x, e, out_own = tie(
-        (states, rounded, out_x, query_y, query_x, e, out_weight)
-    )
+    states, rounded, out_x, query_y, query_x, e, sib_e, out_own = tie(
+        (states, rounded, out_x, query_y, query_x, e, sib_e, out_weight)
+    )
+    sib_e += [sib(array) for array in e[1:]]
     out_y = swap(out_x)
     others = permute(rounded, "ctx", to_far)
-    e = jnp.stack(e)
-    sib_e = sib(e)
 
     chip_rows = 2 * rows_local
     share = rows_local // nhead
@@ -455,15 +477,12 @@
         grid_spec=pltpu.PrefetchScalarGridSpec(
             num_scalar_prefetch=1,
             grid=(cols // wide,),
-            in_specs=anywhere(2)
+            in_specs=[pl.BlockSpec((rows_local, block), lambda n, m: (0, 0))] * nblocks
             + [own_spec(k, wide) for k in range(3)]
             + [sib_spec(k, wide) for k in range(3)]
             + [far_spec(wide)] * 6,
             out_specs=(row_spec, row_spec, pl.BlockSpec((share, nhead * block), lambda n, m: (0, 0))),
-            scratch_shapes=[
-                pltpu.VMEM((chip_rows, nhead * block), BF16),
-                pltpu.SemaphoreType.DMA((nblocks,)),
-            ],
+            scratch_shapes=[pltpu.VMEM((nhead, chip_rows, block), BF16)],
         ),
         compiler_params=pltpu.CompilerParams(vmem_limit_bytes=VMEM_LIMIT),
         cost_estimate=pl.CostEstimate(
@@ -472,8 +491,8 @@
         name="response_rows",
     )(
         meta,
-        e,
-        sib_e,
+        *e,
+        *sib_e,
         *([qkv_weight] * 3),
         *([sib_weight] * 3),
         *far_of(0),
@@ -481,28 +500,21 @@
         *far_of(2),
     )
 
-    which = [
-        jnp.tile(lax.dynamic_slice_in_dim(assignment, owner * resp_local, resp_local, 0), steps)
-        for owner in (ctx, ctx ^ 1)
-    ]
     heads_own, heads_sib = pl.pallas_call(
         attend_kernel,
         out_shape=(jax.ShapeDtypeStruct((rows_local, cols), BF16),) * 2,
         compiler_params=pltpu.CompilerParams(vmem_limit_bytes=VMEM_SMALL),
         name="attend",
-    )(query, local, jnp.concatenate(which)[:, None], states, others)
+    )(query, local, chosen, states, others)
     heads_sib = sib(heads_sib)
     out_sib = sib(out_own)
-
-    ahead = [(head + k) % nhead for k in range(nhead)]
-    out_meta = jnp.stack(ahead + [core, grp]).astype(jnp.int32)
 
     def spread(kernel, name, heads, operands, scratch):
         outs = (jax.ShapeDtypeStruct((share, 2 * width), F32),)
         outs += (jax.ShapeDtypeStruct((share, 2 * width), BF16),) * (nhead - 1)
         scratch = [*scratch, pltpu.VMEM((rows_local, 2 * width), F32)]
         flops = 4 * rows_local * block * width
-        terms = small_call(kernel, name, out_meta, (*heads, *operands), outs, scratch, flops, VMEM_LIMIT)
+        terms = small_call(kernel, name, out_meta, (*heads, *operands), outs, scratch, flops)
         moved = {k: permute(terms[k], "head", shift_pairs(nhead, k)) for k in (2, 3, 1)}
         return [terms[0]] + [moved[k] for k in range(1, nhead)]
 
@@ -516,8 +528,6 @@
         (out_x, out_y, diag_x, sib(out_y)),
         [pltpu.VMEM((2, rows_local, cols), BF16)],
     )
-    norm_meta = [ctx ^ f for f in ahead]
-    norm_meta = jnp.stack([jnp.where(j < 2, j, j ^ grp) for j in norm_meta]).astype(jnp.int32)
     normed = small_call(
         functools.partial(norm_kernel, nhead),
         "final_norm",
@@ -527,7 +537,6 @@
         [pltpu.VMEM((nhead, share, width), F32)],
     )
     pieces = [normed[0]] + [permute(normed[k], "head", shift_pairs(nhead, k)) for k in range(1, nhead)]
-    behind = jnp.stack([(head - k) % nhead for k in range(nhead)]).astype(jnp.int32)
     result = small_call(
         place_kernel, "place", behind, pieces, jax.ShapeDtypeStruct((rows_local, width), BF16)
     )

time: 198 us -> 182 us (0.919)
  local copies, waits for them, and re-layouts: 33.9 us -> 23.4 us
  Pallas kernels: 40.7 us -> 34.9 us
  starting transfers between devices: 37.3 us -> 40.6 us
  other arithmetic: 6.5 us -> 4.38 us
    unnamed x35 -> x22, local copies, waits for them, and re-layouts: 8.03 us -> 2.02 us
    pallas_call x4, Pallas kernels: 11.2 us -> 7.52 us  [small_call(): pl.pallas_call(kernel, out_shape=outs, grid_spec=pltpu.PrefetchScalarGrid...]
    ppermute x36 -> x39, starting transfers between devices: 37.3 us -> 40.6 us  [permute(): return lax.ppermute(array, axis, pairs)]
    dynamic_slice x1, local copies, waits for them, and re-layouts: 3.71 us -> 0.85 us  [by_core(): given = lax.dynamic_index_in_dim(looked, 1 - core, 2, keepdims=False)]
    pallas_call x1, Pallas kernels: 11.7 us -> 9.42 us  [permuted_plan(): pl.pallas_call(functools.partial(project_kernel, nhead, steps), out_shape...]
    dynamic_slice x1, local copies, waits for them, and re-layouts: 2.33 us -> 0.08 us  [permuted_plan(): out_half = lax.dynamic_slice(out_weight, (grp * depth, 0), (depth, width))]
    ppermute x36 -> x39, waiting for transfers between devices: 78.2 us -> 77.6 us  [permute(): return lax.ppermute(array, axis, pairs)]
  transfers between devices with their start and end apart: 36 -> 39, of which waited for: 17 -> 16; matrix products, arithmetic and copies ran while one was open for 14% -> 13% of each run, Pallas kernels for 20% -> 18%
where the time goes in v3:
time: 182 us; the launch traced here: 181 us
  waiting for transfers between devices  77.6 us (43%)
  starting transfers between devices  40.6 us (22%)
  Pallas kernels  34.9 us (19%)
  local copies, waits for them, and re-layouts  23.4 us (13%)
  other arithmetic  4.38 us (2%)
    ppermute x39, waiting for transfers between devices, permute(): return lax.ppermute(array, axis, pairs)  77.6 us
    ppermute x39, starting transfers between devices, permute(): return lax.ppermute(array, axis, pairs)  40.6 us
    pallas_call x1, Pallas kernels, permuted_plan(): pl.pallas_call(functools.partial(state_kernel, nblocks), out_shape=(jax.S...  17.4 us
    gather x1, local copies, waits for them, and re-layouts, lookup(): jnp.take(embed_table, jnp.clip(offset_ids, 0, embed_table.shape[0] - 1),...  11.4 us
    pallas_call x1, Pallas kernels, permuted_plan(): pl.pallas_call(functools.partial(project_kernel, nhead, steps), out_shape...  9.42 us
    pallas_call x4, Pallas kernels, small_call(): pl.pallas_call(kernel, out_shape=outs, grid_spec=pltpu.PrefetchScalarGrid...  7.52 us
    squeeze x3, local copies, waits for them, and re-layouts, fetched(): lax.dynamic_slice(weight, (k, 0, (core ^ grp) * cols), (1, block, cols))[0]  6.86 us
  transfers between devices with their start and end apart: 39, of which 16 were waited for; matrix products, arithmetic and copies ran while one was open for 13% of the time, Pallas kernels for 18%

profile of v3, /device:TPU:0, one launch (start us, length us, event | category | flops | bytes accessed | tf_op | source)
XLA Modules:
  0.0 181.2 jit_solution(17591858451514744246)
XLA Ops:
  0.0 2.3 %dynamic-slice_bitcast_fusion.2 = bf16[1024,512]{1,0:T(8,128)(2,1)} fusion(bf16[3,1024,1024]{2,1,0:T(8,128)(2,1)} %refs_10_.1, s32[]{:T(128)S(6)} %select_n.115), kind=kLoop, calls=%fused_computation.4 | loop fusion | bytes 2097156 | tf_op jit(solution)/shard_map/squeeze | solution.py:347
  2.7 2.6 %collective-permute-start = (bf16[2,256,1024]{2,1,0:T(8,128)(2,1)}, bf16[2,256,1024]{2,1,0:T(8,128)(2,1)}, u32[]{:S(2)}, u32[]{:S(2)}) collective-permute-start(bf16[2,256,1024]{2,1,0:T(8,128)(2,1)} %refs_0_), channel_id=1, source_target_pairs={{0,1},{1,2},{2,3},{3,0},{4,5},{5,6},{6,7},{7,4},{8,9},{9,10},{10,1... | collective-permute-start | bytes 3145736 | tf_op jit(solution)/shard_map/ppermute | solution.py:82
  5.5 1.5 collective-permute-start.1
  7.0 2.3 %dynamic-slice_bitcast_fusion.1 = bf16[1024,512]{1,0:T(8,128)(2,1)} fusion(bf16[3,1024,1024]{2,1,0:T(8,128)(2,1)} %refs_10_.1, s32[]{:T(128)S(6)} %select_n.115), kind=kLoop, calls=%fused_computation.3 | loop fusion | bytes 2097156 | tf_op jit(solution)/shard_map/squeeze | solution.py:347
  10.9 11.4 %gather_fusion = bf16[512,1024]{1,0:T(8,128)(2,1)} fusion(bf16[8192,1024]{1,0:T(8,128)(2,1)} %param.9, s32[1024]{0:T(1024)S(1)} %pad_clamp_fusion), kind=kCustom, calls=%fused_computation | custom fusion | bytes 2099200 | tf_op jit(solution)/shard_map/jit(_take)/gather | solution.py:324
  22.3 1.6 select_select_fusion
  23.9 0.9 constant_dynamic-slice_fusion.3
  24.8 0.8 copy.14
  26.7 4.7 %collective-permute-done.refs_1_ = bf16[2,256,1024]{2,1,0:T(8,128)(2,1)} collective-permute-done((bf16[2,256,1024]{2,1,0:T(8,128)(2,1)}, bf16[2,256,1024]{2,1,0:T(8,128)(2,1)}, u32[]{:S(2)}, u32[]{:S(2)}) %collective-permute-start) | collective-permute-done | bytes 1048608 | tf_op jit(solution)/shard_map/ppermute | solution.py:82
  31.6 1.2 collective-permute-start.4
  32.8 1.5 collective-permute-start.5
  34.3 1.0 collective-permute-start.6
  35.5 1.3 bitcast_add_fusion
  37.4 2.3 %dynamic-slice_bitcast_fusion = bf16[1024,512]{1,0:T(8,128)(2,1)} fusion(bf16[3,1024,1024]{2,1,0:T(8,128)(2,1)} %refs_10_.1, s32[]{:T(128)S(6)} %select_n.115), kind=kLoop, calls=%fused_computation.1 | loop fusion | bytes 2097156 | tf_op jit(solution)/shard_map/squeeze | solution.py:347
  39.7 24.1 %collective-permute-done.9 = bf16[128,1024]{1,0:T(8,128)(2,1)S(1)} collective-permute-done((bf16[128,1024]{1,0:T(8,128)(2,1)S(1)}, bf16[128,1024]{1,0:T(8,128)(2,1)S(1)}, u32[]{:S(2)}, u32[]{:S(2)}) %collective-permute-start.9) | collective-permute-done | bytes 262176 | tf_op jit(solution)/shard_map/ppermute | solution.py:82
  63.9 1.6 collective-permute-start.10
  65.5 1.5 collective-permute-start.11
  67.0 0.9 collective-permute-start.12
  68.7 2.5 %collective-permute-done.14.refs_4_ = bf16[128,1024]{1,0:T(8,128)(2,1)} collective-permute-done((bf16[128,1024]{1,0:T(8,128)(2,1)S(1)}, bf16[128,1024]{1,0:T(8,128)(2,1)}, u32[]{:S(2)}, u32[]{:S(2)}) %collective-permute-start.14) | collective-permute-done | bytes 262176 | tf_op jit(solution)/shard_map/ppermute | solution.py:82
  71.2 19.2 %collective-permute-done.10.refs_3_ = bf16[2,256,1024]{2,1,0:T(8,128)(2,1)} collective-permute-done((bf16[2,256,1024]{2,1,0:T(8,128)(2,1)}, bf16[2,256,1024]{2,1,0:T(8,128)(2,1)}, u32[]{:S(2)}, u32[]{:S(2)}) %collective-permute-start.10) | collective-permute-done | bytes 1048608 | tf_op jit(solution)/shard_map/ppermute | solution.py:82
  90.4 1.9 %collective-permute-done.12.refs_15_.refs_19_ = bf16[1024,512]{1,0:T(8,128)(2,1)} collective-permute-done((bf16[1024,512]{1,0:T(8,128)(2,1)}, bf16[1024,512]{1,0:T(8,128)(2,1)}, u32[]{:S(2)}, u32[]{:S(2)}) %collective-permute-start.12) | collective-permute-done | bytes 1048608 | tf_op jit(solution)/shard_map/ppermute | solution.py:82
  93.0 1.7 collective-permute-start.17
  95.0 2.5 %collective-permute-start.19 = (bf16[128,1024]{1,0:T(8,128)(2,1)S(1)}, bf16[128,1024]{1,0:T(8,128)(2,1)}, u32[]{:S(2)}, u32[]{:S(2)}) collective-permute-start(bf16[128,1024]{1,0:T(8,128)(2,1)S(1)} %add.105.refs_0_), channel_id=1, source_target_pairs={{0,2},{1,3},{2,0},{3,1},{4,6},{5,7},{6,4},{7,5},{8,10},{9,11},{10,... | collective-permute-start | bytes 786440 | tf_op jit(solution)/shard_map/ppermute | solution.py:82
  97.5 1.9 %collective-permute-start.20 = (bf16[128,1024]{1,0:T(8,128)(2,1)S(1)}, bf16[128,1024]{1,0:T(8,128)(2,1)}, u32[]{:S(2)}, u32[]{:S(2)}) collective-permute-start(bf16[128,1024]{1,0:T(8,128)(2,1)S(1)} %add.105.refs_0_), channel_id=1, source_target_pairs={{0,3},{1,0},{2,1},{3,2},{4,7},{5,4},{6,5},{7,6},{8,11},{9,8},{10,9... | collective-permute-start | bytes 786440 | tf_op jit(solution)/shard_map/ppermute | solution.py:82
  99.4 17.4 %prompt_state.1 = (f32[2,4,128,128]{3,2,1,0:T(8,128)}, bf16[2,4,128,128]{3,2,1,0:T(8,128)(2,1)}) custom-call(s32[7]{0:T(128)} %stack.74.meta, bf16[2,256,1024]{2,1,0:T(8,128)(2,1)} %refs_0_, bf16[2,256,1024]{2,1,0:T(8,128)(2,1)} %collective-permute-done.refs_1_, bf16[2,256,1024]{2,1,0:T(8,128)(2,1)} %collective-permute-done.4.refs_2_, ...), custom_call_target="tpu_custom_call" | custom-call | flops 8589934592 | bytes 16777216 | tf_op jit(solution)/shard_map/prompt_state/pallas_call | solution.py:424
  116.9 1.0 collective-permute-done.16.far_x
  118.4 1.7 collective-permute-start.30
  121.0 2.5 %collective-permute-done.21.refs_5_ = bf16[128,1024]{1,0:T(8,128)(2,1)S(1)} collective-permute-done((bf16[128,1024]{1,0:T(8,128)(2,1)}, bf16[128,1024]{1,0:T(8,128)(2,1)S(1)}, u32[]{:S(2)}, u32[]{:S(2)}) %collective-permute-start.21) | collective-permute-done | bytes 262176 | tf_op jit(solution)/shard_map/ppermute | solution.py:82
  123.5 1.5 collective-permute-start.24
  125.0 9.4 %response_rows.1 = (bf16[256,512]{1,0:T(8,128)(2,1)}, f32[256,512]{1,0:T(8,128)}, bf16[32,4096]{1,0:T(8,128)(2,1)}) custom-call(s32[7]{0:T(128)} %stack.74.meta, bf16[128,1024]{1,0:T(8,128)(2,1)} %copy-done.6, bf16[128,1024]{1,0:T(8,128)(2,1)} %collective-permute-done.18.refs_1_, bf16[128,1024]{1,0:T(8,128)(2,1)} %collective-permute-done.19.refs_2_, ...), custom_call_target="tpu_custom_call" | custom-call | flops 3221225472 | bytes 14680064 | tf_op jit(solution)/shard_map/response_rows/pallas_call | solution.py:470
  134.5 1.0 copy-done.2
  135.5 0.9 copy-done.4
  138.4 2.9 %near_terms.1 = (f32[32,2048]{1,0:T(8,128)S(1)}, bf16[32,2048]{1,0:T(8,128)(2,1)S(1)}, bf16[32,2048]{1,0:T(8,128)(2,1)S(1)}, bf16[32,2048]{1,0:T(8,128)(2,1)S(1)}) custom-call(s32[6]{0:T(128)S(1)} %stack.79.meta, bf16[128,512]{1,0:T(8,128)(2,1)S(1)} %get-tuple-element.138.heads_own, bf16[128,512]{1,0:T(8,128)(2,1)S(1)} %collective-permute-done.25.heads_sib, ...), custom_call_target="tpu_custom_call" | custom-call | flops 536870912 | bytes 4194304 | tf_op jit(solution)/shard_map/near_terms/pallas_call | solution.py:288
  141.3 2.8 %collective-permute-done.30.far_y = bf16[512,1024]{1,0:T(8,128)(2,1)} collective-permute-done((bf16[512,1024]{1,0:T(8,128)(2,1)S(1)}, bf16[512,1024]{1,0:T(8,128)(2,1)}, u32[]{:S(2)}, u32[]{:S(2)}) %collective-permute-start.30) | collective-permute-done | bytes 1048608 | tf_op jit(solution)/shard_map/ppermute | solution.py:82
  144.1 3.0 %collective-permute-start.27 = (bf16[32,2048]{1,0:T(8,128)(2,1)S(1)}, bf16[32,2048]{1,0:T(8,128)(2,1)S(1)}, u32[]{:S(2)}, u32[]{:S(2)}) collective-permute-start(bf16[32,2048]{1,0:T(8,128)(2,1)S(1)} %get-tuple-element.134), channel_id=1, source_target_pairs={{0,1},{1,2},{2,3},{3,0},{4,5},{5,6},{6,7},{7,4},{8,9},{9,10},{10,1... | collective-permute-start | bytes 393224 | tf_op jit(solution)/shard_map/ppermute | solution.py:82
  147.1 1.7 collective-permute-start.28
  149.4 2.5 %far_terms.1 = (f32[32,2048]{1,0:T(8,128)S(1)}, bf16[32,2048]{1,0:T(8,128)(2,1)S(1)}, bf16[32,2048]{1,0:T(8,128)(2,1)S(1)}, bf16[32,2048]{1,0:T(8,128)(2,1)S(1)}) custom-call(s32[6]{0:T(128)S(1)} %stack.79.meta, bf16[128,512]{1,0:T(8,128)(2,1)S(1)} %get-tuple-element.138.heads_own, bf16[128,512]{1,0:T(8,128)(2,1)S(1)} %collective-permute-done.25.heads_sib, ...), custom_call_target="tpu_custom_call" | custom-call | flops 536870912 | bytes 4194304 | tf_op jit(solution)/shard_map/far_terms/pallas_call | solution.py:288
  152.0 1.4 collective-permute-start.33
  153.4 1.2 collective-permute-start.34
  154.6 1.2 collective-permute-start.35
  155.9 2.4 %collective-permute-done.28.refs_2_ = bf16[32,2048]{1,0:T(8,128)(2,1)S(1)} collective-permute-done((bf16[32,2048]{1,0:T(8,128)(2,1)S(1)}, bf16[32,2048]{1,0:T(8,128)(2,1)S(1)}, u32[]{:S(2)}, u32[]{:S(2)}) %collective-permute-start.28) | collective-permute-done | bytes 131104 | tf_op jit(solution)/shard_map/ppermute | solution.py:82
  158.3 2.8 %collective-permute-done.33.refs_5_ = bf16[32,2048]{1,0:T(8,128)(2,1)S(1)} collective-permute-done((bf16[32,2048]{1,0:T(8,128)(2,1)S(1)}, bf16[32,2048]{1,0:T(8,128)(2,1)S(1)}, u32[]{:S(2)}, u32[]{:S(2)}) %collective-permute-start.33) | collective-permute-done | bytes 131104 | tf_op jit(solution)/shard_map/ppermute | solution.py:82
  161.1 8.2 %collective-permute-done.34.refs_6_ = bf16[32,2048]{1,0:T(8,128)(2,1)S(1)} collective-permute-done((bf16[32,2048]{1,0:T(8,128)(2,1)S(1)}, bf16[32,2048]{1,0:T(8,128)(2,1)S(1)}, u32[]{:S(2)}, u32[]{:S(2)}) %collective-permute-start.34) | collective-permute-done | bytes 131104 | tf_op jit(solution)/shard_map/ppermute | solution.py:82
  170.1 3.4 %collective-permute-start.36 = (bf16[32,1024]{1,0:T(8,128)(2,1)S(1)}, bf16[32,1024]{1,0:T(8,128)(2,1)S(1)}, u32[]{:S(2)}, u32[]{:S(2)}) collective-permute-start(bf16[32,1024]{1,0:T(8,128)(2,1)S(1)} %get-tuple-element.146), channel_id=1, source_target_pairs={{0,1},{1,2},{2,3},{3,0},{4,5},{5,6},{6,7},{7,4},{8,9},{9,10},{10,1... | collective-permute-start | bytes 196616 | tf_op jit(solution)/shard_map/ppermute | solution.py:82
  173.5 1.2 collective-permute-start.37
  174.7 1.2 collective-permute-start.38
  176.4 3.2 %collective-permute-done.37.refs_2_ = bf16[32,1024]{1,0:T(8,128)(2,1)S(1)} collective-permute-done((bf16[32,1024]{1,0:T(8,128)(2,1)S(1)}, bf16[32,1024]{1,0:T(8,128)(2,1)S(1)}, u32[]{:S(2)}, u32[]{:S(2)}) %collective-permute-start.37) | collective-permute-done | bytes 65568 | tf_op jit(solution)/shard_map/ppermute | solution.py:82
  179.9 1.3 place.1
  (85 shorter events, 11.6 us)
Async XLA Ops:
  2.3 29.2 %collective-permute-start.3 = (bf16[3,1024,1024]{2,1,0:T(8,128)(2,1)}, bf16[3,1024,1024]{2,1,0:T(8,128)(2,1)}, u32[]{:S(2)}, u32[]{:S(2)}) collective-permute-start(bf16[3,1024,1024]{2,1,0:T(8,128)(2,1)} %refs_10_.1), channel_id=1, source_target_pairs={{0,4},{4,0},{8,12},{12,8},{1,5},{5,1},{9,13},{13,9},{2,6},{6,2},{1... | collective-permute-start | bytes 18874376 | tf_op jit(solution)/shard_map/ppermute | solution.py:82
  2.7 28.7 %collective-permute-start = (bf16[2,256,1024]{2,1,0:T(8,128)(2,1)}, bf16[2,256,1024]{2,1,0:T(8,128)(2,1)}, u32[]{:S(2)}, u32[]{:S(2)}) collective-permute-start(bf16[2,256,1024]{2,1,0:T(8,128)(2,1)} %refs_0_), channel_id=1, source_target_pairs={{0,1},{1,2},{2,3},{3,0},{4,5},{5,6},{6,7},{7,4},{8,9},{9,10},{10,1... | collective-permute-start | bytes 3145736 | tf_op jit(solution)/shard_map/ppermute | solution.py:82
  5.3 26.2 %collective-permute-start.2 = (bf16[2,256,1024]{2,1,0:T(8,128)(2,1)}, bf16[2,256,1024]{2,1,0:T(8,128)(2,1)}, u32[]{:S(2)}, u32[]{:S(2)}) collective-permute-start(bf16[2,256,1024]{2,1,0:T(8,128)(2,1)} %refs_0_), channel_id=1, source_target_pairs={{0,4},{4,0},{8,12},{12,8},{1,5},{5,1},{9,13},{13,9},{2,6},{6,2},{1... | collective-permute-start | bytes 3145736 | tf_op jit(solution)/shard_map/ppermute | solution.py:82
  5.5 25.9 %collective-permute-start.1 = (bf16[1024,512]{1,0:T(8,128)(2,1)}, bf16[1024,512]{1,0:T(8,128)(2,1)S(1)}, u32[]{:S(2)}, u32[]{:S(2)}) collective-permute-start(bf16[1024,512]{1,0:T(8,128)(2,1)} %dynamic-slice_bitcast_fusion.2), channel_id=1, source_target_pairs={{0,8},{4,12},{8,0},{12,4},{16,28},{20,24},{24,20},{28,16},{1,9},{5... | collective-permute-start | bytes 3145736 | tf_op jit(solution)/shard_map/ppermute | solution.py:82
  10.9 14.8 %copy-start.10 = (s32[128]{0:T(128)S(1)}, s32[128]{0:T(128)}, u32[]{:S(2)}) copy-start(s32[128]{0:T(128)} %param.11) | copy-start | bytes 1540
  22.3 46.3 %copy-start = (bf16[1024,1024]{1,0:T(8,128)(2,1)S(1)}, bf16[1024,1024]{1,0:T(8,128)(2,1)}, u32[]{:S(2)}) copy-start(bf16[1024,1024]{1,0:T(8,128)(2,1)} %own.1) | copy-start | bytes 6291460
  31.5 60.9 %copy-start.5 = (bf16[1024,512]{1,0:T(8,128)(2,1)}, bf16[1024,512]{1,0:T(8,128)(2,1)S(1)}, u32[]{:S(2)}) copy-start(bf16[1024,512]{1,0:T(8,128)(2,1)S(1)} %collective-permute-done.1.refs_12_.refs_16_) | copy-start | bytes 3145732
  31.5 4.0 %collective-permute-start.8 = (bf16[4,2,32,1024]{3,2,0,1:T(8,128)(2,1)}, bf16[4,2,32,1024]{3,2,0,1:T(8,128)(2,1)}, u32[]{:S(2)}, u32[]{:S(2)}) collective-permute-start(bf16[4,2,32,1024]{3,2,0,1:T(8,128)(2,1)} %bitcast.37), channel_id=1, source_target_pairs={{0,4},{4,0},{8,12},{12,8},{1,5},{5,1},{9,13},{13,9},{2,6},{6,2},{1... | collective-permute-start | bytes 1572872 | tf_op jit(solution)/shard_map/ppermute | solution.py:82
  31.6 32.3 %collective-permute-start.4 = (bf16[2,256,1024]{2,1,0:T(8,128)(2,1)}, bf16[2,256,1024]{2,1,0:T(8,128)(2,1)}, u32[]{:S(2)}, u32[]{:S(2)}) collective-permute-start(bf16[2,256,1024]{2,1,0:T(8,128)(2,1)} %collective-permute-done.refs_1_), channel_id=1, source_target_pairs={{0,1},{1,2},{2,3},{3,0},{4,5},{5,6},{6,7},{7,4},{8,9},{9,10},{10,1... | collective-permute-start | bytes 3145736 | tf_op jit(solution)/shard_map/ppermute | solution.py:82
  32.8 31.1 %collective-permute-start.5 = (bf16[1024,512]{1,0:T(8,128)(2,1)}, bf16[1024,512]{1,0:T(8,128)(2,1)}, u32[]{:S(2)}, u32[]{:S(2)}) collective-permute-start(bf16[1024,512]{1,0:T(8,128)(2,1)} %dynamic-slice_bitcast_fusion.1), channel_id=1, source_target_pairs={{0,8},{4,12},{8,0},{12,4},{16,28},{20,24},{24,20},{28,16},{1,9},{5... | collective-permute-start | bytes 3145736 | tf_op jit(solution)/shard_map/ppermute | solution.py:82
  34.3 29.6 %collective-permute-start.6 = (bf16[1024,512]{1,0:T(8,128)(2,1)S(1)}, bf16[1024,512]{1,0:T(8,128)(2,1)}, u32[]{:S(2)}, u32[]{:S(2)}) collective-permute-start(bf16[1024,512]{1,0:T(8,128)(2,1)S(1)} %collective-permute-done.1.refs_12_.refs_16_), channel_id=1, source_target_pairs={{0,16},{16,0},{1,17},{17,1},{2,18},{18,2},{3,19},{19,3},{4,20},{20... | collective-permute-start | bytes 3145736 | tf_op jit(solution)/shard_map/ppermute | solution.py:82
  35.3 28.6 %collective-permute-start.7 = (bf16[2,256,1024]{2,1,0:T(8,128)(2,1)}, bf16[2,256,1024]{2,1,0:T(8,128)(2,1)}, u32[]{:S(2)}, u32[]{:S(2)}) collective-permute-start(bf16[2,256,1024]{2,1,0:T(8,128)(2,1)} %collective-permute-done.refs_1_), channel_id=1, source_target_pairs={{0,4},{4,0},{8,12},{12,8},{1,5},{5,1},{9,13},{13,9},{2,6},{6,2},{1... | collective-permute-start | bytes 3145736 | tf_op jit(solution)/shard_map/ppermute | solution.py:82
  36.8 27.0 %collective-permute-start.9 = (bf16[128,1024]{1,0:T(8,128)(2,1)S(1)}, bf16[128,1024]{1,0:T(8,128)(2,1)S(1)}, u32[]{:S(2)}, u32[]{:S(2)}) collective-permute-start(bf16[128,1024]{1,0:T(8,128)(2,1)S(1)} %bitcast.38), channel_id=1, source_target_pairs={{0,8},{4,12},{8,0},{12,4},{1,9},{5,13},{9,1},{13,5},{2,10},{6,14},... | collective-permute-start | bytes 786440 | tf_op jit(solution)/shard_map/ppermute | solution.py:82
  63.9 26.6 %collective-permute-start.10 = (bf16[2,256,1024]{2,1,0:T(8,128)(2,1)}, bf16[2,256,1024]{2,1,0:T(8,128)(2,1)}, u32[]{:S(2)}, u32[]{:S(2)}) collective-permute-start(bf16[2,256,1024]{2,1,0:T(8,128)(2,1)} %collective-permute-done.4.refs_2_), channel_id=1, source_target_pairs={{0,1},{1,2},{2,3},{3,0},{4,5},{5,6},{6,7},{7,4},{8,9},{9,10},{10,1... | collective-permute-start | bytes 3145736 | tf_op jit(solution)/shard_map/ppermute | solution.py:82
  65.5 24.9 %collective-permute-start.11 = (bf16[1024,512]{1,0:T(8,128)(2,1)}, bf16[1024,512]{1,0:T(8,128)(2,1)}, u32[]{:S(2)}, u32[]{:S(2)}) collective-permute-start(bf16[1024,512]{1,0:T(8,128)(2,1)} %dynamic-slice_bitcast_fusion), channel_id=1, source_target_pairs={{0,8},{4,12},{8,0},{12,4},{16,28},{20,24},{24,20},{28,16},{1,9},{5... | collective-permute-start | bytes 3145736 | tf_op jit(solution)/shard_map/ppermute | solution.py:82
  67.0 25.4 %collective-permute-start.12 = (bf16[1024,512]{1,0:T(8,128)(2,1)}, bf16[1024,512]{1,0:T(8,128)(2,1)}, u32[]{:S(2)}, u32[]{:S(2)}) collective-permute-start(bf16[1024,512]{1,0:T(8,128)(2,1)} %collective-permute-done.5.refs_14_.refs_18_), channel_id=1, source_target_pairs={{0,16},{16,0},{1,17},{17,1},{2,18},{18,2},{3,19},{19,3},{4,20},{20... | collective-permute-start | bytes 3145736 | tf_op jit(solution)/shard_map/ppermute | solution.py:82
  67.8 24.5 %collective-permute-start.13 = (bf16[2,256,1024]{2,1,0:T(8,128)(2,1)}, bf16[2,256,1024]{2,1,0:T(8,128)(2,1)}, u32[]{:S(2)}, u32[]{:S(2)}) collective-permute-start(bf16[2,256,1024]{2,1,0:T(8,128)(2,1)} %collective-permute-done.4.refs_2_), channel_id=1, source_target_pairs={{0,4},{4,0},{8,12},{12,8},{1,5},{5,1},{9,13},{13,9},{2,6},{6,2},{1... | collective-permute-start | bytes 3145736 | tf_op jit(solution)/shard_map/ppermute | solution.py:82
  68.5 48.4 %copy-start.6 = (bf16[128,1024]{1,0:T(8,128)(2,1)}, bf16[128,1024]{1,0:T(8,128)(2,1)S(1)}, u32[]{:S(2)}) copy-start(bf16[128,1024]{1,0:T(8,128)(2,1)S(1)} %add.105.refs_0_) | copy-start | bytes 786436
  68.5 2.7 %collective-permute-start.14 = (bf16[128,1024]{1,0:T(8,128)(2,1)S(1)}, bf16[128,1024]{1,0:T(8,128)(2,1)}, u32[]{:S(2)}, u32[]{:S(2)}) collective-permute-start(bf16[128,1024]{1,0:T(8,128)(2,1)S(1)} %add.105.refs_0_), channel_id=1, source_target_pairs={{0,4},{4,0},{8,12},{12,8},{1,5},{5,1},{9,13},{13,9},{2,6},{6,2},{1... | collective-permute-start | bytes 786440 | tf_op jit(solution)/shard_map/ppermute | solution.py:82
  92.4 5.2 %collective-permute-start.15 = (bf16[2,256,1024]{2,1,0:T(8,128)(2,1)}, bf16[2,256,1024]{2,1,0:T(8,128)(2,1)S(1)}, u32[]{:S(2)}, u32[]{:S(2)}) collective-permute-start(bf16[2,256,1024]{2,1,0:T(8,128)(2,1)} %collective-permute-done.10.refs_3_), channel_id=1, source_target_pairs={{0,4},{4,0},{8,12},{12,8},{1,5},{5,1},{9,13},{13,9},{2,6},{6,2},{1... | collective-permute-start | bytes 3145736 | tf_op jit(solution)/shard_map/ppermute | solution.py:82
  92.4 25.6 %collective-permute-start.16 = (bf16[512,1024]{1,0:T(8,128)(2,1)S(1)}, bf16[512,1024]{1,0:T(8,128)(2,1)S(1)}, u32[]{:S(2)}, u32[]{:S(2)}) collective-permute-start(bf16[512,1024]{1,0:T(8,128)(2,1)S(1)} %constant_dynamic-slice_fusion), channel_id=1, source_target_pairs={{0,8},{4,12},{8,0},{12,4},{1,9},{5,13},{9,1},{13,5},{2,10},{6,14},... | collective-permute-start | bytes 3145736 | tf_op jit(solution)/shard_map/ppermute | solution.py:82
  93.0 25.4 %collective-permute-start.17 = (bf16[1024,512]{1,0:T(8,128)(2,1)}, bf16[1024,512]{1,0:T(8,128)(2,1)S(1)}, u32[]{:S(2)}, u32[]{:S(2)}) collective-permute-start(bf16[1024,512]{1,0:T(8,128)(2,1)} %collective-permute-done.11.refs_14_), channel_id=1, source_target_pairs={{0,16},{16,0},{1,17},{17,1},{2,18},{18,2},{3,19},{19,3},{4,20},{20... | collective-permute-start | bytes 3145736 | tf_op jit(solution)/shard_map/ppermute | solution.py:82
  94.7 22.2 %collective-permute-start.18 = (bf16[128,1024]{1,0:T(8,128)(2,1)S(1)}, bf16[128,1024]{1,0:T(8,128)(2,1)}, u32[]{:S(2)}, u32[]{:S(2)}) collective-permute-start(bf16[128,1024]{1,0:T(8,128)(2,1)S(1)} %add.105.refs_0_), channel_id=1, source_target_pairs={{0,1},{1,2},{2,3},{3,0},{4,5},{5,6},{6,7},{7,4},{8,9},{9,10},{10,1... | collective-permute-start | bytes 786440 | tf_op jit(solution)/shard_map/ppermute | solution.py:82
  95.0 21.9 %collective-permute-start.19 = (bf16[128,1024]{1,0:T(8,128)(2,1)S(1)}, bf16[128,1024]{1,0:T(8,128)(2,1)}, u32[]{:S(2)}, u32[]{:S(2)}) collective-permute-start(bf16[128,1024]{1,0:T(8,128)(2,1)S(1)} %add.105.refs_0_), channel_id=1, source_target_pairs={{0,2},{1,3},{2,0},{3,1},{4,6},{5,7},{6,4},{7,5},{8,10},{9,11},{10,... | collective-permute-start | bytes 786440 | tf_op jit(solution)/shard_map/ppermute | solution.py:82
  97.5 1.9 %copy-start.8 = (bf16[2,256,1024]{2,1,0:T(8,128)(2,1)}, bf16[2,256,1024]{2,1,0:T(8,128)(2,1)S(1)}, u32[]{:S(2)}) copy-start(bf16[2,256,1024]{2,1,0:T(8,128)(2,1)S(1)} %collective-permute-done.15.refs_7_) | copy-start | bytes 3145732
  97.5 19.4 %collective-permute-start.20 = (bf16[128,1024]{1,0:T(8,128)(2,1)S(1)}, bf16[128,1024]{1,0:T(8,128)(2,1)}, u32[]{:S(2)}, u32[]{:S(2)}) collective-permute-start(bf16[128,1024]{1,0:T(8,128)(2,1)S(1)} %add.105.refs_0_), channel_id=1, source_target_pairs={{0,3},{1,0},{2,1},{3,2},{4,7},{5,4},{6,5},{7,6},{8,11},{9,8},{10,9... | collective-permute-start | bytes 786440 | tf_op jit(solution)/shard_map/ppermute | solution.py:82
  118.4 2.3 %copy-start.7 = (bf16[1024,512]{1,0:T(8,128)(2,1)}, bf16[1024,512]{1,0:T(8,128)(2,1)S(1)}, u32[]{:S(2)}) copy-start(bf16[1024,512]{1,0:T(8,128)(2,1)S(1)} %collective-permute-done.17.refs_15_) | copy-start | bytes 3145732
  118.4 20.0 %collective-permute-start.26 = (bf16[1024,1024]{1,0:T(8,128)(2,1)S(1)}, bf16[1024,1024]{1,0:T(8,128)(2,1)}, u32[]{:S(2)}, u32[]{:S(2)}) collective-permute-start(bf16[1024,1024]{1,0:T(8,128)(2,1)S(1)} %copy-done), channel_id=1, source_target_pairs={{0,4},{4,0},{8,12},{12,8},{1,5},{5,1},{9,13},{13,9},{2,6},{6,2},{1... | collective-permute-start | bytes 6291464 | tf_op jit(solution)/shard_map/ppermute | solution.py:82
  118.4 25.7 %collective-permute-start.30 = (bf16[512,1024]{1,0:T(8,128)(2,1)S(1)}, bf16[512,1024]{1,0:T(8,128)(2,1)}, u32[]{:S(2)}, u32[]{:S(2)}) collective-permute-start(bf16[512,1024]{1,0:T(8,128)(2,1)S(1)} %collective-permute-done.16.far_x), channel_id=1, source_target_pairs={{0,16},{16,0},{1,17},{17,1},{2,18},{18,2},{3,19},{19,3},{4,20},{20... | collective-permute-start | bytes 3145736 | tf_op jit(solution)/shard_map/ppermute | solution.py:82
  120.2 3.4 %collective-permute-start.21 = (bf16[128,1024]{1,0:T(8,128)(2,1)}, bf16[128,1024]{1,0:T(8,128)(2,1)S(1)}, u32[]{:S(2)}, u32[]{:S(2)}) collective-permute-start(bf16[128,1024]{1,0:T(8,128)(2,1)} %collective-permute-done.18.refs_1_), channel_id=1, source_target_pairs={{0,4},{4,0},{8,12},{12,8},{1,5},{5,1},{9,13},{13,9},{2,6},{6,2},{1... | collective-permute-start | bytes 786440 | tf_op jit(solution)/shard_map/ppermute | solution.py:82
  120.4 4.6 %collective-permute-start.22 = (bf16[128,1024]{1,0:T(8,128)(2,1)}, bf16[128,1024]{1,0:T(8,128)(2,1)}, u32[]{:S(2)}, u32[]{:S(2)}) collective-permute-start(bf16[128,1024]{1,0:T(8,128)(2,1)} %collective-permute-done.19.refs_2_), channel_id=1, source_target_pairs={{0,4},{4,0},{8,12},{12,8},{1,5},{5,1},{9,13},{13,9},{2,6},{6,2},{1... | collective-permute-start | bytes 786440 | tf_op jit(solution)/shard_map/ppermute | solution.py:82
  120.7 4.4 %collective-permute-start.23 = (bf16[128,1024]{1,0:T(8,128)(2,1)}, bf16[128,1024]{1,0:T(8,128)(2,1)}, u32[]{:S(2)}, u32[]{:S(2)}) collective-permute-start(bf16[128,1024]{1,0:T(8,128)(2,1)} %collective-permute-done.20.refs_3_), channel_id=1, source_target_pairs={{0,4},{4,0},{8,12},{12,8},{1,5},{5,1},{9,13},{13,9},{2,6},{6,2},{1... | collective-permute-start | bytes 786440 | tf_op jit(solution)/shard_map/ppermute | solution.py:82
  121.0 13.4 %copy-start.1 = (f32[2,4,128,128]{3,2,1,0:T(8,128)S(1)}, f32[2,4,128,128]{3,2,1,0:T(8,128)}, u32[]{:S(2)}) copy-start(f32[2,4,128,128]{3,2,1,0:T(8,128)} %get-tuple-element.128.states) | copy-start | bytes 1572868
  123.5 1.5 copy-start.9
  123.5 10.9 %collective-permute-start.24 = (bf16[2,4,128,128]{3,2,1,0:T(8,128)(2,1)}, bf16[2,4,128,128]{3,2,1,0:T(8,128)(2,1)S(1)}, u32[]{:S(2)}, u32[]{:S(2)}) collective-permute-start(bf16[2,4,128,128]{3,2,1,0:T(8,128)(2,1)} %get-tuple-element.129), channel_id=1, source_target_pairs={{0,8},{4,12},{8,0},{12,4},{1,9},{5,13},{9,1},{13,5},{2,10},{6,14},... | collective-permute-start | bytes 786440 | tf_op jit(solution)/shard_map/ppermute | solution.py:82
  136.5 32.8 %copy-start.3 = (bf16[32,4096]{1,0:T(8,128)(2,1)S(1)}, bf16[32,4096]{1,0:T(8,128)(2,1)}, u32[]{:S(2)}) copy-start(bf16[32,4096]{1,0:T(8,128)(2,1)} %get-tuple-element.123.residual) | copy-start | bytes 786436
  137.0 1.4 collective-permute-start.25
  137.1 12.3 %collective-permute-start.31 = (bf16[512,1024]{1,0:T(8,128)(2,1)S(1)}, bf16[512,1024]{1,0:T(8,128)(2,1)S(1)}, u32[]{:S(2)}, u32[]{:S(2)}) collective-permute-start(bf16[512,1024]{1,0:T(8,128)(2,1)S(1)} %collective-permute-done.16.far_x), channel_id=1, source_target_pairs={{0,4},{4,0},{8,12},{12,8},{1,5},{5,1},{9,13},{13,9},{2,6},{6,2},{1... | collective-permute-start | bytes 3145736 | tf_op jit(solution)/shard_map/ppermute | solution.py:82
  144.1 5.3 %collective-permute-start.32 = (bf16[512,1024]{1,0:T(8,128)(2,1)}, bf16[512,1024]{1,0:T(8,128)(2,1)S(1)}, u32[]{:S(2)}, u32[]{:S(2)}) collective-permute-start(bf16[512,1024]{1,0:T(8,128)(2,1)} %collective-permute-done.30.far_y), channel_id=1, source_target_pairs={{0,4},{4,0},{8,12},{12,8},{1,5},{5,1},{9,13},{13,9},{2,6},{6,2},{1... | collective-permute-start | bytes 3145736 | tf_op jit(solution)/shard_map/ppermute | solution.py:82
  144.1 10.5 %collective-permute-start.27 = (bf16[32,2048]{1,0:T(8,128)(2,1)S(1)}, bf16[32,2048]{1,0:T(8,128)(2,1)S(1)}, u32[]{:S(2)}, u32[]{:S(2)}) collective-permute-start(bf16[32,2048]{1,0:T(8,128)(2,1)S(1)} %get-tuple-element.134), channel_id=1, source_target_pairs={{0,1},{1,2},{2,3},{3,0},{4,5},{5,6},{6,7},{7,4},{8,9},{9,10},{10,1... | collective-permute-start | bytes 393224 | tf_op jit(solution)/shard_map/ppermute | solution.py:82
  147.1 11.2 %collective-permute-start.28 = (bf16[32,2048]{1,0:T(8,128)(2,1)S(1)}, bf16[32,2048]{1,0:T(8,128)(2,1)S(1)}, u32[]{:S(2)}, u32[]{:S(2)}) collective-permute-start(bf16[32,2048]{1,0:T(8,128)(2,1)S(1)} %get-tuple-element.135), channel_id=1, source_target_pairs={{0,2},{1,3},{2,0},{3,1},{4,6},{5,7},{6,4},{7,5},{8,10},{9,11},{10,... | collective-permute-start | bytes 393224 | tf_op jit(solution)/shard_map/ppermute | solution.py:82
  148.8 9.5 %collective-permute-start.29 = (bf16[32,2048]{1,0:T(8,128)(2,1)S(1)}, bf16[32,2048]{1,0:T(8,128)(2,1)S(1)}, u32[]{:S(2)}, u32[]{:S(2)}) collective-permute-start(bf16[32,2048]{1,0:T(8,128)(2,1)S(1)} %get-tuple-element.136), channel_id=1, source_target_pairs={{0,3},{1,0},{2,1},{3,2},{4,7},{5,4},{6,5},{7,6},{8,11},{9,8},{10,9... | collective-permute-start | bytes 393224 | tf_op jit(solution)/shard_map/ppermute | solution.py:82
  152.0 9.2 %collective-permute-start.33 = (bf16[32,2048]{1,0:T(8,128)(2,1)S(1)}, bf16[32,2048]{1,0:T(8,128)(2,1)S(1)}, u32[]{:S(2)}, u32[]{:S(2)}) collective-permute-start(bf16[32,2048]{1,0:T(8,128)(2,1)S(1)} %get-tuple-element.142), channel_id=1, source_target_pairs={{0,1},{1,2},{2,3},{3,0},{4,5},{5,6},{6,7},{7,4},{8,9},{9,10},{10,1... | collective-permute-start | bytes 393224 | tf_op jit(solution)/shard_map/ppermute | solution.py:82
  153.4 15.9 %collective-permute-start.34 = (bf16[32,2048]{1,0:T(8,128)(2,1)S(1)}, bf16[32,2048]{1,0:T(8,128)(2,1)S(1)}, u32[]{:S(2)}, u32[]{:S(2)}) collective-permute-start(bf16[32,2048]{1,0:T(8,128)(2,1)S(1)} %get-tuple-element.143), channel_id=1, source_target_pairs={{0,2},{1,3},{2,0},{3,1},{4,6},{5,7},{6,4},{7,5},{8,10},{9,11},{10,... | collective-permute-start | bytes 393224 | tf_op jit(solution)/shard_map/ppermute | solution.py:82
  154.6 14.7 %collective-permute-start.35 = (bf16[32,2048]{1,0:T(8,128)(2,1)S(1)}, bf16[32,2048]{1,0:T(8,128)(2,1)S(1)}, u32[]{:S(2)}, u32[]{:S(2)}) collective-permute-start(bf16[32,2048]{1,0:T(8,128)(2,1)S(1)} %get-tuple-element.144), channel_id=1, source_target_pairs={{0,3},{1,0},{2,1},{3,2},{4,7},{5,4},{6,5},{7,6},{8,11},{9,8},{10,9... | collective-permute-start | bytes 393224 | tf_op jit(solution)/shard_map/ppermute | solution.py:82
  170.1 6.3 %collective-permute-start.36 = (bf16[32,1024]{1,0:T(8,128)(2,1)S(1)}, bf16[32,1024]{1,0:T(8,128)(2,1)S(1)}, u32[]{:S(2)}, u32[]{:S(2)}) collective-permute-start(bf16[32,1024]{1,0:T(8,128)(2,1)S(1)} %get-tuple-element.146), channel_id=1, source_target_pairs={{0,1},{1,2},{2,3},{3,0},{4,5},{5,6},{6,7},{7,4},{8,9},{9,10},{10,1... | collective-permute-start | bytes 196616 | tf_op jit(solution)/shard_map/ppermute | solution.py:82
  173.5 6.1 %collective-permute-start.37 = (bf16[32,1024]{1,0:T(8,128)(2,1)S(1)}, bf16[32,1024]{1,0:T(8,128)(2,1)S(1)}, u32[]{:S(2)}, u32[]{:S(2)}) collective-permute-start(bf16[32,1024]{1,0:T(8,128)(2,1)S(1)} %get-tuple-element.147), channel_id=1, source_target_pairs={{0,2},{1,3},{2,0},{3,1},{4,6},{5,7},{6,4},{7,5},{8,10},{9,11},{10,... | collective-permute-start | bytes 196616 | tf_op jit(solution)/shard_map/ppermute | solution.py:82
  174.7 5.2 %collective-permute-start.38 = (bf16[32,1024]{1,0:T(8,128)(2,1)S(1)}, bf16[32,1024]{1,0:T(8,128)(2,1)S(1)}, u32[]{:S(2)}, u32[]{:S(2)}) collective-permute-start(bf16[32,1024]{1,0:T(8,128)(2,1)S(1)} %get-tuple-element.148), channel_id=1, source_target_pairs={{0,3},{1,0},{2,1},{3,2},{4,7},{5,4},{6,5},{7,6},{8,11},{9,8},{10,9... | collective-permute-start | bytes 196616 | tf_op jit(solution)/shard_map/ppermute | solution.py:82
  (2 other events, 2.0 us)

commit v4 on v3

--- a/solution.py
+++ b/solution.py
@@ -151,7 +151,7 @@
     mine, other, refs = refs[:nhead], refs[nhead : 2 * nhead], refs[2 * nhead :]
     own, sib = refs[:3], refs[3:6]
     far = refs[6:8], refs[8:10], refs[10:12]
-    query_out, local_out, residual, held = refs[12:]
+    rows_out, residual, held = refs[12:]
     rows, block = held.shape[1:]
     features = nhead * block
 
@@ -173,15 +173,16 @@
         squares += jnp.sum(part * part, axis=-1, keepdims=True)
     scale = lax.rsqrt(squares / features + 1e-06)
 
-    def projected(i):
-        total = None
-        for part, weight in zip(blocks, (own[i][0], sib[i][0], far[i][0][...], far[i][1][...])):
-            term = jnp.dot(part, weight, preferred_element_type=F32)
-            total = term if total is None else total + term
-        return (total * scale).astype(BF16)
-
-    query, key, value = (projected(i) for i in range(3))
-    query_out[...] = query
+    total = None
+    for j, part in enumerate(blocks):
+        each = [(own[i][0], sib[i][0], far[i][0][...], far[i][1][...])[j] for i in range(3)]
+        term = jnp.dot(part, jnp.concatenate(each, axis=1), preferred_element_type=F32)
+        total = term if total is None else total + term
+    total = (total * scale).astype(BF16)
+    wide = total.shape[1] // 3
+    query, key, value = (total[:, i * wide : (i + 1) * wide] for i in range(3))
+    width = query.shape[1]
+    rows_out[:, :width] = query.astype(F32)
     query, key, value = query.astype(F32), key.astype(F32), value.astype(F32)
     each = rows // 2 // steps
     for part in range(2):
@@ -195,15 +196,16 @@
                     score = jnp.sum(query[at_s, cols] * key[at_u, cols], axis=-1, keepdims=True)
                     term = score.astype(BF16).astype(F32) * value[at_u, cols]
                     total = term if total is None else total + term
-                local_out[at_s, cols] = total
-
-
-def attend_kernel(query, local, chosen, states, others, out, given):
+                rows_out[at_s, width + head * DH : width + (head + 1) * DH] = total
+
+
+def attend_kernel(wide, arrived, chosen, states, others, out, given):
     second = chosen[...] != 0
     rows = out.shape[0]
     for head in range(states.shape[1]):
         cols = slice(head * DH, (head + 1) * DH)
-        q = query[:, cols]
+        at = 2 * wide * (head * DH // wide) + head * DH % wide
+        q = arrived[:, at : at + DH].astype(BF16)
         both = []
         for p in range(2):
             state = states[p, head] + others[p, head].astype(F32)
@@ -212,7 +214,7 @@
             both.append(
                 jnp.dot(q, high, preferred_element_type=F32) + jnp.dot(q, low, preferred_element_type=F32)
             )
-        attended = jnp.where(second, both[1], both[0]) + local[:, cols]
+        attended = jnp.where(second, both[1], both[0]) + arrived[:, at + wide : at + wide + DH]
         normed = rms_rows(attended).astype(BF16)
         out[:, cols] = normed[:rows]
         given[:, cols] = normed[rows:]
@@ -372,28 +374,30 @@
     keys_x = cross(first_half)
     sib_tokens = [sib(prompt_hidden)]
     sib_weight = sib(later_weight)
+    out_sib = sib(out_weight)
     next_half, ids, later_weight = tie((fetched(2, later_weight), response_ids, later_weight))
     given, halves_of = by_core(lookup(ids))
 
     metas = (meta, out_meta, norm_meta, behind, chosen)
-    tokens, keys_x, sib_tokens, sib_weight, given, next_half, later_weight, metas = tie(
-        (tokens, keys_x, sib_tokens, sib_weight, given, next_half, later_weight, metas)
+    next_half, tokens, keys_x, sib_tokens, sib_weight, given, later_weight, metas, out_sib = tie(
+        (next_half, tokens, keys_x, sib_tokens, sib_weight, given, later_weight, metas, out_sib)
     )
     meta, out_meta, norm_meta, behind, chosen = metas
+    values_x = cross(next_half)
     tokens.append(up(tokens[1]))
-    values_x = cross(next_half)
     keys_y = swap(keys_x)
     sib_tokens.append(sib(tokens[1]))
     mine, given = halves_of(sib(given))
     given = permute(given, "ctx", to_far)
 
-    tokens, values_x, keys_y, sib_tokens, mine, given, next_half = tie(
-        (tokens, values_x, keys_y, sib_tokens, mine, given, fetched(0, later_weight))
-    )
+    values_x, tokens, keys_y, sib_tokens, mine, next_half = tie(
+        (values_x, tokens, keys_y, sib_tokens, mine, fetched(0, later_weight))
+    )
+    passed_on, given = tie((tokens[2], given))
     tokens.append(up(tokens[2]))
     query_x = cross(next_half)
     values_y = swap(values_x)
-    sib_tokens.append(sib(tokens[2]))
+    sib_tokens.append(sib(passed_on))
     embedded = mine + given
     sib_e = [sib(embedded)]
     out_half = lax.dynamic_slice(out_weight, (grp * depth, 0), (depth, width))
@@ -456,8 +460,8 @@
         *far_of(2),
     )
 
-    states, rounded, out_x, query_y, query_x, e, sib_e, out_own = tie(
-        (states, rounded, out_x, query_y, query_x, e, sib_e, out_weight)
+    states, rounded, out_x, query_y, query_x, e, sib_e = tie(
+        (states, rounded, out_x, query_y, query_x, e, sib_e)
     )
     sib_e += [sib(array) for array in e[1:]]
     out_y = swap(out_x)
@@ -466,12 +470,11 @@
     chip_rows = 2 * rows_local
     share = rows_local // nhead
     wide = 2 * DH
-    row_spec = pl.BlockSpec((chip_rows, wide), lambda n, m: (0, n))
-    query, local, residual = pl.pallas_call(
+    row_spec = pl.BlockSpec((chip_rows, 2 * wide), lambda n, m: (0, n))
+    rows_out, residual = pl.pallas_call(
         functools.partial(project_kernel, nhead, steps),
         out_shape=(
-            jax.ShapeDtypeStruct((chip_rows, cols), BF16),
-            jax.ShapeDtypeStruct((chip_rows, cols), F32),
+            jax.ShapeDtypeStruct((chip_rows, 2 * cols), F32),
             jax.ShapeDtypeStruct((share, nhead * block), BF16),
         ),
         grid_spec=pltpu.PrefetchScalarGridSpec(
@@ -481,7 +484,7 @@
             + [own_spec(k, wide) for k in range(3)]
             + [sib_spec(k, wide) for k in range(3)]
             + [far_spec(wide)] * 6,
-            out_specs=(row_spec, row_spec, pl.BlockSpec((share, nhead * block), lambda n, m: (0, 0))),
+            out_specs=(row_spec, pl.BlockSpec((share, nhead * block), lambda n, m: (0, 0))),
             scratch_shapes=[pltpu.VMEM((nhead, chip_rows, block), BF16)],
         ),
         compiler_params=pltpu.CompilerParams(vmem_limit_bytes=VMEM_LIMIT),
@@ -501,13 +504,12 @@
     )
 
     heads_own, heads_sib = pl.pallas_call(
-        attend_kernel,
+        functools.partial(attend_kernel, wide),
         out_shape=(jax.ShapeDtypeStruct((rows_local, cols), BF16),) * 2,
         compiler_params=pltpu.CompilerParams(vmem_limit_bytes=VMEM_SMALL),
         name="attend",
-    )(query, local, chosen, states, others)
+    )(rows_out, chosen, states, others)
     heads_sib = sib(heads_sib)
-    out_sib = sib(out_own)
 
     def spread(kernel, name, heads, operands, scratch):
         outs = (jax.ShapeDtypeStruct((share, 2 * width), F32),)
@@ -519,7 +521,7 @@
         return [terms[0]] + [moved[k] for k in range(1, nhead)]
 
     near = spread(near_kernel, "near_terms", (heads_own, heads_sib), (out_weight, out_sib), [])
-    heads_own, heads_sib, out_y = tie((heads_own, heads_sib, out_y, near[0]))[:3]
+    heads_own, heads_sib, out_y = tie((heads_own, heads_sib, out_y, near[1]))[:3]
     diag_x = sib(out_x)
     far = spread(
         far_kernel,

time: 182 us -> 177 us (0.973)
  waiting for transfers between devices: 77.6 us -> 74.3 us
    ppermute x39, waiting for transfers between devices: 77.6 us -> 74.3 us  [permute(): return lax.ppermute(array, axis, pairs)]
  transfers between devices with their start and end apart: 39 -> 39, of which waited for: 16 -> 20; matrix products, arithmetic and copies ran while one was open for 13% -> 13% of each run, Pallas kernels for 18% -> 19%
where the time goes in v4:
time: 177 us
  waiting for transfers between devices  74.3 us (42%)
  starting transfers between devices  39.9 us (23%)
  Pallas kernels  34.8 us (20%)
  local copies, waits for them, and re-layouts  23 us (13%)
  other arithmetic  4.38 us (2%)
    ppermute x39, waiting for transfers between devices, permute(): return lax.ppermute(array, axis, pairs)  74.3 us
    ppermute x39, starting transfers between devices, permute(): return lax.ppermute(array, axis, pairs)  39.9 us
    pallas_call x1, Pallas kernels, permuted_plan(): pl.pallas_call(functools.partial(state_kernel, nblocks), out_shape=(jax.S...  17.4 us
    gather x1, local copies, waits for them, and re-layouts, lookup(): jnp.take(embed_table, jnp.clip(offset_ids, 0, embed_table.shape[0] - 1),...  11.4 us
    pallas_call x1, Pallas kernels, permuted_plan(): pl.pallas_call(functools.partial(project_kernel, nhead, steps), out_shape...  9.35 us
    pallas_call x4, Pallas kernels, small_call(): pl.pallas_call(kernel, out_shape=outs, grid_spec=pltpu.PrefetchScalarGrid...  7.51 us
    squeeze x3, local copies, waits for them, and re-layouts, fetched(): lax.dynamic_slice(weight, (k, 0, (core ^ grp) * cols), (1, block, cols))[0]  6.84 us
  transfers between devices with their start and end apart: 39, of which 20 were waited for; matrix products, arithmetic and copies ran while one was open for 13% of the time, Pallas kernels for 19%

profile of v4, /device:TPU:0, one launch (start us, length us, event | category | flops | bytes accessed | tf_op | source)
XLA Modules:
  0.0 176.6 jit_solution(13628805092291892132)
XLA Ops:
  0.0 2.3 %dynamic-slice_bitcast_fusion.2 = bf16[1024,512]{1,0:T(8,128)(2,1)} fusion(bf16[3,1024,1024]{2,1,0:T(8,128)(2,1)} %refs_10_.1, s32[]{:T(128)S(6)} %select_n.115), kind=kLoop, calls=%fused_computation.4 | loop fusion | bytes 2097156 | tf_op jit(solution)/shard_map/squeeze | solution.py:349
  2.8 3.0 %collective-permute-start = (bf16[2,256,1024]{2,1,0:T(8,128)(2,1)}, bf16[2,256,1024]{2,1,0:T(8,128)(2,1)}, u32[]{:S(2)}, u32[]{:S(2)}) collective-permute-start(bf16[2,256,1024]{2,1,0:T(8,128)(2,1)} %refs_0_), channel_id=1, source_target_pairs={{0,1},{1,2},{2,3},{3,0},{4,5},{5,6},{6,7},{7,4},{8,9},{9,10},{10,1... | collective-permute-start | bytes 3145736 | tf_op jit(solution)/shard_map/ppermute | solution.py:82
  5.8 1.5 collective-permute-start.1
  7.3 2.3 %dynamic-slice_bitcast_fusion.1 = bf16[1024,512]{1,0:T(8,128)(2,1)} fusion(bf16[3,1024,1024]{2,1,0:T(8,128)(2,1)} %refs_10_.1, s32[]{:T(128)S(6)} %select_n.115), kind=kLoop, calls=%fused_computation.3 | loop fusion | bytes 2097156 | tf_op jit(solution)/shard_map/squeeze | solution.py:349
  11.2 11.4 %gather_fusion = bf16[512,1024]{1,0:T(8,128)(2,1)} fusion(bf16[8192,1024]{1,0:T(8,128)(2,1)} %param.9, s32[1024]{0:T(1024)S(1)} %pad_clamp_fusion), kind=kCustom, calls=%fused_computation | custom fusion | bytes 2099200 | tf_op jit(solution)/shard_map/jit(_take)/gather | solution.py:326
  22.6 1.6 select_select_fusion
  24.2 0.9 constant_dynamic-slice_fusion.3
  25.1 0.9 copy.14
  27.0 4.5 %collective-permute-done.refs_1_ = bf16[2,256,1024]{2,1,0:T(8,128)(2,1)} collective-permute-done((bf16[2,256,1024]{2,1,0:T(8,128)(2,1)}, bf16[2,256,1024]{2,1,0:T(8,128)(2,1)}, u32[]{:S(2)}, u32[]{:S(2)}) %collective-permute-start) | collective-permute-done | bytes 1048608 | tf_op jit(solution)/shard_map/ppermute | solution.py:82
  31.7 1.6 collective-permute-start.5
  33.2 1.6 collective-permute-start.6
  35.7 1.3 bitcast_add_fusion
  37.6 2.3 %dynamic-slice_bitcast_fusion = bf16[1024,512]{1,0:T(8,128)(2,1)} fusion(bf16[3,1024,1024]{2,1,0:T(8,128)(2,1)} %refs_10_.1, s32[]{:T(128)S(6)} %select_n.115), kind=kLoop, calls=%fused_computation.1 | loop fusion | bytes 2097156 | tf_op jit(solution)/shard_map/squeeze | solution.py:349
  39.8 18.2 %collective-permute-done.5.refs_14_.refs_18_ = bf16[1024,512]{1,0:T(8,128)(2,1)} collective-permute-done((bf16[1024,512]{1,0:T(8,128)(2,1)}, bf16[1024,512]{1,0:T(8,128)(2,1)}, u32[]{:S(2)}, u32[]{:S(2)}) %collective-permute-start.5) | collective-permute-done | bytes 1048608 | tf_op jit(solution)/shard_map/ppermute | solution.py:82
  58.0 2.6 %collective-permute-done.6.refs_2_ = bf16[2,256,1024]{2,1,0:T(8,128)(2,1)} collective-permute-done((bf16[2,256,1024]{2,1,0:T(8,128)(2,1)}, bf16[2,256,1024]{2,1,0:T(8,128)(2,1)}, u32[]{:S(2)}, u32[]{:S(2)}) %collective-permute-start.6) | collective-permute-done | bytes 1048608 | tf_op jit(solution)/shard_map/ppermute | solution.py:82
  61.5 1.6 collective-permute-done.13
  63.1 1.5 collective-permute-start.11
  64.6 1.5 collective-permute-start.12
  66.3 1.6 collective-permute-done.15.refs_4_
  67.9 19.2 %collective-permute-done.10.refs_3_ = bf16[2,256,1024]{2,1,0:T(8,128)(2,1)} collective-permute-done((bf16[2,256,1024]{2,1,0:T(8,128)(2,1)}, bf16[2,256,1024]{2,1,0:T(8,128)(2,1)}, u32[]{:S(2)}, u32[]{:S(2)}) %collective-permute-start.10) | collective-permute-done | bytes 1048608 | tf_op jit(solution)/shard_map/ppermute | solution.py:82
  87.1 1.9 %collective-permute-done.11.refs_14_ = bf16[1024,512]{1,0:T(8,128)(2,1)} collective-permute-done((bf16[1024,512]{1,0:T(8,128)(2,1)}, bf16[1024,512]{1,0:T(8,128)(2,1)}, u32[]{:S(2)}, u32[]{:S(2)}) %collective-permute-start.11) | collective-permute-done | bytes 1048608 | tf_op jit(solution)/shard_map/ppermute | solution.py:82
  89.0 1.2 collective-permute-done.12.refs_15_.refs_19_
  90.7 1.3 collective-permute-start.18
  92.0 1.3 collective-permute-start.19
  93.3 1.2 collective-permute-start.20
  94.5 2.7 %collective-permute-start.21 = (bf16[128,1024]{1,0:T(8,128)(2,1)S(1)}, bf16[128,1024]{1,0:T(8,128)(2,1)}, u32[]{:S(2)}, u32[]{:S(2)}) collective-permute-start(bf16[128,1024]{1,0:T(8,128)(2,1)S(1)} %add.105.refs_0_), channel_id=1, source_target_pairs={{0,3},{1,0},{2,1},{3,2},{4,7},{5,4},{6,5},{7,6},{8,11},{9,8},{10,9... | collective-permute-start | bytes 786440 | tf_op jit(solution)/shard_map/ppermute | solution.py:82
  97.2 17.4 %prompt_state.1 = (f32[2,4,128,128]{3,2,1,0:T(8,128)}, bf16[2,4,128,128]{3,2,1,0:T(8,128)(2,1)}) custom-call(s32[7]{0:T(128)} %stack.74.meta, bf16[2,256,1024]{2,1,0:T(8,128)(2,1)} %refs_0_, bf16[2,256,1024]{2,1,0:T(8,128)(2,1)} %collective-permute-done.refs_1_, bf16[2,256,1024]{2,1,0:T(8,128)(2,1)} %collective-permute-done.6.refs_2_, ...), custom_call_target="tpu_custom_call" | custom-call | flops 8589934592 | bytes 16777216 | tf_op jit(solution)/shard_map/prompt_state/pallas_call | solution.py:428
  114.7 1.1 collective-permute-done.17.far_x
  116.2 1.3 collective-permute-start.30
  118.2 1.6 collective-permute-start.25
  120.5 9.4 %response_rows.1 = (f32[256,1024]{1,0:T(8,128)}, bf16[32,4096]{1,0:T(8,128)(2,1)}) custom-call(s32[7]{0:T(128)} %stack.74.meta, bf16[128,1024]{1,0:T(8,128)(2,1)} %copy-done.5, bf16[128,1024]{1,0:T(8,128)(2,1)} %collective-permute-done.19.refs_1_, bf16[128,1024]{1,0:T(8,128)(2,1)} %collective-permute-done.20.refs_2_, ...), custom_call_target="tpu_custom_call" | custom-call | flops 3221225472 | bytes 14680064 | tf_op jit(solution)/shard_map/response_rows/pallas_call | solution.py:474
  129.8 1.2 copy-done.1
  131.9 1.1 collective-permute-done.26.heads_sib
  133.0 2.9 %near_terms.1 = (f32[32,2048]{1,0:T(8,128)S(1)}, bf16[32,2048]{1,0:T(8,128)(2,1)S(1)}, bf16[32,2048]{1,0:T(8,128)(2,1)S(1)}, bf16[32,2048]{1,0:T(8,128)(2,1)S(1)}) custom-call(s32[6]{0:T(128)S(1)} %stack.79.meta, bf16[128,512]{1,0:T(8,128)(2,1)S(1)} %get-tuple-element.138.heads_own, bf16[128,512]{1,0:T(8,128)(2,1)S(1)} %collective-permute-done.26.heads_sib, ...), custom_call_target="tpu_custom_call" | custom-call | flops 536870912 | bytes 4194304 | tf_op jit(solution)/shard_map/near_terms/pallas_call | solution.py:290
  135.9 2.9 %collective-permute-start.27 = (bf16[32,2048]{1,0:T(8,128)(2,1)S(1)}, bf16[32,2048]{1,0:T(8,128)(2,1)S(1)}, u32[]{:S(2)}, u32[]{:S(2)}) collective-permute-start(bf16[32,2048]{1,0:T(8,128)(2,1)S(1)} %get-tuple-element.134), channel_id=1, source_target_pairs={{0,1},{1,2},{2,3},{3,0},{4,5},{5,6},{6,7},{7,4},{8,9},{9,10},{10,1... | collective-permute-start | bytes 393224 | tf_op jit(solution)/shard_map/ppermute | solution.py:82
  138.8 5.0 %collective-permute-done.27.refs_1_ = bf16[32,2048]{1,0:T(8,128)(2,1)S(1)} collective-permute-done((bf16[32,2048]{1,0:T(8,128)(2,1)S(1)}, bf16[32,2048]{1,0:T(8,128)(2,1)S(1)}, u32[]{:S(2)}, u32[]{:S(2)}) %collective-permute-start.27) | collective-permute-done | bytes 131104 | tf_op jit(solution)/shard_map/ppermute | solution.py:82
  144.2 3.0 %collective-permute-start.29 = (bf16[32,2048]{1,0:T(8,128)(2,1)S(1)}, bf16[32,2048]{1,0:T(8,128)(2,1)S(1)}, u32[]{:S(2)}, u32[]{:S(2)}) collective-permute-start(bf16[32,2048]{1,0:T(8,128)(2,1)S(1)} %get-tuple-element.136), channel_id=1, source_target_pairs={{0,3},{1,0},{2,1},{3,2},{4,7},{5,4},{6,5},{7,6},{8,11},{9,8},{10,9... | collective-permute-start | bytes 393224 | tf_op jit(solution)/shard_map/ppermute | solution.py:82
  147.2 2.5 %far_terms.1 = (f32[32,2048]{1,0:T(8,128)S(1)}, bf16[32,2048]{1,0:T(8,128)(2,1)S(1)}, bf16[32,2048]{1,0:T(8,128)(2,1)S(1)}, bf16[32,2048]{1,0:T(8,128)(2,1)S(1)}) custom-call(s32[6]{0:T(128)S(1)} %stack.79.meta, bf16[128,512]{1,0:T(8,128)(2,1)S(1)} %get-tuple-element.138.heads_own, bf16[128,512]{1,0:T(8,128)(2,1)S(1)} %collective-permute-done.26.heads_sib, ...), custom_call_target="tpu_custom_call" | custom-call | flops 536870912 | bytes 4194304 | tf_op jit(solution)/shard_map/far_terms/pallas_call | solution.py:290
  150.3 1.3 collective-permute-start.34
  151.6 2.0 %collective-permute-start.35 = (bf16[32,2048]{1,0:T(8,128)(2,1)S(1)}, bf16[32,2048]{1,0:T(8,128)(2,1)S(1)}, u32[]{:S(2)}, u32[]{:S(2)}) collective-permute-start(bf16[32,2048]{1,0:T(8,128)(2,1)S(1)} %get-tuple-element.144), channel_id=1, source_target_pairs={{0,3},{1,0},{2,1},{3,2},{4,7},{5,4},{6,5},{7,6},{8,11},{9,8},{10,9... | collective-permute-start | bytes 393224 | tf_op jit(solution)/shard_map/ppermute | solution.py:82
  153.8 4.2 %collective-permute-done.33.refs_5_ = bf16[32,2048]{1,0:T(8,128)(2,1)S(1)} collective-permute-done((bf16[32,2048]{1,0:T(8,128)(2,1)S(1)}, bf16[32,2048]{1,0:T(8,128)(2,1)S(1)}, u32[]{:S(2)}, u32[]{:S(2)}) %collective-permute-start.33) | collective-permute-done | bytes 131104 | tf_op jit(solution)/shard_map/ppermute | solution.py:82
  158.0 7.0 %collective-permute-done.34.refs_6_ = bf16[32,2048]{1,0:T(8,128)(2,1)S(1)} collective-permute-done((bf16[32,2048]{1,0:T(8,128)(2,1)S(1)}, bf16[32,2048]{1,0:T(8,128)(2,1)S(1)}, u32[]{:S(2)}, u32[]{:S(2)}) %collective-permute-start.34) | collective-permute-done | bytes 131104 | tf_op jit(solution)/shard_map/ppermute | solution.py:82
  165.8 3.0 %collective-permute-start.36 = (bf16[32,1024]{1,0:T(8,128)(2,1)S(1)}, bf16[32,1024]{1,0:T(8,128)(2,1)S(1)}, u32[]{:S(2)}, u32[]{:S(2)}) collective-permute-start(bf16[32,1024]{1,0:T(8,128)(2,1)S(1)} %get-tuple-element.146), channel_id=1, source_target_pairs={{0,1},{1,2},{2,3},{3,0},{4,5},{5,6},{6,7},{7,4},{8,9},{9,10},{10,1... | collective-permute-start | bytes 196616 | tf_op jit(solution)/shard_map/ppermute | solution.py:82
  168.9 1.3 collective-permute-start.37
  170.2 1.1 collective-permute-start.38
  171.3 1.2 collective-permute-done.36.refs_1_
  172.5 2.7 %collective-permute-done.37.refs_2_ = bf16[32,1024]{1,0:T(8,128)(2,1)S(1)} collective-permute-done((bf16[32,1024]{1,0:T(8,128)(2,1)S(1)}, bf16[32,1024]{1,0:T(8,128)(2,1)S(1)}, u32[]{:S(2)}, u32[]{:S(2)}) %collective-permute-start.37) | collective-permute-done | bytes 65568 | tf_op jit(solution)/shard_map/ppermute | solution.py:82
  175.3 1.3 place.1
  (83 shorter events, 11.2 us)
Async XLA Ops:
  2.3 29.3 %collective-permute-start.3 = (bf16[3,1024,1024]{2,1,0:T(8,128)(2,1)}, bf16[3,1024,1024]{2,1,0:T(8,128)(2,1)}, u32[]{:S(2)}, u32[]{:S(2)}) collective-permute-start(bf16[3,1024,1024]{2,1,0:T(8,128)(2,1)} %refs_10_.1), channel_id=1, source_target_pairs={{0,4},{4,0},{8,12},{12,8},{1,5},{5,1},{9,13},{13,9},{2,6},{6,2},{1... | collective-permute-start | bytes 18874376 | tf_op jit(solution)/shard_map/ppermute | solution.py:82
  2.7 28.9 %collective-permute-start.4 = (bf16[1024,1024]{1,0:T(8,128)(2,1)}, bf16[1024,1024]{1,0:T(8,128)(2,1)}, u32[]{:S(2)}, u32[]{:S(2)}) collective-permute-start(bf16[1024,1024]{1,0:T(8,128)(2,1)} %own.1), channel_id=1, source_target_pairs={{0,4},{4,0},{8,12},{12,8},{1,5},{5,1},{9,13},{13,9},{2,6},{6,2},{1... | collective-permute-start | bytes 6291464 | tf_op jit(solution)/shard_map/ppermute | solution.py:82
  2.8 28.7 %collective-permute-start = (bf16[2,256,1024]{2,1,0:T(8,128)(2,1)}, bf16[2,256,1024]{2,1,0:T(8,128)(2,1)}, u32[]{:S(2)}, u32[]{:S(2)}) collective-permute-start(bf16[2,256,1024]{2,1,0:T(8,128)(2,1)} %refs_0_), channel_id=1, source_target_pairs={{0,1},{1,2},{2,3},{3,0},{4,5},{5,6},{6,7},{7,4},{8,9},{9,10},{10,1... | collective-permute-start | bytes 3145736 | tf_op jit(solution)/shard_map/ppermute | solution.py:82
  5.8 25.8 %collective-permute-start.2 = (bf16[2,256,1024]{2,1,0:T(8,128)(2,1)}, bf16[2,256,1024]{2,1,0:T(8,128)(2,1)}, u32[]{:S(2)}, u32[]{:S(2)}) collective-permute-start(bf16[2,256,1024]{2,1,0:T(8,128)(2,1)} %refs_0_), channel_id=1, source_target_pairs={{0,4},{4,0},{8,12},{12,8},{1,5},{5,1},{9,13},{13,9},{2,6},{6,2},{1... | collective-permute-start | bytes 3145736 | tf_op jit(solution)/shard_map/ppermute | solution.py:82
  5.8 25.8 %collective-permute-start.1 = (bf16[1024,512]{1,0:T(8,128)(2,1)}, bf16[1024,512]{1,0:T(8,128)(2,1)S(1)}, u32[]{:S(2)}, u32[]{:S(2)}) collective-permute-start(bf16[1024,512]{1,0:T(8,128)(2,1)} %dynamic-slice_bitcast_fusion.2), channel_id=1, source_target_pairs={{0,8},{4,12},{8,0},{12,4},{16,28},{20,24},{24,20},{28,16},{1,9},{5... | collective-permute-start | bytes 3145736 | tf_op jit(solution)/shard_map/ppermute | solution.py:82
  11.2 14.8 %copy-start.9 = (s32[128]{0:T(128)S(1)}, s32[128]{0:T(128)}, u32[]{:S(2)}) copy-start(s32[128]{0:T(128)} %param.11) | copy-start | bytes 1540
  22.6 43.6 %copy-start = (bf16[1024,1024]{1,0:T(8,128)(2,1)S(1)}, bf16[1024,1024]{1,0:T(8,128)(2,1)}, u32[]{:S(2)}) copy-start(bf16[1024,1024]{1,0:T(8,128)(2,1)} %own.1) | copy-start | bytes 6291460
  31.6 58.6 %copy-start.4 = (bf16[1024,512]{1,0:T(8,128)(2,1)}, bf16[1024,512]{1,0:T(8,128)(2,1)S(1)}, u32[]{:S(2)}) copy-start(bf16[1024,512]{1,0:T(8,128)(2,1)S(1)} %collective-permute-done.1.refs_12_.refs_16_) | copy-start | bytes 3145732
  31.6 4.1 %collective-permute-start.9 = (bf16[4,2,32,1024]{3,2,0,1:T(8,128)(2,1)}, bf16[4,2,32,1024]{3,2,0,1:T(8,128)(2,1)}, u32[]{:S(2)}, u32[]{:S(2)}) collective-permute-start(bf16[4,2,32,1024]{3,2,0,1:T(8,128)(2,1)} %bitcast.37), channel_id=1, source_target_pairs={{0,4},{4,0},{8,12},{12,8},{1,5},{5,1},{9,13},{13,9},{2,6},{6,2},{1... | collective-permute-start | bytes 1572872 | tf_op jit(solution)/shard_map/ppermute | solution.py:82
  31.7 26.3 %collective-permute-start.5 = (bf16[1024,512]{1,0:T(8,128)(2,1)}, bf16[1024,512]{1,0:T(8,128)(2,1)}, u32[]{:S(2)}, u32[]{:S(2)}) collective-permute-start(bf16[1024,512]{1,0:T(8,128)(2,1)} %dynamic-slice_bitcast_fusion.1), channel_id=1, source_target_pairs={{0,8},{4,12},{8,0},{12,4},{16,28},{20,24},{24,20},{28,16},{1,9},{5... | collective-permute-start | bytes 3145736 | tf_op jit(solution)/shard_map/ppermute | solution.py:82
  33.2 27.3 %collective-permute-start.6 = (bf16[2,256,1024]{2,1,0:T(8,128)(2,1)}, bf16[2,256,1024]{2,1,0:T(8,128)(2,1)}, u32[]{:S(2)}, u32[]{:S(2)}) collective-permute-start(bf16[2,256,1024]{2,1,0:T(8,128)(2,1)} %collective-permute-done.refs_1_), channel_id=1, source_target_pairs={{0,1},{1,2},{2,3},{3,0},{4,5},{5,6},{6,7},{7,4},{8,9},{9,10},{10,1... | collective-permute-start | bytes 3145736 | tf_op jit(solution)/shard_map/ppermute | solution.py:82
  34.8 25.8 %collective-permute-start.7 = (bf16[1024,512]{1,0:T(8,128)(2,1)S(1)}, bf16[1024,512]{1,0:T(8,128)(2,1)}, u32[]{:S(2)}, u32[]{:S(2)}) collective-permute-start(bf16[1024,512]{1,0:T(8,128)(2,1)S(1)} %collective-permute-done.1.refs_12_.refs_16_), channel_id=1, source_target_pairs={{0,16},{16,0},{1,17},{17,1},{2,18},{18,2},{3,19},{19,3},{4,20},{20... | collective-permute-start | bytes 3145736 | tf_op jit(solution)/shard_map/ppermute | solution.py:82
  35.7 24.9 %collective-permute-start.8 = (bf16[2,256,1024]{2,1,0:T(8,128)(2,1)}, bf16[2,256,1024]{2,1,0:T(8,128)(2,1)}, u32[]{:S(2)}, u32[]{:S(2)}) collective-permute-start(bf16[2,256,1024]{2,1,0:T(8,128)(2,1)} %collective-permute-done.refs_1_), channel_id=1, source_target_pairs={{0,4},{4,0},{8,12},{12,8},{1,5},{5,1},{9,13},{13,9},{2,6},{6,2},{1... | collective-permute-start | bytes 3145736 | tf_op jit(solution)/shard_map/ppermute | solution.py:82
  37.0 26.1 %collective-permute-start.13 = (bf16[128,1024]{1,0:T(8,128)(2,1)S(1)}, bf16[128,1024]{1,0:T(8,128)(2,1)S(1)}, u32[]{:S(2)}, u32[]{:S(2)}) collective-permute-start(bf16[128,1024]{1,0:T(8,128)(2,1)S(1)} %bitcast.38), channel_id=1, source_target_pairs={{0,8},{4,12},{8,0},{12,4},{1,9},{5,13},{9,1},{13,5},{2,10},{6,14},... | collective-permute-start | bytes 786440 | tf_op jit(solution)/shard_map/ppermute | solution.py:82
  60.6 26.5 %collective-permute-start.10 = (bf16[2,256,1024]{2,1,0:T(8,128)(2,1)}, bf16[2,256,1024]{2,1,0:T(8,128)(2,1)}, u32[]{:S(2)}, u32[]{:S(2)}) collective-permute-start(bf16[2,256,1024]{2,1,0:T(8,128)(2,1)} %collective-permute-done.6.refs_2_), channel_id=1, source_target_pairs={{0,1},{1,2},{2,3},{3,0},{4,5},{5,6},{6,7},{7,4},{8,9},{9,10},{10,1... | collective-permute-start | bytes 3145736 | tf_op jit(solution)/shard_map/ppermute | solution.py:82
  63.1 4.8 %collective-permute-start.14 = (bf16[2,256,1024]{2,1,0:T(8,128)(2,1)}, bf16[2,256,1024]{2,1,0:T(8,128)(2,1)}, u32[]{:S(2)}, u32[]{:S(2)}) collective-permute-start(bf16[2,256,1024]{2,1,0:T(8,128)(2,1)} %collective-permute-done.6.refs_2_), channel_id=1, source_target_pairs={{0,4},{4,0},{8,12},{12,8},{1,5},{5,1},{9,13},{13,9},{2,6},{6,2},{1... | collective-permute-start | bytes 3145736 | tf_op jit(solution)/shard_map/ppermute | solution.py:82
  63.1 25.9 %collective-permute-start.11 = (bf16[1024,512]{1,0:T(8,128)(2,1)}, bf16[1024,512]{1,0:T(8,128)(2,1)}, u32[]{:S(2)}, u32[]{:S(2)}) collective-permute-start(bf16[1024,512]{1,0:T(8,128)(2,1)} %dynamic-slice_bitcast_fusion), channel_id=1, source_target_pairs={{0,8},{4,12},{8,0},{12,4},{16,28},{20,24},{24,20},{28,16},{1,9},{5... | collective-permute-start | bytes 3145736 | tf_op jit(solution)/shard_map/ppermute | solution.py:82
  64.6 25.6 %collective-permute-start.12 = (bf16[1024,512]{1,0:T(8,128)(2,1)}, bf16[1024,512]{1,0:T(8,128)(2,1)}, u32[]{:S(2)}, u32[]{:S(2)}) collective-permute-start(bf16[1024,512]{1,0:T(8,128)(2,1)} %collective-permute-done.5.refs_14_.refs_18_), channel_id=1, source_target_pairs={{0,16},{16,0},{1,17},{17,1},{2,18},{18,2},{3,19},{19,3},{4,20},{20... | collective-permute-start | bytes 3145736 | tf_op jit(solution)/shard_map/ppermute | solution.py:82
  66.2 48.5 %copy-start.5 = (bf16[128,1024]{1,0:T(8,128)(2,1)}, bf16[128,1024]{1,0:T(8,128)(2,1)S(1)}, u32[]{:S(2)}) copy-start(bf16[128,1024]{1,0:T(8,128)(2,1)S(1)} %add.105.refs_0_) | copy-start | bytes 786436
  66.2 1.7 collective-permute-start.15
  90.2 4.3 %collective-permute-start.16 = (bf16[2,256,1024]{2,1,0:T(8,128)(2,1)}, bf16[2,256,1024]{2,1,0:T(8,128)(2,1)S(1)}, u32[]{:S(2)}, u32[]{:S(2)}) collective-permute-start(bf16[2,256,1024]{2,1,0:T(8,128)(2,1)} %collective-permute-done.10.refs_3_), channel_id=1, source_target_pairs={{0,4},{4,0},{8,12},{12,8},{1,5},{5,1},{9,13},{13,9},{2,6},{6,2},{1... | collective-permute-start | bytes 3145736 | tf_op jit(solution)/shard_map/ppermute | solution.py:82
  90.2 25.6 %collective-permute-start.17 = (bf16[512,1024]{1,0:T(8,128)(2,1)S(1)}, bf16[512,1024]{1,0:T(8,128)(2,1)S(1)}, u32[]{:S(2)}, u32[]{:S(2)}) collective-permute-start(bf16[512,1024]{1,0:T(8,128)(2,1)S(1)} %constant_dynamic-slice_fusion), channel_id=1, source_target_pairs={{0,8},{4,12},{8,0},{12,4},{1,9},{5,13},{9,1},{13,5},{2,10},{6,14},... | collective-permute-start | bytes 3145736 | tf_op jit(solution)/shard_map/ppermute | solution.py:82
  90.7 25.5 %collective-permute-start.18 = (bf16[1024,512]{1,0:T(8,128)(2,1)}, bf16[1024,512]{1,0:T(8,128)(2,1)S(1)}, u32[]{:S(2)}, u32[]{:S(2)}) collective-permute-start(bf16[1024,512]{1,0:T(8,128)(2,1)} %collective-permute-done.11.refs_14_), channel_id=1, source_target_pairs={{0,16},{16,0},{1,17},{17,1},{2,18},{18,2},{3,19},{19,3},{4,20},{20... | collective-permute-start | bytes 3145736 | tf_op jit(solution)/shard_map/ppermute | solution.py:82
  92.0 22.7 %collective-permute-start.19 = (bf16[128,1024]{1,0:T(8,128)(2,1)S(1)}, bf16[128,1024]{1,0:T(8,128)(2,1)}, u32[]{:S(2)}, u32[]{:S(2)}) collective-permute-start(bf16[128,1024]{1,0:T(8,128)(2,1)S(1)} %add.105.refs_0_), channel_id=1, source_target_pairs={{0,1},{1,2},{2,3},{3,0},{4,5},{5,6},{6,7},{7,4},{8,9},{9,10},{10,1... | collective-permute-start | bytes 786440 | tf_op jit(solution)/shard_map/ppermute | solution.py:82
  93.3 21.4 %collective-permute-start.20 = (bf16[128,1024]{1,0:T(8,128)(2,1)S(1)}, bf16[128,1024]{1,0:T(8,128)(2,1)}, u32[]{:S(2)}, u32[]{:S(2)}) collective-permute-start(bf16[128,1024]{1,0:T(8,128)(2,1)S(1)} %add.105.refs_0_), channel_id=1, source_target_pairs={{0,2},{1,3},{2,0},{3,1},{4,6},{5,7},{6,4},{7,5},{8,10},{9,11},{10,... | collective-permute-start | bytes 786440 | tf_op jit(solution)/shard_map/ppermute | solution.py:82
  94.5 2.7 %copy-start.7 = (bf16[2,256,1024]{2,1,0:T(8,128)(2,1)}, bf16[2,256,1024]{2,1,0:T(8,128)(2,1)S(1)}, u32[]{:S(2)}) copy-start(bf16[2,256,1024]{2,1,0:T(8,128)(2,1)S(1)} %collective-permute-done.16.refs_7_) | copy-start | bytes 3145732
  94.5 20.2 %collective-permute-start.21 = (bf16[128,1024]{1,0:T(8,128)(2,1)S(1)}, bf16[128,1024]{1,0:T(8,128)(2,1)}, u32[]{:S(2)}, u32[]{:S(2)}) collective-permute-start(bf16[128,1024]{1,0:T(8,128)(2,1)S(1)} %add.105.refs_0_), channel_id=1, source_target_pairs={{0,3},{1,0},{2,1},{3,2},{4,7},{5,4},{6,5},{7,6},{8,11},{9,8},{10,9... | collective-permute-start | bytes 786440 | tf_op jit(solution)/shard_map/ppermute | solution.py:82
  116.2 1.8 %copy-start.6 = (bf16[1024,512]{1,0:T(8,128)(2,1)}, bf16[1024,512]{1,0:T(8,128)(2,1)S(1)}, u32[]{:S(2)}) copy-start(bf16[1024,512]{1,0:T(8,128)(2,1)S(1)} %collective-permute-done.18.refs_15_) | copy-start | bytes 3145732
  116.2 27.6 %collective-permute-start.30 = (bf16[512,1024]{1,0:T(8,128)(2,1)S(1)}, bf16[512,1024]{1,0:T(8,128)(2,1)}, u32[]{:S(2)}, u32[]{:S(2)}) collective-permute-start(bf16[512,1024]{1,0:T(8,128)(2,1)S(1)} %collective-permute-done.17.far_x), channel_id=1, source_target_pairs={{0,16},{16,0},{1,17},{17,1},{2,18},{18,2},{3,19},{19,3},{4,20},{20... | collective-permute-start | bytes 3145736 | tf_op jit(solution)/shard_map/ppermute | solution.py:82
  117.5 2.2 %collective-permute-start.22 = (bf16[128,1024]{1,0:T(8,128)(2,1)}, bf16[128,1024]{1,0:T(8,128)(2,1)S(1)}, u32[]{:S(2)}, u32[]{:S(2)}) collective-permute-start(bf16[128,1024]{1,0:T(8,128)(2,1)} %collective-permute-done.19.refs_1_), channel_id=1, source_target_pairs={{0,4},{4,0},{8,12},{12,8},{1,5},{5,1},{9,13},{13,9},{2,6},{6,2},{1... | collective-permute-start | bytes 786440 | tf_op jit(solution)/shard_map/ppermute | solution.py:82
  117.5 2.2 %collective-permute-start.23 = (bf16[128,1024]{1,0:T(8,128)(2,1)}, bf16[128,1024]{1,0:T(8,128)(2,1)}, u32[]{:S(2)}, u32[]{:S(2)}) collective-permute-start(bf16[128,1024]{1,0:T(8,128)(2,1)} %collective-permute-done.20.refs_2_), channel_id=1, source_target_pairs={{0,4},{4,0},{8,12},{12,8},{1,5},{5,1},{9,13},{13,9},{2,6},{6,2},{1... | collective-permute-start | bytes 786440 | tf_op jit(solution)/shard_map/ppermute | solution.py:82
  118.0 2.1 %collective-permute-start.24 = (bf16[128,1024]{1,0:T(8,128)(2,1)}, bf16[128,1024]{1,0:T(8,128)(2,1)}, u32[]{:S(2)}, u32[]{:S(2)}) collective-permute-start(bf16[128,1024]{1,0:T(8,128)(2,1)} %collective-permute-done.21.refs_3_), channel_id=1, source_target_pairs={{0,4},{4,0},{8,12},{12,8},{1,5},{5,1},{9,13},{13,9},{2,6},{6,2},{1... | collective-permute-start | bytes 786440 | tf_op jit(solution)/shard_map/ppermute | solution.py:82
  118.2 11.6 %copy-start.2 = (f32[2,4,128,128]{3,2,1,0:T(8,128)S(1)}, f32[2,4,128,128]{3,2,1,0:T(8,128)}, u32[]{:S(2)}) copy-start(f32[2,4,128,128]{3,2,1,0:T(8,128)} %get-tuple-element.128.states) | copy-start | bytes 1572868
  118.2 11.6 %collective-permute-start.25 = (bf16[2,4,128,128]{3,2,1,0:T(8,128)(2,1)}, bf16[2,4,128,128]{3,2,1,0:T(8,128)(2,1)S(1)}, u32[]{:S(2)}, u32[]{:S(2)}) collective-permute-start(bf16[2,4,128,128]{3,2,1,0:T(8,128)(2,1)} %get-tuple-element.129), channel_id=1, source_target_pairs={{0,8},{4,12},{8,0},{12,4},{1,9},{5,13},{9,1},{13,5},{2,10},{6,14},... | collective-permute-start | bytes 786440 | tf_op jit(solution)/shard_map/ppermute | solution.py:82
  129.8 1.2 copy-start.1
  131.1 34.0 %copy-start.3 = (bf16[32,4096]{1,0:T(8,128)(2,1)S(1)}, bf16[32,4096]{1,0:T(8,128)(2,1)}, u32[]{:S(2)}) copy-start(bf16[32,4096]{1,0:T(8,128)(2,1)} %get-tuple-element.124.residual) | copy-start | bytes 786436
  131.6 1.4 collective-permute-start.26
  135.9 7.9 %collective-permute-start.27 = (bf16[32,2048]{1,0:T(8,128)(2,1)S(1)}, bf16[32,2048]{1,0:T(8,128)(2,1)S(1)}, u32[]{:S(2)}, u32[]{:S(2)}) collective-permute-start(bf16[32,2048]{1,0:T(8,128)(2,1)S(1)} %get-tuple-element.134), channel_id=1, source_target_pairs={{0,1},{1,2},{2,3},{3,0},{4,5},{5,6},{6,7},{7,4},{8,9},{9,10},{10,1... | collective-permute-start | bytes 393224 | tf_op jit(solution)/shard_map/ppermute | solution.py:82
  138.8 8.3 %collective-permute-start.31 = (bf16[512,1024]{1,0:T(8,128)(2,1)S(1)}, bf16[512,1024]{1,0:T(8,128)(2,1)S(1)}, u32[]{:S(2)}, u32[]{:S(2)}) collective-permute-start(bf16[512,1024]{1,0:T(8,128)(2,1)S(1)} %collective-permute-done.17.far_x), channel_id=1, source_target_pairs={{0,4},{4,0},{8,12},{12,8},{1,5},{5,1},{9,13},{13,9},{2,6},{6,2},{1... | collective-permute-start | bytes 3145736 | tf_op jit(solution)/shard_map/ppermute | solution.py:82
  143.8 3.4 %collective-permute-start.32 = (bf16[512,1024]{1,0:T(8,128)(2,1)}, bf16[512,1024]{1,0:T(8,128)(2,1)S(1)}, u32[]{:S(2)}, u32[]{:S(2)}) collective-permute-start(bf16[512,1024]{1,0:T(8,128)(2,1)} %collective-permute-done.30.far_y), channel_id=1, source_target_pairs={{0,4},{4,0},{8,12},{12,8},{1,5},{5,1},{9,13},{13,9},{2,6},{6,2},{1... | collective-permute-start | bytes 3145736 | tf_op jit(solution)/shard_map/ppermute | solution.py:82
  143.8 10.0 %collective-permute-start.28 = (bf16[32,2048]{1,0:T(8,128)(2,1)S(1)}, bf16[32,2048]{1,0:T(8,128)(2,1)S(1)}, u32[]{:S(2)}, u32[]{:S(2)}) collective-permute-start(bf16[32,2048]{1,0:T(8,128)(2,1)S(1)} %get-tuple-element.135), channel_id=1, source_target_pairs={{0,2},{1,3},{2,0},{3,1},{4,6},{5,7},{6,4},{7,5},{8,10},{9,11},{10,... | collective-permute-start | bytes 393224 | tf_op jit(solution)/shard_map/ppermute | solution.py:82
  144.2 9.6 %collective-permute-start.29 = (bf16[32,2048]{1,0:T(8,128)(2,1)S(1)}, bf16[32,2048]{1,0:T(8,128)(2,1)S(1)}, u32[]{:S(2)}, u32[]{:S(2)}) collective-permute-start(bf16[32,2048]{1,0:T(8,128)(2,1)S(1)} %get-tuple-element.136), channel_id=1, source_target_pairs={{0,3},{1,0},{2,1},{3,2},{4,7},{5,4},{6,5},{7,6},{8,11},{9,8},{10,9... | collective-permute-start | bytes 393224 | tf_op jit(solution)/shard_map/ppermute | solution.py:82
  149.7 8.3 %collective-permute-start.33 = (bf16[32,2048]{1,0:T(8,128)(2,1)S(1)}, bf16[32,2048]{1,0:T(8,128)(2,1)S(1)}, u32[]{:S(2)}, u32[]{:S(2)}) collective-permute-start(bf16[32,2048]{1,0:T(8,128)(2,1)S(1)} %get-tuple-element.142), channel_id=1, source_target_pairs={{0,1},{1,2},{2,3},{3,0},{4,5},{5,6},{6,7},{7,4},{8,9},{9,10},{10,1... | collective-permute-start | bytes 393224 | tf_op jit(solution)/shard_map/ppermute | solution.py:82
  150.3 14.8 %collective-permute-start.34 = (bf16[32,2048]{1,0:T(8,128)(2,1)S(1)}, bf16[32,2048]{1,0:T(8,128)(2,1)S(1)}, u32[]{:S(2)}, u32[]{:S(2)}) collective-permute-start(bf16[32,2048]{1,0:T(8,128)(2,1)S(1)} %get-tuple-element.143), channel_id=1, source_target_pairs={{0,2},{1,3},{2,0},{3,1},{4,6},{5,7},{6,4},{7,5},{8,10},{9,11},{10,... | collective-permute-start | bytes 393224 | tf_op jit(solution)/shard_map/ppermute | solution.py:82
  151.6 13.5 %collective-permute-start.35 = (bf16[32,2048]{1,0:T(8,128)(2,1)S(1)}, bf16[32,2048]{1,0:T(8,128)(2,1)S(1)}, u32[]{:S(2)}, u32[]{:S(2)}) collective-permute-start(bf16[32,2048]{1,0:T(8,128)(2,1)S(1)} %get-tuple-element.144), channel_id=1, source_target_pairs={{0,3},{1,0},{2,1},{3,2},{4,7},{5,4},{6,5},{7,6},{8,11},{9,8},{10,9... | collective-permute-start | bytes 393224 | tf_op jit(solution)/shard_map/ppermute | solution.py:82
  165.8 6.7 %collective-permute-start.36 = (bf16[32,1024]{1,0:T(8,128)(2,1)S(1)}, bf16[32,1024]{1,0:T(8,128)(2,1)S(1)}, u32[]{:S(2)}, u32[]{:S(2)}) collective-permute-start(bf16[32,1024]{1,0:T(8,128)(2,1)S(1)} %get-tuple-element.146), channel_id=1, source_target_pairs={{0,1},{1,2},{2,3},{3,0},{4,5},{5,6},{6,7},{7,4},{8,9},{9,10},{10,1... | collective-permute-start | bytes 196616 | tf_op jit(solution)/shard_map/ppermute | solution.py:82
  168.9 6.3 %collective-permute-start.37 = (bf16[32,1024]{1,0:T(8,128)(2,1)S(1)}, bf16[32,1024]{1,0:T(8,128)(2,1)S(1)}, u32[]{:S(2)}, u32[]{:S(2)}) collective-permute-start(bf16[32,1024]{1,0:T(8,128)(2,1)S(1)} %get-tuple-element.147), channel_id=1, source_target_pairs={{0,2},{1,3},{2,0},{3,1},{4,6},{5,7},{6,4},{7,5},{8,10},{9,11},{10,... | collective-permute-start | bytes 196616 | tf_op jit(solution)/shard_map/ppermute | solution.py:82
  170.2 5.1 %collective-permute-start.38 = (bf16[32,1024]{1,0:T(8,128)(2,1)S(1)}, bf16[32,1024]{1,0:T(8,128)(2,1)S(1)}, u32[]{:S(2)}, u32[]{:S(2)}) collective-permute-start(bf16[32,1024]{1,0:T(8,128)(2,1)S(1)} %get-tuple-element.148), channel_id=1, source_target_pairs={{0,3},{1,0},{2,1},{3,2},{4,7},{5,4},{6,5},{7,6},{8,11},{9,8},{10,9... | collective-permute-start | bytes 196616 | tf_op jit(solution)/shard_map/ppermute | solution.py:82
  (1 other events, 0.7 us)

commit v5 on v4

--- a/solution.py
+++ b/solution.py
@@ -460,10 +460,9 @@
         *far_of(2),
     )
 
-    states, rounded, out_x, query_y, query_x, e, sib_e = tie(
-        (states, rounded, out_x, query_y, query_x, e, sib_e)
-    )
+    states, rounded, e, sib_e = tie((states, rounded, e, sib_e))
     sib_e += [sib(array) for array in e[1:]]
+    states, rounded, out_x, query_y, query_x = tie((states, rounded, out_x, query_y, query_x))
     out_y = swap(out_x)
     others = permute(rounded, "ctx", to_far)
 
@@ -521,7 +520,7 @@
         return [terms[0]] + [moved[k] for k in range(1, nhead)]
 
     near = spread(near_kernel, "near_terms", (heads_own, heads_sib), (out_weight, out_sib), [])
-    heads_own, heads_sib, out_y = tie((heads_own, heads_sib, out_y, near[1]))[:3]
+    heads_own, heads_sib, out_y = tie((heads_own, heads_sib, out_y, near[2]))[:3]
     diag_x = sib(out_x)
     far = spread(
         far_kernel,

time: 177 us -> 176 us (level)
  no operation moved by 1% of the time
where the time goes in v5:
time: 176 us
  waiting for transfers between devices  75.1 us (43%)
  starting transfers between devices  38.5 us (22%)
  Pallas kernels  34.8 us (20%)
  local copies, waits for them, and re-layouts  22.8 us (13%)
  other arithmetic  4.38 us (2%)
    ppermute x39, waiting for transfers between devices, permute(): return lax.ppermute(array, axis, pairs)  75.1 us
    ppermute x39, starting transfers between devices, permute(): return lax.ppermute(array, axis, pairs)  38.5 us
    pallas_call x1, Pallas kernels, permuted_plan(): pl.pallas_call(functools.partial(state_kernel, nblocks), out_shape=(jax.S...  17.4 us
    gather x1, local copies, waits for them, and re-layouts, lookup(): jnp.take(embed_table, jnp.clip(offset_ids, 0, embed_table.shape[0] - 1),...  11.4 us
    pallas_call x1, Pallas kernels, permuted_plan(): pl.pallas_call(functools.partial(project_kernel, nhead, steps), out_shape...  9.35 us
    pallas_call x4, Pallas kernels, small_call(): pl.pallas_call(kernel, out_shape=outs, grid_spec=pltpu.PrefetchScalarGrid...  7.51 us
    squeeze x3, local copies, waits for them, and re-layouts, fetched(): lax.dynamic_slice(weight, (k, 0, (core ^ grp) * cols), (1, block, cols))[0]  6.84 us
  transfers between devices with their start and end apart: 39, of which 20 were waited for; matrix products, arithmetic and copies ran while one was open for 13% of the time, Pallas kernels for 19%

profile of v5, /device:TPU:0, one launch (start us, length us, event | category | flops | bytes accessed | tf_op | source)
XLA Modules:
  0.0 175.9 jit_solution(4634878083681691979)
XLA Ops:
  0.0 2.3 %dynamic-slice_bitcast_fusion.2 = bf16[1024,512]{1,0:T(8,128)(2,1)} fusion(bf16[3,1024,1024]{2,1,0:T(8,128)(2,1)} %refs_10_.1, s32[]{:T(128)S(6)} %select_n.115), kind=kLoop, calls=%fused_computation.4 | loop fusion | bytes 2097156 | tf_op jit(solution)/shard_map/squeeze | solution.py:349
  2.8 3.0 %collective-permute-start = (bf16[2,256,1024]{2,1,0:T(8,128)(2,1)}, bf16[2,256,1024]{2,1,0:T(8,128)(2,1)}, u32[]{:S(2)}, u32[]{:S(2)}) collective-permute-start(bf16[2,256,1024]{2,1,0:T(8,128)(2,1)} %refs_0_), channel_id=1, source_target_pairs={{0,1},{1,2},{2,3},{3,0},{4,5},{5,6},{6,7},{7,4},{8,9},{9,10},{10,1... | collective-permute-start | bytes 3145736 | tf_op jit(solution)/shard_map/ppermute | solution.py:82
  5.8 1.5 collective-permute-start.1
  7.3 2.3 %dynamic-slice_bitcast_fusion.1 = bf16[1024,512]{1,0:T(8,128)(2,1)} fusion(bf16[3,1024,1024]{2,1,0:T(8,128)(2,1)} %refs_10_.1, s32[]{:T(128)S(6)} %select_n.115), kind=kLoop, calls=%fused_computation.3 | loop fusion | bytes 2097156 | tf_op jit(solution)/shard_map/squeeze | solution.py:349
  11.2 11.4 %gather_fusion = bf16[512,1024]{1,0:T(8,128)(2,1)} fusion(bf16[8192,1024]{1,0:T(8,128)(2,1)} %param.9, s32[1024]{0:T(1024)S(1)} %pad_clamp_fusion), kind=kCustom, calls=%fused_computation | custom fusion | bytes 2099200 | tf_op jit(solution)/shard_map/jit(_take)/gather | solution.py:326
  22.6 1.6 select_select_fusion
  24.2 0.9 constant_dynamic-slice_fusion.3
  25.1 0.9 copy.14
  27.0 4.5 %collective-permute-done.refs_1_ = bf16[2,256,1024]{2,1,0:T(8,128)(2,1)} collective-permute-done((bf16[2,256,1024]{2,1,0:T(8,128)(2,1)}, bf16[2,256,1024]{2,1,0:T(8,128)(2,1)}, u32[]{:S(2)}, u32[]{:S(2)}) %collective-permute-start) | collective-permute-done | bytes 1048608 | tf_op jit(solution)/shard_map/ppermute | solution.py:82
  31.7 1.6 collective-permute-start.5
  33.2 1.6 collective-permute-start.6
  34.8 0.8 collective-permute-start.7
  35.7 1.3 bitcast_add_fusion
  37.6 2.3 %dynamic-slice_bitcast_fusion = bf16[1024,512]{1,0:T(8,128)(2,1)} fusion(bf16[3,1024,1024]{2,1,0:T(8,128)(2,1)} %refs_10_.1, s32[]{:T(128)S(6)} %select_n.115), kind=kLoop, calls=%fused_computation.1 | loop fusion | bytes 2097156 | tf_op jit(solution)/shard_map/squeeze | solution.py:349
  39.8 18.2 %collective-permute-done.5.refs_14_.refs_18_ = bf16[1024,512]{1,0:T(8,128)(2,1)} collective-permute-done((bf16[1024,512]{1,0:T(8,128)(2,1)}, bf16[1024,512]{1,0:T(8,128)(2,1)}, u32[]{:S(2)}, u32[]{:S(2)}) %collective-permute-start.5) | collective-permute-done | bytes 1048608 | tf_op jit(solution)/shard_map/ppermute | solution.py:82
  58.0 2.6 %collective-permute-done.6.refs_2_ = bf16[2,256,1024]{2,1,0:T(8,128)(2,1)} collective-permute-done((bf16[2,256,1024]{2,1,0:T(8,128)(2,1)}, bf16[2,256,1024]{2,1,0:T(8,128)(2,1)}, u32[]{:S(2)}, u32[]{:S(2)}) %collective-permute-start.6) | collective-permute-done | bytes 1048608 | tf_op jit(solution)/shard_map/ppermute | solution.py:82
  60.6 0.9 collective-permute-start.10
  61.5 1.6 collective-permute-done.13
  63.1 1.5 collective-permute-start.11
  64.6 1.5 collective-permute-start.12
  66.3 1.6 collective-permute-done.15.refs_4_
  67.9 19.2 %collective-permute-done.10.refs_3_ = bf16[2,256,1024]{2,1,0:T(8,128)(2,1)} collective-permute-done((bf16[2,256,1024]{2,1,0:T(8,128)(2,1)}, bf16[2,256,1024]{2,1,0:T(8,128)(2,1)}, u32[]{:S(2)}, u32[]{:S(2)}) %collective-permute-start.10) | collective-permute-done | bytes 1048608 | tf_op jit(solution)/shard_map/ppermute | solution.py:82
  87.1 1.9 %collective-permute-done.11.refs_14_ = bf16[1024,512]{1,0:T(8,128)(2,1)} collective-permute-done((bf16[1024,512]{1,0:T(8,128)(2,1)}, bf16[1024,512]{1,0:T(8,128)(2,1)}, u32[]{:S(2)}, u32[]{:S(2)}) %collective-permute-start.11) | collective-permute-done | bytes 1048608 | tf_op jit(solution)/shard_map/ppermute | solution.py:82
  89.0 1.2 collective-permute-done.12.refs_15_.refs_19_
  90.2 1.3 collective-permute-start.23
  92.0 1.3 collective-permute-start.17
  93.3 1.2 collective-permute-start.18
  94.5 2.7 %collective-permute-start.19 = (bf16[128,1024]{1,0:T(8,128)(2,1)S(1)}, bf16[128,1024]{1,0:T(8,128)(2,1)}, u32[]{:S(2)}, u32[]{:S(2)}) collective-permute-start(bf16[128,1024]{1,0:T(8,128)(2,1)S(1)} %add.105.refs_0_), channel_id=1, source_target_pairs={{0,3},{1,0},{2,1},{3,2},{4,7},{5,4},{6,5},{7,6},{8,11},{9,8},{10,9... | collective-permute-start | bytes 786440 | tf_op jit(solution)/shard_map/ppermute | solution.py:82
  97.2 17.4 %prompt_state.1 = (f32[2,4,128,128]{3,2,1,0:T(8,128)}, bf16[2,4,128,128]{3,2,1,0:T(8,128)(2,1)}) custom-call(s32[7]{0:T(128)} %stack.74.meta, bf16[2,256,1024]{2,1,0:T(8,128)(2,1)} %refs_0_, bf16[2,256,1024]{2,1,0:T(8,128)(2,1)} %collective-permute-done.refs_1_, bf16[2,256,1024]{2,1,0:T(8,128)(2,1)} %collective-permute-done.6.refs_2_, ...), custom_call_target="tpu_custom_call" | custom-call | flops 8589934592 | bytes 16777216 | tf_op jit(solution)/shard_map/prompt_state/pallas_call | solution.py:428
  114.7 1.3 collective-permute-done.23.refs_15_
  118.8 0.8 collective-permute-done.20.refs_5_
  120.3 9.3 %response_rows.1 = (f32[256,1024]{1,0:T(8,128)}, bf16[32,4096]{1,0:T(8,128)(2,1)}) custom-call(s32[7]{0:T(128)} %stack.74.meta, bf16[128,1024]{1,0:T(8,128)(2,1)} %copy-done.5, bf16[128,1024]{1,0:T(8,128)(2,1)} %collective-permute-done.17.refs_1_, bf16[128,1024]{1,0:T(8,128)(2,1)} %collective-permute-done.18.refs_2_, ...), custom_call_target="tpu_custom_call" | custom-call | flops 3221225472 | bytes 14680064 | tf_op jit(solution)/shard_map/response_rows/pallas_call | solution.py:473
  129.7 1.2 copy-done.1
  131.7 1.2 collective-permute-done.26.heads_sib
  132.9 2.9 %near_terms.1 = (f32[32,2048]{1,0:T(8,128)S(1)}, bf16[32,2048]{1,0:T(8,128)(2,1)S(1)}, bf16[32,2048]{1,0:T(8,128)(2,1)S(1)}, bf16[32,2048]{1,0:T(8,128)(2,1)S(1)}) custom-call(s32[6]{0:T(128)S(1)} %stack.79.meta, bf16[128,512]{1,0:T(8,128)(2,1)S(1)} %get-tuple-element.142.heads_own, bf16[128,512]{1,0:T(8,128)(2,1)S(1)} %collective-permute-done.26.heads_sib, ...), custom_call_target="tpu_custom_call" | custom-call | flops 536870912 | bytes 4194304 | tf_op jit(solution)/shard_map/near_terms/pallas_call | solution.py:290
  135.8 2.7 %collective-permute-start.28 = (bf16[32,2048]{1,0:T(8,128)(2,1)S(1)}, bf16[32,2048]{1,0:T(8,128)(2,1)S(1)}, u32[]{:S(2)}, u32[]{:S(2)}) collective-permute-start(bf16[32,2048]{1,0:T(8,128)(2,1)S(1)} %get-tuple-element.139), channel_id=1, source_target_pairs={{0,2},{1,3},{2,0},{3,1},{4,6},{5,7},{6,4},{7,5},{8,10},{9,11},{10,... | collective-permute-start | bytes 393224 | tf_op jit(solution)/shard_map/ppermute | solution.py:82
  138.4 6.7 %collective-permute-done.28.refs_2_ = bf16[32,2048]{1,0:T(8,128)(2,1)S(1)} collective-permute-done((bf16[32,2048]{1,0:T(8,128)(2,1)S(1)}, bf16[32,2048]{1,0:T(8,128)(2,1)S(1)}, u32[]{:S(2)}, u32[]{:S(2)}) %collective-permute-start.28) | collective-permute-done | bytes 131104 | tf_op jit(solution)/shard_map/ppermute | solution.py:82
  145.8 3.1 %collective-permute-start.29 = (bf16[32,2048]{1,0:T(8,128)(2,1)S(1)}, bf16[32,2048]{1,0:T(8,128)(2,1)S(1)}, u32[]{:S(2)}, u32[]{:S(2)}) collective-permute-start(bf16[32,2048]{1,0:T(8,128)(2,1)S(1)} %get-tuple-element.140), channel_id=1, source_target_pairs={{0,3},{1,0},{2,1},{3,2},{4,7},{5,4},{6,5},{7,6},{8,11},{9,8},{10,9... | collective-permute-start | bytes 393224 | tf_op jit(solution)/shard_map/ppermute | solution.py:82
  148.9 2.5 %far_terms.1 = (f32[32,2048]{1,0:T(8,128)S(1)}, bf16[32,2048]{1,0:T(8,128)(2,1)S(1)}, bf16[32,2048]{1,0:T(8,128)(2,1)S(1)}, bf16[32,2048]{1,0:T(8,128)(2,1)S(1)}) custom-call(s32[6]{0:T(128)S(1)} %stack.79.meta, bf16[128,512]{1,0:T(8,128)(2,1)S(1)} %get-tuple-element.142.heads_own, bf16[128,512]{1,0:T(8,128)(2,1)S(1)} %collective-permute-done.26.heads_sib, ...), custom_call_target="tpu_custom_call" | custom-call | flops 536870912 | bytes 4194304 | tf_op jit(solution)/shard_map/far_terms/pallas_call | solution.py:290
  151.6 3.1 %collective-permute-start.34 = (bf16[32,2048]{1,0:T(8,128)(2,1)S(1)}, bf16[32,2048]{1,0:T(8,128)(2,1)S(1)}, u32[]{:S(2)}, u32[]{:S(2)}) collective-permute-start(bf16[32,2048]{1,0:T(8,128)(2,1)S(1)} %get-tuple-element.147), channel_id=1, source_target_pairs={{0,2},{1,3},{2,0},{3,1},{4,6},{5,7},{6,4},{7,5},{8,10},{9,11},{10,... | collective-permute-start | bytes 393224 | tf_op jit(solution)/shard_map/ppermute | solution.py:82
  155.4 4.4 %collective-permute-done.33.refs_5_ = bf16[32,2048]{1,0:T(8,128)(2,1)S(1)} collective-permute-done((bf16[32,2048]{1,0:T(8,128)(2,1)S(1)}, bf16[32,2048]{1,0:T(8,128)(2,1)S(1)}, u32[]{:S(2)}, u32[]{:S(2)}) %collective-permute-start.33) | collective-permute-done | bytes 131104 | tf_op jit(solution)/shard_map/ppermute | solution.py:82
  159.8 4.7 %collective-permute-done.34.refs_6_ = bf16[32,2048]{1,0:T(8,128)(2,1)S(1)} collective-permute-done((bf16[32,2048]{1,0:T(8,128)(2,1)S(1)}, bf16[32,2048]{1,0:T(8,128)(2,1)S(1)}, u32[]{:S(2)}, u32[]{:S(2)}) %collective-permute-start.34) | collective-permute-done | bytes 131104 | tf_op jit(solution)/shard_map/ppermute | solution.py:82
  164.5 0.8 final_norm.1
  165.3 3.0 %collective-permute-start.36 = (bf16[32,1024]{1,0:T(8,128)(2,1)S(1)}, bf16[32,1024]{1,0:T(8,128)(2,1)S(1)}, u32[]{:S(2)}, u32[]{:S(2)}) collective-permute-start(bf16[32,1024]{1,0:T(8,128)(2,1)S(1)} %get-tuple-element.150), channel_id=1, source_target_pairs={{0,1},{1,2},{2,3},{3,0},{4,5},{5,6},{6,7},{7,4},{8,9},{9,10},{10,1... | collective-permute-start | bytes 196616 | tf_op jit(solution)/shard_map/ppermute | solution.py:82
  169.1 1.7 collective-permute-start.38
  170.7 1.2 collective-permute-done.36.refs_1_
  171.9 2.7 %collective-permute-done.37.refs_2_ = bf16[32,1024]{1,0:T(8,128)(2,1)S(1)} collective-permute-done((bf16[32,1024]{1,0:T(8,128)(2,1)S(1)}, bf16[32,1024]{1,0:T(8,128)(2,1)S(1)}, u32[]{:S(2)}, u32[]{:S(2)}) %collective-permute-start.37) | collective-permute-done | bytes 65568 | tf_op jit(solution)/shard_map/ppermute | solution.py:82
  174.6 1.3 place.1
  (83 shorter events, 11.3 us)
Async XLA Ops:
  2.3 29.3 %collective-permute-start.3 = (bf16[3,1024,1024]{2,1,0:T(8,128)(2,1)}, bf16[3,1024,1024]{2,1,0:T(8,128)(2,1)}, u32[]{:S(2)}, u32[]{:S(2)}) collective-permute-start(bf16[3,1024,1024]{2,1,0:T(8,128)(2,1)} %refs_10_.1), channel_id=1, source_target_pairs={{0,4},{4,0},{8,12},{12,8},{1,5},{5,1},{9,13},{13,9},{2,6},{6,2},{1... | collective-permute-start | bytes 18874376 | tf_op jit(solution)/shard_map/ppermute | solution.py:82
  2.7 28.9 %collective-permute-start.4 = (bf16[1024,1024]{1,0:T(8,128)(2,1)}, bf16[1024,1024]{1,0:T(8,128)(2,1)}, u32[]{:S(2)}, u32[]{:S(2)}) collective-permute-start(bf16[1024,1024]{1,0:T(8,128)(2,1)} %own.1), channel_id=1, source_target_pairs={{0,4},{4,0},{8,12},{12,8},{1,5},{5,1},{9,13},{13,9},{2,6},{6,2},{1... | collective-permute-start | bytes 6291464 | tf_op jit(solution)/shard_map/ppermute | solution.py:82
  2.8 28.7 %collective-permute-start = (bf16[2,256,1024]{2,1,0:T(8,128)(2,1)}, bf16[2,256,1024]{2,1,0:T(8,128)(2,1)}, u32[]{:S(2)}, u32[]{:S(2)}) collective-permute-start(bf16[2,256,1024]{2,1,0:T(8,128)(2,1)} %refs_0_), channel_id=1, source_target_pairs={{0,1},{1,2},{2,3},{3,0},{4,5},{5,6},{6,7},{7,4},{8,9},{9,10},{10,1... | collective-permute-start | bytes 3145736 | tf_op jit(solution)/shard_map/ppermute | solution.py:82
  5.8 25.8 %collective-permute-start.2 = (bf16[2,256,1024]{2,1,0:T(8,128)(2,1)}, bf16[2,256,1024]{2,1,0:T(8,128)(2,1)}, u32[]{:S(2)}, u32[]{:S(2)}) collective-permute-start(bf16[2,256,1024]{2,1,0:T(8,128)(2,1)} %refs_0_), channel_id=1, source_target_pairs={{0,4},{4,0},{8,12},{12,8},{1,5},{5,1},{9,13},{13,9},{2,6},{6,2},{1... | collective-permute-start | bytes 3145736 | tf_op jit(solution)/shard_map/ppermute | solution.py:82
  5.8 25.8 %collective-permute-start.1 = (bf16[1024,512]{1,0:T(8,128)(2,1)}, bf16[1024,512]{1,0:T(8,128)(2,1)S(1)}, u32[]{:S(2)}, u32[]{:S(2)}) collective-permute-start(bf16[1024,512]{1,0:T(8,128)(2,1)} %dynamic-slice_bitcast_fusion.2), channel_id=1, source_target_pairs={{0,8},{4,12},{8,0},{12,4},{16,28},{20,24},{24,20},{28,16},{1,9},{5... | collective-permute-start | bytes 3145736 | tf_op jit(solution)/shard_map/ppermute | solution.py:82
  11.2 14.8 %copy-start.9 = (s32[128]{0:T(128)S(1)}, s32[128]{0:T(128)}, u32[]{:S(2)}) copy-start(s32[128]{0:T(128)} %param.11) | copy-start | bytes 1540
  22.6 43.6 %copy-start = (bf16[1024,1024]{1,0:T(8,128)(2,1)S(1)}, bf16[1024,1024]{1,0:T(8,128)(2,1)}, u32[]{:S(2)}) copy-start(bf16[1024,1024]{1,0:T(8,128)(2,1)} %own.1) | copy-start | bytes 6291460
  31.6 58.6 %copy-start.4 = (bf16[1024,512]{1,0:T(8,128)(2,1)}, bf16[1024,512]{1,0:T(8,128)(2,1)S(1)}, u32[]{:S(2)}) copy-start(bf16[1024,512]{1,0:T(8,128)(2,1)S(1)} %collective-permute-done.1.refs_12_.refs_16_) | copy-start | bytes 3145732
  31.6 4.1 %collective-permute-start.9 = (bf16[4,2,32,1024]{3,2,0,1:T(8,128)(2,1)}, bf16[4,2,32,1024]{3,2,0,1:T(8,128)(2,1)}, u32[]{:S(2)}, u32[]{:S(2)}) collective-permute-start(bf16[4,2,32,1024]{3,2,0,1:T(8,128)(2,1)} %bitcast.37), channel_id=1, source_target_pairs={{0,4},{4,0},{8,12},{12,8},{1,5},{5,1},{9,13},{13,9},{2,6},{6,2},{1... | collective-permute-start | bytes 1572872 | tf_op jit(solution)/shard_map/ppermute | solution.py:82
  31.7 26.3 %collective-permute-start.5 = (bf16[1024,512]{1,0:T(8,128)(2,1)}, bf16[1024,512]{1,0:T(8,128)(2,1)}, u32[]{:S(2)}, u32[]{:S(2)}) collective-permute-start(bf16[1024,512]{1,0:T(8,128)(2,1)} %dynamic-slice_bitcast_fusion.1), channel_id=1, source_target_pairs={{0,8},{4,12},{8,0},{12,4},{16,28},{20,24},{24,20},{28,16},{1,9},{5... | collective-permute-start | bytes 3145736 | tf_op jit(solution)/shard_map/ppermute | solution.py:82
  33.2 27.3 %collective-permute-start.6 = (bf16[2,256,1024]{2,1,0:T(8,128)(2,1)}, bf16[2,256,1024]{2,1,0:T(8,128)(2,1)}, u32[]{:S(2)}, u32[]{:S(2)}) collective-permute-start(bf16[2,256,1024]{2,1,0:T(8,128)(2,1)} %collective-permute-done.refs_1_), channel_id=1, source_target_pairs={{0,1},{1,2},{2,3},{3,0},{4,5},{5,6},{6,7},{7,4},{8,9},{9,10},{10,1... | collective-permute-start | bytes 3145736 | tf_op jit(solution)/shard_map/ppermute | solution.py:82
  34.8 25.8 %collective-permute-start.7 = (bf16[1024,512]{1,0:T(8,128)(2,1)S(1)}, bf16[1024,512]{1,0:T(8,128)(2,1)}, u32[]{:S(2)}, u32[]{:S(2)}) collective-permute-start(bf16[1024,512]{1,0:T(8,128)(2,1)S(1)} %collective-permute-done.1.refs_12_.refs_16_), channel_id=1, source_target_pairs={{0,16},{16,0},{1,17},{17,1},{2,18},{18,2},{3,19},{19,3},{4,20},{20... | collective-permute-start | bytes 3145736 | tf_op jit(solution)/shard_map/ppermute | solution.py:82
  35.7 24.9 %collective-permute-start.8 = (bf16[2,256,1024]{2,1,0:T(8,128)(2,1)}, bf16[2,256,1024]{2,1,0:T(8,128)(2,1)}, u32[]{:S(2)}, u32[]{:S(2)}) collective-permute-start(bf16[2,256,1024]{2,1,0:T(8,128)(2,1)} %collective-permute-done.refs_1_), channel_id=1, source_target_pairs={{0,4},{4,0},{8,12},{12,8},{1,5},{5,1},{9,13},{13,9},{2,6},{6,2},{1... | collective-permute-start | bytes 3145736 | tf_op jit(solution)/shard_map/ppermute | solution.py:82
  37.0 26.1 %collective-permute-start.13 = (bf16[128,1024]{1,0:T(8,128)(2,1)S(1)}, bf16[128,1024]{1,0:T(8,128)(2,1)S(1)}, u32[]{:S(2)}, u32[]{:S(2)}) collective-permute-start(bf16[128,1024]{1,0:T(8,128)(2,1)S(1)} %bitcast.38), channel_id=1, source_target_pairs={{0,8},{4,12},{8,0},{12,4},{1,9},{5,13},{9,1},{13,5},{2,10},{6,14},... | collective-permute-start | bytes 786440 | tf_op jit(solution)/shard_map/ppermute | solution.py:82
  60.6 26.5 %collective-permute-start.10 = (bf16[2,256,1024]{2,1,0:T(8,128)(2,1)}, bf16[2,256,1024]{2,1,0:T(8,128)(2,1)}, u32[]{:S(2)}, u32[]{:S(2)}) collective-permute-start(bf16[2,256,1024]{2,1,0:T(8,128)(2,1)} %collective-permute-done.6.refs_2_), channel_id=1, source_target_pairs={{0,1},{1,2},{2,3},{3,0},{4,5},{5,6},{6,7},{7,4},{8,9},{9,10},{10,1... | collective-permute-start | bytes 3145736 | tf_op jit(solution)/shard_map/ppermute | solution.py:82
  63.1 4.8 %collective-permute-start.14 = (bf16[2,256,1024]{2,1,0:T(8,128)(2,1)}, bf16[2,256,1024]{2,1,0:T(8,128)(2,1)}, u32[]{:S(2)}, u32[]{:S(2)}) collective-permute-start(bf16[2,256,1024]{2,1,0:T(8,128)(2,1)} %collective-permute-done.6.refs_2_), channel_id=1, source_target_pairs={{0,4},{4,0},{8,12},{12,8},{1,5},{5,1},{9,13},{13,9},{2,6},{6,2},{1... | collective-permute-start | bytes 3145736 | tf_op jit(solution)/shard_map/ppermute | solution.py:82
  63.1 25.9 %collective-permute-start.11 = (bf16[1024,512]{1,0:T(8,128)(2,1)}, bf16[1024,512]{1,0:T(8,128)(2,1)}, u32[]{:S(2)}, u32[]{:S(2)}) collective-permute-start(bf16[1024,512]{1,0:T(8,128)(2,1)} %dynamic-slice_bitcast_fusion), channel_id=1, source_target_pairs={{0,8},{4,12},{8,0},{12,4},{16,28},{20,24},{24,20},{28,16},{1,9},{5... | collective-permute-start | bytes 3145736 | tf_op jit(solution)/shard_map/ppermute | solution.py:82
  64.6 25.6 %collective-permute-start.12 = (bf16[1024,512]{1,0:T(8,128)(2,1)}, bf16[1024,512]{1,0:T(8,128)(2,1)}, u32[]{:S(2)}, u32[]{:S(2)}) collective-permute-start(bf16[1024,512]{1,0:T(8,128)(2,1)} %collective-permute-done.5.refs_14_.refs_18_), channel_id=1, source_target_pairs={{0,16},{16,0},{1,17},{17,1},{2,18},{18,2},{3,19},{19,3},{4,20},{20... | collective-permute-start | bytes 3145736 | tf_op jit(solution)/shard_map/ppermute | solution.py:82
  66.2 48.5 %copy-start.5 = (bf16[128,1024]{1,0:T(8,128)(2,1)}, bf16[128,1024]{1,0:T(8,128)(2,1)S(1)}, u32[]{:S(2)}) copy-start(bf16[128,1024]{1,0:T(8,128)(2,1)S(1)} %add.105.refs_0_) | copy-start | bytes 786436
  66.2 1.7 collective-permute-start.15
  90.2 4.3 %collective-permute-start.16 = (bf16[2,256,1024]{2,1,0:T(8,128)(2,1)}, bf16[2,256,1024]{2,1,0:T(8,128)(2,1)S(1)}, u32[]{:S(2)}, u32[]{:S(2)}) collective-permute-start(bf16[2,256,1024]{2,1,0:T(8,128)(2,1)} %collective-permute-done.10.refs_3_), channel_id=1, source_target_pairs={{0,4},{4,0},{8,12},{12,8},{1,5},{5,1},{9,13},{13,9},{2,6},{6,2},{1... | collective-permute-start | bytes 3145736 | tf_op jit(solution)/shard_map/ppermute | solution.py:82
  90.2 25.8 %collective-permute-start.23 = (bf16[1024,512]{1,0:T(8,128)(2,1)}, bf16[1024,512]{1,0:T(8,128)(2,1)S(1)}, u32[]{:S(2)}, u32[]{:S(2)}) collective-permute-start(bf16[1024,512]{1,0:T(8,128)(2,1)} %collective-permute-done.11.refs_14_), channel_id=1, source_target_pairs={{0,16},{16,0},{1,17},{17,1},{2,18},{18,2},{3,19},{19,3},{4,20},{20... | collective-permute-start | bytes 3145736 | tf_op jit(solution)/shard_map/ppermute | solution.py:82
  91.5 25.3 %collective-permute-start.24 = (bf16[512,1024]{1,0:T(8,128)(2,1)S(1)}, bf16[512,1024]{1,0:T(8,128)(2,1)S(1)}, u32[]{:S(2)}, u32[]{:S(2)}) collective-permute-start(bf16[512,1024]{1,0:T(8,128)(2,1)S(1)} %constant_dynamic-slice_fusion), channel_id=1, source_target_pairs={{0,8},{4,12},{8,0},{12,4},{1,9},{5,13},{9,1},{13,5},{2,10},{6,14},... | collective-permute-start | bytes 3145736 | tf_op jit(solution)/shard_map/ppermute | solution.py:82
  92.0 22.7 %collective-permute-start.17 = (bf16[128,1024]{1,0:T(8,128)(2,1)S(1)}, bf16[128,1024]{1,0:T(8,128)(2,1)}, u32[]{:S(2)}, u32[]{:S(2)}) collective-permute-start(bf16[128,1024]{1,0:T(8,128)(2,1)S(1)} %add.105.refs_0_), channel_id=1, source_target_pairs={{0,1},{1,2},{2,3},{3,0},{4,5},{5,6},{6,7},{7,4},{8,9},{9,10},{10,1... | collective-permute-start | bytes 786440 | tf_op jit(solution)/shard_map/ppermute | solution.py:82
  93.3 21.4 %collective-permute-start.18 = (bf16[128,1024]{1,0:T(8,128)(2,1)S(1)}, bf16[128,1024]{1,0:T(8,128)(2,1)}, u32[]{:S(2)}, u32[]{:S(2)}) collective-permute-start(bf16[128,1024]{1,0:T(8,128)(2,1)S(1)} %add.105.refs_0_), channel_id=1, source_target_pairs={{0,2},{1,3},{2,0},{3,1},{4,6},{5,7},{6,4},{7,5},{8,10},{9,11},{10,... | collective-permute-start | bytes 786440 | tf_op jit(solution)/shard_map/ppermute | solution.py:82
  94.5 2.7 %copy-start.7 = (bf16[2,256,1024]{2,1,0:T(8,128)(2,1)}, bf16[2,256,1024]{2,1,0:T(8,128)(2,1)S(1)}, u32[]{:S(2)}) copy-start(bf16[2,256,1024]{2,1,0:T(8,128)(2,1)S(1)} %collective-permute-done.16.refs_7_) | copy-start | bytes 3145732
  94.5 20.2 %collective-permute-start.19 = (bf16[128,1024]{1,0:T(8,128)(2,1)S(1)}, bf16[128,1024]{1,0:T(8,128)(2,1)}, u32[]{:S(2)}, u32[]{:S(2)}) collective-permute-start(bf16[128,1024]{1,0:T(8,128)(2,1)S(1)} %add.105.refs_0_), channel_id=1, source_target_pairs={{0,3},{1,0},{2,1},{3,2},{4,7},{5,4},{6,5},{7,6},{8,11},{9,8},{10,9... | collective-permute-start | bytes 786440 | tf_op jit(solution)/shard_map/ppermute | solution.py:82
  116.0 2.0 %copy-start.6 = (bf16[1024,512]{1,0:T(8,128)(2,1)}, bf16[1024,512]{1,0:T(8,128)(2,1)S(1)}, u32[]{:S(2)}) copy-start(bf16[1024,512]{1,0:T(8,128)(2,1)S(1)} %collective-permute-done.23.refs_15_) | copy-start | bytes 3145732
  116.8 28.3 %collective-permute-start.30 = (bf16[512,1024]{1,0:T(8,128)(2,1)S(1)}, bf16[512,1024]{1,0:T(8,128)(2,1)}, u32[]{:S(2)}, u32[]{:S(2)}) collective-permute-start(bf16[512,1024]{1,0:T(8,128)(2,1)S(1)} %collective-permute-done.24.far_x), channel_id=1, source_target_pairs={{0,16},{16,0},{1,17},{17,1},{2,18},{18,2},{3,19},{19,3},{4,20},{20... | collective-permute-start | bytes 3145736 | tf_op jit(solution)/shard_map/ppermute | solution.py:82
  117.5 2.1 %collective-permute-start.20 = (bf16[128,1024]{1,0:T(8,128)(2,1)}, bf16[128,1024]{1,0:T(8,128)(2,1)S(1)}, u32[]{:S(2)}, u32[]{:S(2)}) collective-permute-start(bf16[128,1024]{1,0:T(8,128)(2,1)} %collective-permute-done.17.refs_1_), channel_id=1, source_target_pairs={{0,4},{4,0},{8,12},{12,8},{1,5},{5,1},{9,13},{13,9},{2,6},{6,2},{1... | collective-permute-start | bytes 786440 | tf_op jit(solution)/shard_map/ppermute | solution.py:82
  117.5 2.2 %collective-permute-start.21 = (bf16[128,1024]{1,0:T(8,128)(2,1)}, bf16[128,1024]{1,0:T(8,128)(2,1)}, u32[]{:S(2)}, u32[]{:S(2)}) collective-permute-start(bf16[128,1024]{1,0:T(8,128)(2,1)} %collective-permute-done.18.refs_2_), channel_id=1, source_target_pairs={{0,4},{4,0},{8,12},{12,8},{1,5},{5,1},{9,13},{13,9},{2,6},{6,2},{1... | collective-permute-start | bytes 786440 | tf_op jit(solution)/shard_map/ppermute | solution.py:82
  118.0 2.1 %collective-permute-start.22 = (bf16[128,1024]{1,0:T(8,128)(2,1)}, bf16[128,1024]{1,0:T(8,128)(2,1)}, u32[]{:S(2)}, u32[]{:S(2)}) collective-permute-start(bf16[128,1024]{1,0:T(8,128)(2,1)} %collective-permute-done.19.refs_3_), channel_id=1, source_target_pairs={{0,4},{4,0},{8,12},{12,8},{1,5},{5,1},{9,13},{13,9},{2,6},{6,2},{1... | collective-permute-start | bytes 786440 | tf_op jit(solution)/shard_map/ppermute | solution.py:82
  118.2 11.5 %copy-start.2 = (f32[2,4,128,128]{3,2,1,0:T(8,128)S(1)}, f32[2,4,128,128]{3,2,1,0:T(8,128)}, u32[]{:S(2)}) copy-start(f32[2,4,128,128]{3,2,1,0:T(8,128)} %get-tuple-element.132.states) | copy-start | bytes 1572868
  118.2 11.5 %collective-permute-start.25 = (bf16[2,4,128,128]{3,2,1,0:T(8,128)(2,1)}, bf16[2,4,128,128]{3,2,1,0:T(8,128)(2,1)S(1)}, u32[]{:S(2)}, u32[]{:S(2)}) collective-permute-start(bf16[2,4,128,128]{3,2,1,0:T(8,128)(2,1)} %get-tuple-element.133), channel_id=1, source_target_pairs={{0,8},{4,12},{8,0},{12,4},{1,9},{5,13},{9,1},{13,5},{2,10},{6,14},... | collective-permute-start | bytes 786440 | tf_op jit(solution)/shard_map/ppermute | solution.py:82
  129.7 1.2 copy-start.1
  130.9 33.6 %copy-start.3 = (bf16[32,4096]{1,0:T(8,128)(2,1)S(1)}, bf16[32,4096]{1,0:T(8,128)(2,1)}, u32[]{:S(2)}) copy-start(bf16[32,4096]{1,0:T(8,128)(2,1)} %get-tuple-element.125.residual) | copy-start | bytes 786436
  131.5 1.4 collective-permute-start.26
  135.8 9.3 %collective-permute-start.28 = (bf16[32,2048]{1,0:T(8,128)(2,1)S(1)}, bf16[32,2048]{1,0:T(8,128)(2,1)S(1)}, u32[]{:S(2)}, u32[]{:S(2)}) collective-permute-start(bf16[32,2048]{1,0:T(8,128)(2,1)S(1)} %get-tuple-element.139), channel_id=1, source_target_pairs={{0,2},{1,3},{2,0},{3,1},{4,6},{5,7},{6,4},{7,5},{8,10},{9,11},{10,... | collective-permute-start | bytes 393224 | tf_op jit(solution)/shard_map/ppermute | solution.py:82
  138.4 10.5 %collective-permute-start.31 = (bf16[512,1024]{1,0:T(8,128)(2,1)S(1)}, bf16[512,1024]{1,0:T(8,128)(2,1)S(1)}, u32[]{:S(2)}, u32[]{:S(2)}) collective-permute-start(bf16[512,1024]{1,0:T(8,128)(2,1)S(1)} %collective-permute-done.24.far_x), channel_id=1, source_target_pairs={{0,4},{4,0},{8,12},{12,8},{1,5},{5,1},{9,13},{13,9},{2,6},{6,2},{1... | collective-permute-start | bytes 3145736 | tf_op jit(solution)/shard_map/ppermute | solution.py:82
  145.1 3.8 %collective-permute-start.32 = (bf16[512,1024]{1,0:T(8,128)(2,1)}, bf16[512,1024]{1,0:T(8,128)(2,1)S(1)}, u32[]{:S(2)}, u32[]{:S(2)}) collective-permute-start(bf16[512,1024]{1,0:T(8,128)(2,1)} %collective-permute-done.30.far_y), channel_id=1, source_target_pairs={{0,4},{4,0},{8,12},{12,8},{1,5},{5,1},{9,13},{13,9},{2,6},{6,2},{1... | collective-permute-start | bytes 3145736 | tf_op jit(solution)/shard_map/ppermute | solution.py:82
  145.1 10.3 %collective-permute-start.27 = (bf16[32,2048]{1,0:T(8,128)(2,1)S(1)}, bf16[32,2048]{1,0:T(8,128)(2,1)S(1)}, u32[]{:S(2)}, u32[]{:S(2)}) collective-permute-start(bf16[32,2048]{1,0:T(8,128)(2,1)S(1)} %get-tuple-element.138), channel_id=1, source_target_pairs={{0,1},{1,2},{2,3},{3,0},{4,5},{5,6},{6,7},{7,4},{8,9},{9,10},{10,1... | collective-permute-start | bytes 393224 | tf_op jit(solution)/shard_map/ppermute | solution.py:82
  145.8 9.6 %collective-permute-start.29 = (bf16[32,2048]{1,0:T(8,128)(2,1)S(1)}, bf16[32,2048]{1,0:T(8,128)(2,1)S(1)}, u32[]{:S(2)}, u32[]{:S(2)}) collective-permute-start(bf16[32,2048]{1,0:T(8,128)(2,1)S(1)} %get-tuple-element.140), channel_id=1, source_target_pairs={{0,3},{1,0},{2,1},{3,2},{4,7},{5,4},{6,5},{7,6},{8,11},{9,8},{10,9... | collective-permute-start | bytes 393224 | tf_op jit(solution)/shard_map/ppermute | solution.py:82
  151.5 8.3 %collective-permute-start.33 = (bf16[32,2048]{1,0:T(8,128)(2,1)S(1)}, bf16[32,2048]{1,0:T(8,128)(2,1)S(1)}, u32[]{:S(2)}, u32[]{:S(2)}) collective-permute-start(bf16[32,2048]{1,0:T(8,128)(2,1)S(1)} %get-tuple-element.146), channel_id=1, source_target_pairs={{0,1},{1,2},{2,3},{3,0},{4,5},{5,6},{6,7},{7,4},{8,9},{9,10},{10,1... | collective-permute-start | bytes 393224 | tf_op jit(solution)/shard_map/ppermute | solution.py:82
  151.6 12.9 %collective-permute-start.34 = (bf16[32,2048]{1,0:T(8,128)(2,1)S(1)}, bf16[32,2048]{1,0:T(8,128)(2,1)S(1)}, u32[]{:S(2)}, u32[]{:S(2)}) collective-permute-start(bf16[32,2048]{1,0:T(8,128)(2,1)S(1)} %get-tuple-element.147), channel_id=1, source_target_pairs={{0,2},{1,3},{2,0},{3,1},{4,6},{5,7},{6,4},{7,5},{8,10},{9,11},{10,... | collective-permute-start | bytes 393224 | tf_op jit(solution)/shard_map/ppermute | solution.py:82
  154.6 9.8 %collective-permute-start.35 = (bf16[32,2048]{1,0:T(8,128)(2,1)S(1)}, bf16[32,2048]{1,0:T(8,128)(2,1)S(1)}, u32[]{:S(2)}, u32[]{:S(2)}) collective-permute-start(bf16[32,2048]{1,0:T(8,128)(2,1)S(1)} %get-tuple-element.148), channel_id=1, source_target_pairs={{0,3},{1,0},{2,1},{3,2},{4,7},{5,4},{6,5},{7,6},{8,11},{9,8},{10,9... | collective-permute-start | bytes 393224 | tf_op jit(solution)/shard_map/ppermute | solution.py:82
  165.3 6.6 %collective-permute-start.36 = (bf16[32,1024]{1,0:T(8,128)(2,1)S(1)}, bf16[32,1024]{1,0:T(8,128)(2,1)S(1)}, u32[]{:S(2)}, u32[]{:S(2)}) collective-permute-start(bf16[32,1024]{1,0:T(8,128)(2,1)S(1)} %get-tuple-element.150), channel_id=1, source_target_pairs={{0,1},{1,2},{2,3},{3,0},{4,5},{5,6},{6,7},{7,4},{8,9},{9,10},{10,1... | collective-permute-start | bytes 196616 | tf_op jit(solution)/shard_map/ppermute | solution.py:82
  168.3 6.3 %collective-permute-start.37 = (bf16[32,1024]{1,0:T(8,128)(2,1)S(1)}, bf16[32,1024]{1,0:T(8,128)(2,1)S(1)}, u32[]{:S(2)}, u32[]{:S(2)}) collective-permute-start(bf16[32,1024]{1,0:T(8,128)(2,1)S(1)} %get-tuple-element.151), channel_id=1, source_target_pairs={{0,2},{1,3},{2,0},{3,1},{4,6},{5,7},{6,4},{7,5},{8,10},{9,11},{10,... | collective-permute-start | bytes 196616 | tf_op jit(solution)/shard_map/ppermute | solution.py:82
  169.1 5.5 %collective-permute-start.38 = (bf16[32,1024]{1,0:T(8,128)(2,1)S(1)}, bf16[32,1024]{1,0:T(8,128)(2,1)S(1)}, u32[]{:S(2)}, u32[]{:S(2)}) collective-permute-start(bf16[32,1024]{1,0:T(8,128)(2,1)S(1)} %get-tuple-element.152), channel_id=1, source_target_pairs={{0,3},{1,0},{2,1},{3,2},{4,7},{5,4},{6,5},{7,6},{8,11},{9,8},{10,9... | collective-permute-start | bytes 196616 | tf_op jit(solution)/shard_map/ppermute | solution.py:82
  (1 other events, 0.7 us)

commit v6 on v5

--- a/solution.py
+++ b/solution.py
@@ -379,8 +379,9 @@
     given, halves_of = by_core(lookup(ids))
 
     metas = (meta, out_meta, norm_meta, behind, chosen)
-    next_half, tokens, keys_x, sib_tokens, sib_weight, given, later_weight, metas, out_sib = tie(
-        (next_half, tokens, keys_x, sib_tokens, sib_weight, given, later_weight, metas, out_sib)
+    query_half = fetched(0, later_weight)
+    next_half, tokens, keys_x, sib_tokens, sib_weight, given, query_half, metas, out_sib = tie(
+        (next_half, tokens, keys_x, sib_tokens, sib_weight, given, query_half, metas, out_sib)
     )
     meta, out_meta, norm_meta, behind, chosen = metas
     values_x = cross(next_half)
@@ -390,20 +391,16 @@
     mine, given = halves_of(sib(given))
     given = permute(given, "ctx", to_far)
 
-    values_x, tokens, keys_y, sib_tokens, mine, next_half = tie(
-        (values_x, tokens, keys_y, sib_tokens, mine, fetched(0, later_weight))
-    )
-    passed_on, given = tie((tokens[2], given))
+    query_x = cross(query_half)
+    values_x, tokens, keys_y, sib_tokens, mine = tie((values_x, tokens, keys_y, sib_tokens, mine))
     tokens.append(up(tokens[2]))
-    query_x = cross(next_half)
     values_y = swap(values_x)
-    sib_tokens.append(sib(passed_on))
+    sib_tokens.append(sib(tokens[2]))
     embedded = mine + given
-    sib_e = [sib(embedded)]
     out_half = lax.dynamic_slice(out_weight, (grp * depth, 0), (depth, width))
 
-    tokens, query_x, values_y, sib_tokens, embedded, sib_e, out_half = tie(
-        (tokens, query_x, values_y, sib_tokens, embedded, sib_e, out_half)
+    tokens, query_x, values_y, sib_tokens, embedded, out_half = tie(
+        (tokens, query_x, values_y, sib_tokens, embedded, out_half)
     )
     out_x = permute(out_half, "ctx", to_far)
     query_y = swap(query_x)
@@ -460,8 +457,8 @@
         *far_of(2),
     )
 
-    states, rounded, e, sib_e = tie((states, rounded, e, sib_e))
-    sib_e += [sib(array) for array in e[1:]]
+    states, rounded, e = tie((states, rounded, e))
+    sib_e = [sib(array) for array in e]
     states, rounded, out_x, query_y, query_x = tie((states, rounded, out_x, query_y, query_x))
     out_y = swap(out_x)
     others = permute(rounded, "ctx", to_far)

time: 176 us -> 173 us (0.983)
  waiting for transfers between devices: 75.1 us -> 70.2 us
    ppermute x39, waiting for transfers between devices: 75.1 us -> 70.2 us  [permute(): return lax.ppermute(array, axis, pairs)]
  transfers between devices with their start and end apart: 39 -> 39, of which waited for: 20 -> 16; matrix products, arithmetic and copies ran while one was open for 13% -> 15% of each run, Pallas kernels for 19% -> 19%
where the time goes in v6:
time: 173 us
  waiting for transfers between devices  70.2 us (41%)
  starting transfers between devices  38.8 us (22%)
  Pallas kernels  34.8 us (20%)
  local copies, waits for them, and re-layouts  23.4 us (14%)
  other arithmetic  5.4 us (3%)
    ppermute x39, waiting for transfers between devices, permute(): return lax.ppermute(array, axis, pairs)  70.2 us
    ppermute x39, starting transfers between devices, permute(): return lax.ppermute(array, axis, pairs)  38.8 us
    pallas_call x1, Pallas kernels, permuted_plan(): pl.pallas_call(functools.partial(state_kernel, nblocks), out_shape=(jax.S...  17.4 us
    gather x1, local copies, waits for them, and re-layouts, lookup(): jnp.take(embed_table, jnp.clip(offset_ids, 0, embed_table.shape[0] - 1),...  11.4 us
    pallas_call x1, Pallas kernels, permuted_plan(): pl.pallas_call(functools.partial(project_kernel, nhead, steps), out_shape...  9.35 us
    pallas_call x4, Pallas kernels, small_call(): pl.pallas_call(kernel, out_shape=outs, grid_spec=pltpu.PrefetchScalarGrid...  7.51 us
    squeeze x3, local copies, waits for them, and re-layouts, fetched(): lax.dynamic_slice(weight, (k, 0, (core ^ grp) * cols), (1, block, cols))[0]  6.85 us
  transfers between devices with their start and end apart: 39, of which 16 were waited for; matrix products, arithmetic and copies ran while one was open for 15% of the time, Pallas kernels for 19%

profile of v6, /device:TPU:0, one launch (start us, length us, event | category | flops | bytes accessed | tf_op | source)
XLA Modules:
  0.0 172.9 jit_solution(14595700127794840525)
XLA Ops:
  0.0 2.3 %dynamic-slice_bitcast_fusion.2 = bf16[1024,512]{1,0:T(8,128)(2,1)} fusion(bf16[3,1024,1024]{2,1,0:T(8,128)(2,1)} %refs_10_.1, s32[]{:T(128)S(6)} %select_n.115), kind=kLoop, calls=%fused_computation.4 | loop fusion | bytes 2097156 | tf_op jit(solution)/shard_map/squeeze | solution.py:349
  2.8 3.0 %collective-permute-start = (bf16[2,256,1024]{2,1,0:T(8,128)(2,1)}, bf16[2,256,1024]{2,1,0:T(8,128)(2,1)}, u32[]{:S(2)}, u32[]{:S(2)}) collective-permute-start(bf16[2,256,1024]{2,1,0:T(8,128)(2,1)} %refs_0_), channel_id=1, source_target_pairs={{0,1},{1,2},{2,3},{3,0},{4,5},{5,6},{6,7},{7,4},{8,9},{9,10},{10,1... | collective-permute-start | bytes 3145736 | tf_op jit(solution)/shard_map/ppermute | solution.py:82
  5.9 1.5 collective-permute-start.1
  7.4 2.2 %dynamic-slice_bitcast_fusion.1 = bf16[1024,512]{1,0:T(8,128)(2,1)} fusion(bf16[3,1024,1024]{2,1,0:T(8,128)(2,1)} %refs_10_.1, s32[]{:T(128)S(6)} %select_n.115), kind=kLoop, calls=%fused_computation.3 | loop fusion | bytes 2097156 | tf_op jit(solution)/shard_map/squeeze | solution.py:349
  11.2 11.4 %gather_fusion = bf16[512,1024]{1,0:T(8,128)(2,1)} fusion(bf16[8192,1024]{1,0:T(8,128)(2,1)} %param.9, s32[1024]{0:T(1024)S(1)} %pad_clamp_fusion), kind=kCustom, calls=%fused_computation | custom fusion | bytes 2099200 | tf_op jit(solution)/shard_map/jit(_take)/gather | solution.py:326
  22.6 1.6 select_select_fusion
  24.2 0.9 constant_dynamic-slice_fusion.3
  25.1 0.9 copy.14
  27.0 2.3 %dynamic-slice_bitcast_fusion = bf16[1024,512]{1,0:T(8,128)(2,1)} fusion(bf16[3,1024,1024]{2,1,0:T(8,128)(2,1)} %refs_10_.1, s32[]{:T(128)S(6)} %select_n.115), kind=kLoop, calls=%fused_computation.1 | loop fusion | bytes 2097156 | tf_op jit(solution)/shard_map/squeeze | solution.py:349
  29.3 2.2 %collective-permute-done.refs_1_ = bf16[2,256,1024]{2,1,0:T(8,128)(2,1)} collective-permute-done((bf16[2,256,1024]{2,1,0:T(8,128)(2,1)}, bf16[2,256,1024]{2,1,0:T(8,128)(2,1)}, u32[]{:S(2)}, u32[]{:S(2)}) %collective-permute-start) | collective-permute-done | bytes 1048608 | tf_op jit(solution)/shard_map/ppermute | solution.py:82
  31.7 1.6 collective-permute-start.5
  33.2 1.6 collective-permute-start.6
  34.8 0.8 collective-permute-start.7
  36.2 3.2 %collective-permute-done.9 = bf16[4,2,32,1024]{3,2,0,1:T(8,128)(2,1)} collective-permute-done((bf16[4,2,32,1024]{3,2,0,1:T(8,128)(2,1)}, bf16[4,2,32,1024]{3,2,0,1:T(8,128)(2,1)}, u32[]{:S(2)}, u32[]{:S(2)}) %collective-permute-start.9) | collective-permute-done | bytes 524320 | tf_op jit(solution)/shard_map/ppermute | solution.py:82
  39.9 1.3 bitcast_add_fusion
  41.9 16.2 %collective-permute-done.5.refs_14_.refs_18_ = bf16[1024,512]{1,0:T(8,128)(2,1)} collective-permute-done((bf16[1024,512]{1,0:T(8,128)(2,1)}, bf16[1024,512]{1,0:T(8,128)(2,1)}, u32[]{:S(2)}, u32[]{:S(2)}) %collective-permute-start.5) | collective-permute-done | bytes 1048608 | tf_op jit(solution)/shard_map/ppermute | solution.py:82
  58.1 1.9 %collective-permute-done.6.refs_2_ = bf16[2,256,1024]{2,1,0:T(8,128)(2,1)} collective-permute-done((bf16[2,256,1024]{2,1,0:T(8,128)(2,1)}, bf16[2,256,1024]{2,1,0:T(8,128)(2,1)}, u32[]{:S(2)}, u32[]{:S(2)}) %collective-permute-start.6) | collective-permute-done | bytes 1048608 | tf_op jit(solution)/shard_map/ppermute | solution.py:82
  60.7 1.4 collective-permute-start.12
  62.8 22.3 %collective-permute-done.14 = bf16[128,1024]{1,0:T(8,128)(2,1)} collective-permute-done((bf16[128,1024]{1,0:T(8,128)(2,1)S(1)}, bf16[128,1024]{1,0:T(8,128)(2,1)}, u32[]{:S(2)}, u32[]{:S(2)}) %collective-permute-start.14) | collective-permute-done | bytes 262176 | tf_op jit(solution)/shard_map/ppermute | solution.py:82
  85.0 1.1 add.105.refs_0_
  86.3 2.6 %collective-permute-start.23 = (bf16[1024,512]{1,0:T(8,128)(2,1)}, bf16[1024,512]{1,0:T(8,128)(2,1)S(1)}, u32[]{:S(2)}, u32[]{:S(2)}) collective-permute-start(bf16[1024,512]{1,0:T(8,128)(2,1)} %collective-permute-done.11.refs_14_), channel_id=1, source_target_pairs={{0,16},{16,0},{1,17},{17,1},{2,18},{18,2},{3,19},{19,3},{4,20},{20... | collective-permute-start | bytes 3145736 | tf_op jit(solution)/shard_map/ppermute | solution.py:82
  88.9 0.9 collective-permute-start.24
  89.8 0.9 collective-permute-start.16
  90.7 1.4 collective-permute-start.17
  92.1 2.6 %collective-permute-start.18 = (bf16[128,1024]{1,0:T(8,128)(2,1)S(1)}, bf16[128,1024]{1,0:T(8,128)(2,1)}, u32[]{:S(2)}, u32[]{:S(2)}) collective-permute-start(bf16[128,1024]{1,0:T(8,128)(2,1)S(1)} %add.105.refs_0_), channel_id=1, source_target_pairs={{0,3},{1,0},{2,1},{3,2},{4,7},{5,4},{6,5},{7,6},{8,11},{9,8},{10,9... | collective-permute-start | bytes 786440 | tf_op jit(solution)/shard_map/ppermute | solution.py:82
  94.7 17.4 %prompt_state.1 = (f32[2,4,128,128]{3,2,1,0:T(8,128)}, bf16[2,4,128,128]{3,2,1,0:T(8,128)(2,1)}) custom-call(s32[7]{0:T(128)} %stack.74.meta, bf16[2,256,1024]{2,1,0:T(8,128)(2,1)} %refs_0_, bf16[2,256,1024]{2,1,0:T(8,128)(2,1)} %collective-permute-done.refs_1_, bf16[2,256,1024]{2,1,0:T(8,128)(2,1)} %collective-permute-done.6.refs_2_, ...), custom_call_target="tpu_custom_call" | custom-call | flops 8589934592 | bytes 16777216 | tf_op jit(solution)/shard_map/prompt_state/pallas_call | solution.py:425
  112.8 1.3 collective-permute-done.24.far_x
  115.8 0.8 collective-permute-done.19.refs_4_
  116.6 0.9 collective-permute-start.25
  117.6 9.4 %response_rows.1 = (f32[256,1024]{1,0:T(8,128)}, bf16[32,4096]{1,0:T(8,128)(2,1)}) custom-call(s32[7]{0:T(128)} %stack.74.meta, bf16[128,1024]{1,0:T(8,128)(2,1)} %copy-done.5, bf16[128,1024]{1,0:T(8,128)(2,1)} %collective-permute-done.16.refs_1_, bf16[128,1024]{1,0:T(8,128)(2,1)} %collective-permute-done.17.refs_2_, ...), custom_call_target="tpu_custom_call" | custom-call | flops 3221225472 | bytes 14680064 | tf_op jit(solution)/shard_map/response_rows/pallas_call | solution.py:470
  127.0 1.2 copy-done.1
  128.9 1.2 collective-permute-done.26.heads_sib
  130.2 2.9 %near_terms.1 = (f32[32,2048]{1,0:T(8,128)S(1)}, bf16[32,2048]{1,0:T(8,128)(2,1)S(1)}, bf16[32,2048]{1,0:T(8,128)(2,1)S(1)}, bf16[32,2048]{1,0:T(8,128)(2,1)S(1)}) custom-call(s32[6]{0:T(128)S(1)} %stack.79.meta, bf16[128,512]{1,0:T(8,128)(2,1)S(1)} %get-tuple-element.132.heads_own, bf16[128,512]{1,0:T(8,128)(2,1)S(1)} %collective-permute-done.26.heads_sib, ...), custom_call_target="tpu_custom_call" | custom-call | flops 536870912 | bytes 4194304 | tf_op jit(solution)/shard_map/near_terms/pallas_call | solution.py:290
  133.1 2.1 %collective-permute-start.28 = (bf16[32,2048]{1,0:T(8,128)(2,1)S(1)}, bf16[32,2048]{1,0:T(8,128)(2,1)S(1)}, u32[]{:S(2)}, u32[]{:S(2)}) collective-permute-start(bf16[32,2048]{1,0:T(8,128)(2,1)S(1)} %get-tuple-element.129), channel_id=1, source_target_pairs={{0,2},{1,3},{2,0},{3,1},{4,6},{5,7},{6,4},{7,5},{8,10},{9,11},{10,... | collective-permute-start | bytes 393224 | tf_op jit(solution)/shard_map/ppermute | solution.py:82
  135.1 7.2 %collective-permute-done.28.refs_2_ = bf16[32,2048]{1,0:T(8,128)(2,1)S(1)} collective-permute-done((bf16[32,2048]{1,0:T(8,128)(2,1)S(1)}, bf16[32,2048]{1,0:T(8,128)(2,1)S(1)}, u32[]{:S(2)}, u32[]{:S(2)}) %collective-permute-start.28) | collective-permute-done | bytes 131104 | tf_op jit(solution)/shard_map/ppermute | solution.py:82
  142.7 3.5 %collective-permute-start.29 = (bf16[32,2048]{1,0:T(8,128)(2,1)S(1)}, bf16[32,2048]{1,0:T(8,128)(2,1)S(1)}, u32[]{:S(2)}, u32[]{:S(2)}) collective-permute-start(bf16[32,2048]{1,0:T(8,128)(2,1)S(1)} %get-tuple-element.130), channel_id=1, source_target_pairs={{0,3},{1,0},{2,1},{3,2},{4,7},{5,4},{6,5},{7,6},{8,11},{9,8},{10,9... | collective-permute-start | bytes 393224 | tf_op jit(solution)/shard_map/ppermute | solution.py:82
  146.2 2.5 %far_terms.1 = (f32[32,2048]{1,0:T(8,128)S(1)}, bf16[32,2048]{1,0:T(8,128)(2,1)S(1)}, bf16[32,2048]{1,0:T(8,128)(2,1)S(1)}, bf16[32,2048]{1,0:T(8,128)(2,1)S(1)}) custom-call(s32[6]{0:T(128)S(1)} %stack.79.meta, bf16[128,512]{1,0:T(8,128)(2,1)S(1)} %get-tuple-element.132.heads_own, bf16[128,512]{1,0:T(8,128)(2,1)S(1)} %collective-permute-done.26.heads_sib, ...), custom_call_target="tpu_custom_call" | custom-call | flops 536870912 | bytes 4194304 | tf_op jit(solution)/shard_map/far_terms/pallas_call | solution.py:290
  148.8 2.5 %collective-permute-start.34 = (bf16[32,2048]{1,0:T(8,128)(2,1)S(1)}, bf16[32,2048]{1,0:T(8,128)(2,1)S(1)}, u32[]{:S(2)}, u32[]{:S(2)}) collective-permute-start(bf16[32,2048]{1,0:T(8,128)(2,1)S(1)} %get-tuple-element.137), channel_id=1, source_target_pairs={{0,2},{1,3},{2,0},{3,1},{4,6},{5,7},{6,4},{7,5},{8,10},{9,11},{10,... | collective-permute-start | bytes 393224 | tf_op jit(solution)/shard_map/ppermute | solution.py:82
  151.3 1.3 collective-permute-start.35
  152.7 4.4 %collective-permute-done.33.refs_5_ = bf16[32,2048]{1,0:T(8,128)(2,1)S(1)} collective-permute-done((bf16[32,2048]{1,0:T(8,128)(2,1)S(1)}, bf16[32,2048]{1,0:T(8,128)(2,1)S(1)}, u32[]{:S(2)}, u32[]{:S(2)}) %collective-permute-start.33) | collective-permute-done | bytes 131104 | tf_op jit(solution)/shard_map/ppermute | solution.py:82
  157.1 4.6 %collective-permute-done.34.refs_6_ = bf16[32,2048]{1,0:T(8,128)(2,1)S(1)} collective-permute-done((bf16[32,2048]{1,0:T(8,128)(2,1)S(1)}, bf16[32,2048]{1,0:T(8,128)(2,1)S(1)}, u32[]{:S(2)}, u32[]{:S(2)}) %collective-permute-start.34) | collective-permute-done | bytes 131104 | tf_op jit(solution)/shard_map/ppermute | solution.py:82
  161.7 0.8 final_norm.1
  162.5 2.7 %collective-permute-start.36 = (bf16[32,1024]{1,0:T(8,128)(2,1)S(1)}, bf16[32,1024]{1,0:T(8,128)(2,1)S(1)}, u32[]{:S(2)}, u32[]{:S(2)}) collective-permute-start(bf16[32,1024]{1,0:T(8,128)(2,1)S(1)} %get-tuple-element.140), channel_id=1, source_target_pairs={{0,1},{1,2},{2,3},{3,0},{4,5},{5,6},{6,7},{7,4},{8,9},{9,10},{10,1... | collective-permute-start | bytes 196616 | tf_op jit(solution)/shard_map/ppermute | solution.py:82
  165.2 1.1 collective-permute-start.37
  166.4 1.3 collective-permute-start.38
  167.7 1.5 collective-permute-done.36.refs_1_
  169.2 2.4 %collective-permute-done.37.refs_2_ = bf16[32,1024]{1,0:T(8,128)(2,1)S(1)} collective-permute-done((bf16[32,1024]{1,0:T(8,128)(2,1)S(1)}, bf16[32,1024]{1,0:T(8,128)(2,1)S(1)}, u32[]{:S(2)}, u32[]{:S(2)}) %collective-permute-start.37) | collective-permute-done | bytes 65568 | tf_op jit(solution)/shard_map/ppermute | solution.py:82
  171.6 1.3 place.1
  (81 shorter events, 10.1 us)
Async XLA Ops:
  2.3 29.3 %collective-permute-start.3 = (bf16[3,1024,1024]{2,1,0:T(8,128)(2,1)}, bf16[3,1024,1024]{2,1,0:T(8,128)(2,1)}, u32[]{:S(2)}, u32[]{:S(2)}) collective-permute-start(bf16[3,1024,1024]{2,1,0:T(8,128)(2,1)} %refs_10_.1), channel_id=1, source_target_pairs={{0,4},{4,0},{8,12},{12,8},{1,5},{5,1},{9,13},{13,9},{2,6},{6,2},{1... | collective-permute-start | bytes 18874376 | tf_op jit(solution)/shard_map/ppermute | solution.py:82
  2.8 28.9 %collective-permute-start.4 = (bf16[1024,1024]{1,0:T(8,128)(2,1)}, bf16[1024,1024]{1,0:T(8,128)(2,1)}, u32[]{:S(2)}, u32[]{:S(2)}) collective-permute-start(bf16[1024,1024]{1,0:T(8,128)(2,1)} %own.1), channel_id=1, source_target_pairs={{0,4},{4,0},{8,12},{12,8},{1,5},{5,1},{9,13},{13,9},{2,6},{6,2},{1... | collective-permute-start | bytes 6291464 | tf_op jit(solution)/shard_map/ppermute | solution.py:82
  2.8 28.7 %collective-permute-start = (bf16[2,256,1024]{2,1,0:T(8,128)(2,1)}, bf16[2,256,1024]{2,1,0:T(8,128)(2,1)}, u32[]{:S(2)}, u32[]{:S(2)}) collective-permute-start(bf16[2,256,1024]{2,1,0:T(8,128)(2,1)} %refs_0_), channel_id=1, source_target_pairs={{0,1},{1,2},{2,3},{3,0},{4,5},{5,6},{6,7},{7,4},{8,9},{9,10},{10,1... | collective-permute-start | bytes 3145736 | tf_op jit(solution)/shard_map/ppermute | solution.py:82
  5.9 25.8 %collective-permute-start.2 = (bf16[2,256,1024]{2,1,0:T(8,128)(2,1)}, bf16[2,256,1024]{2,1,0:T(8,128)(2,1)}, u32[]{:S(2)}, u32[]{:S(2)}) collective-permute-start(bf16[2,256,1024]{2,1,0:T(8,128)(2,1)} %refs_0_), channel_id=1, source_target_pairs={{0,4},{4,0},{8,12},{12,8},{1,5},{5,1},{9,13},{13,9},{2,6},{6,2},{1... | collective-permute-start | bytes 3145736 | tf_op jit(solution)/shard_map/ppermute | solution.py:82
  5.9 25.8 %collective-permute-start.1 = (bf16[1024,512]{1,0:T(8,128)(2,1)}, bf16[1024,512]{1,0:T(8,128)(2,1)S(1)}, u32[]{:S(2)}, u32[]{:S(2)}) collective-permute-start(bf16[1024,512]{1,0:T(8,128)(2,1)} %dynamic-slice_bitcast_fusion.2), channel_id=1, source_target_pairs={{0,8},{4,12},{8,0},{12,4},{16,28},{20,24},{24,20},{28,16},{1,9},{5... | collective-permute-start | bytes 3145736 | tf_op jit(solution)/shard_map/ppermute | solution.py:82
  11.2 14.8 %copy-start.8 = (s32[128]{0:T(128)S(1)}, s32[128]{0:T(128)}, u32[]{:S(2)}) copy-start(s32[128]{0:T(128)} %param.11) | copy-start | bytes 1540
  22.6 40.1 %copy-start = (bf16[1024,1024]{1,0:T(8,128)(2,1)S(1)}, bf16[1024,1024]{1,0:T(8,128)(2,1)}, u32[]{:S(2)}) copy-start(bf16[1024,1024]{1,0:T(8,128)(2,1)} %own.1) | copy-start | bytes 6291460
  31.7 54.6 %copy-start.4 = (bf16[1024,512]{1,0:T(8,128)(2,1)}, bf16[1024,512]{1,0:T(8,128)(2,1)S(1)}, u32[]{:S(2)}) copy-start(bf16[1024,512]{1,0:T(8,128)(2,1)S(1)} %collective-permute-done.1.refs_12_.refs_16_) | copy-start | bytes 3145732
  31.7 26.4 %collective-permute-start.5 = (bf16[1024,512]{1,0:T(8,128)(2,1)}, bf16[1024,512]{1,0:T(8,128)(2,1)}, u32[]{:S(2)}, u32[]{:S(2)}) collective-permute-start(bf16[1024,512]{1,0:T(8,128)(2,1)} %dynamic-slice_bitcast_fusion.1), channel_id=1, source_target_pairs={{0,8},{4,12},{8,0},{12,4},{16,28},{20,24},{24,20},{28,16},{1,9},{5... | collective-permute-start | bytes 3145736 | tf_op jit(solution)/shard_map/ppermute | solution.py:82
  33.2 26.7 %collective-permute-start.6 = (bf16[2,256,1024]{2,1,0:T(8,128)(2,1)}, bf16[2,256,1024]{2,1,0:T(8,128)(2,1)}, u32[]{:S(2)}, u32[]{:S(2)}) collective-permute-start(bf16[2,256,1024]{2,1,0:T(8,128)(2,1)} %collective-permute-done.refs_1_), channel_id=1, source_target_pairs={{0,1},{1,2},{2,3},{3,0},{4,5},{5,6},{6,7},{7,4},{8,9},{9,10},{10,1... | collective-permute-start | bytes 3145736 | tf_op jit(solution)/shard_map/ppermute | solution.py:82
  34.8 25.2 %collective-permute-start.7 = (bf16[1024,512]{1,0:T(8,128)(2,1)S(1)}, bf16[1024,512]{1,0:T(8,128)(2,1)}, u32[]{:S(2)}, u32[]{:S(2)}) collective-permute-start(bf16[1024,512]{1,0:T(8,128)(2,1)S(1)} %collective-permute-done.1.refs_12_.refs_16_), channel_id=1, source_target_pairs={{0,16},{16,0},{1,17},{17,1},{2,18},{18,2},{3,19},{19,3},{4,20},{20... | collective-permute-start | bytes 3145736 | tf_op jit(solution)/shard_map/ppermute | solution.py:82
  35.6 24.3 %collective-permute-start.8 = (bf16[2,256,1024]{2,1,0:T(8,128)(2,1)}, bf16[2,256,1024]{2,1,0:T(8,128)(2,1)}, u32[]{:S(2)}, u32[]{:S(2)}) collective-permute-start(bf16[2,256,1024]{2,1,0:T(8,128)(2,1)} %collective-permute-done.refs_1_), channel_id=1, source_target_pairs={{0,4},{4,0},{8,12},{12,8},{1,5},{5,1},{9,13},{13,9},{2,6},{6,2},{1... | collective-permute-start | bytes 3145736 | tf_op jit(solution)/shard_map/ppermute | solution.py:82
  35.6 3.7 %collective-permute-start.9 = (bf16[4,2,32,1024]{3,2,0,1:T(8,128)(2,1)}, bf16[4,2,32,1024]{3,2,0,1:T(8,128)(2,1)}, u32[]{:S(2)}, u32[]{:S(2)}) collective-permute-start(bf16[4,2,32,1024]{3,2,0,1:T(8,128)(2,1)} %bitcast.37), channel_id=1, source_target_pairs={{0,4},{4,0},{8,12},{12,8},{1,5},{5,1},{9,13},{13,9},{2,6},{6,2},{1... | collective-permute-start | bytes 1572872 | tf_op jit(solution)/shard_map/ppermute | solution.py:82
  39.4 46.8 %collective-permute-start.11 = (bf16[1024,512]{1,0:T(8,128)(2,1)}, bf16[1024,512]{1,0:T(8,128)(2,1)}, u32[]{:S(2)}, u32[]{:S(2)}) collective-permute-start(bf16[1024,512]{1,0:T(8,128)(2,1)} %dynamic-slice_bitcast_fusion), channel_id=1, source_target_pairs={{0,8},{4,12},{8,0},{12,4},{16,28},{20,24},{24,20},{28,16},{1,9},{5... | collective-permute-start | bytes 3145736 | tf_op jit(solution)/shard_map/ppermute | solution.py:82
  60.0 26.2 %collective-permute-start.10 = (bf16[2,256,1024]{2,1,0:T(8,128)(2,1)}, bf16[2,256,1024]{2,1,0:T(8,128)(2,1)}, u32[]{:S(2)}, u32[]{:S(2)}) collective-permute-start(bf16[2,256,1024]{2,1,0:T(8,128)(2,1)} %collective-permute-done.6.refs_2_), channel_id=1, source_target_pairs={{0,1},{1,2},{2,3},{3,0},{4,5},{5,6},{6,7},{7,4},{8,9},{9,10},{10,1... | collective-permute-start | bytes 3145736 | tf_op jit(solution)/shard_map/ppermute | solution.py:82
  60.7 25.4 %collective-permute-start.12 = (bf16[1024,512]{1,0:T(8,128)(2,1)}, bf16[1024,512]{1,0:T(8,128)(2,1)}, u32[]{:S(2)}, u32[]{:S(2)}) collective-permute-start(bf16[1024,512]{1,0:T(8,128)(2,1)} %collective-permute-done.5.refs_14_.refs_18_), channel_id=1, source_target_pairs={{0,16},{16,0},{1,17},{17,1},{2,18},{18,2},{3,19},{19,3},{4,20},{20... | collective-permute-start | bytes 3145736 | tf_op jit(solution)/shard_map/ppermute | solution.py:82
  62.2 24.0 %collective-permute-start.13 = (bf16[2,256,1024]{2,1,0:T(8,128)(2,1)}, bf16[2,256,1024]{2,1,0:T(8,128)(2,1)}, u32[]{:S(2)}, u32[]{:S(2)}) collective-permute-start(bf16[2,256,1024]{2,1,0:T(8,128)(2,1)} %collective-permute-done.6.refs_2_), channel_id=1, source_target_pairs={{0,4},{4,0},{8,12},{12,8},{1,5},{5,1},{9,13},{13,9},{2,6},{6,2},{1... | collective-permute-start | bytes 3145736 | tf_op jit(solution)/shard_map/ppermute | solution.py:82
  62.2 22.9 %collective-permute-start.14 = (bf16[128,1024]{1,0:T(8,128)(2,1)S(1)}, bf16[128,1024]{1,0:T(8,128)(2,1)}, u32[]{:S(2)}, u32[]{:S(2)}) collective-permute-start(bf16[128,1024]{1,0:T(8,128)(2,1)S(1)} %bitcast.38), channel_id=1, source_target_pairs={{0,8},{4,12},{8,0},{12,4},{1,9},{5,13},{9,1},{13,5},{2,10},{6,14},... | collective-permute-start | bytes 786440 | tf_op jit(solution)/shard_map/ppermute | solution.py:82
  86.1 28.5 %copy-start.5 = (bf16[128,1024]{1,0:T(8,128)(2,1)}, bf16[128,1024]{1,0:T(8,128)(2,1)S(1)}, u32[]{:S(2)}) copy-start(bf16[128,1024]{1,0:T(8,128)(2,1)S(1)} %add.105.refs_0_) | copy-start | bytes 786436
  86.2 5.9 %collective-permute-start.15 = (bf16[2,256,1024]{2,1,0:T(8,128)(2,1)}, bf16[2,256,1024]{2,1,0:T(8,128)(2,1)S(1)}, u32[]{:S(2)}, u32[]{:S(2)}) collective-permute-start(bf16[2,256,1024]{2,1,0:T(8,128)(2,1)} %collective-permute-done.10.refs_3_), channel_id=1, source_target_pairs={{0,4},{4,0},{8,12},{12,8},{1,5},{5,1},{9,13},{13,9},{2,6},{6,2},{1... | collective-permute-start | bytes 3145736 | tf_op jit(solution)/shard_map/ppermute | solution.py:82
  86.3 26.6 %collective-permute-start.23 = (bf16[1024,512]{1,0:T(8,128)(2,1)}, bf16[1024,512]{1,0:T(8,128)(2,1)S(1)}, u32[]{:S(2)}, u32[]{:S(2)}) collective-permute-start(bf16[1024,512]{1,0:T(8,128)(2,1)} %collective-permute-done.11.refs_14_), channel_id=1, source_target_pairs={{0,16},{16,0},{1,17},{17,1},{2,18},{18,2},{3,19},{19,3},{4,20},{20... | collective-permute-start | bytes 3145736 | tf_op jit(solution)/shard_map/ppermute | solution.py:82
  88.9 25.2 %collective-permute-start.24 = (bf16[512,1024]{1,0:T(8,128)(2,1)S(1)}, bf16[512,1024]{1,0:T(8,128)(2,1)S(1)}, u32[]{:S(2)}, u32[]{:S(2)}) collective-permute-start(bf16[512,1024]{1,0:T(8,128)(2,1)S(1)} %constant_dynamic-slice_fusion), channel_id=1, source_target_pairs={{0,8},{4,12},{8,0},{12,4},{1,9},{5,13},{9,1},{13,5},{2,10},{6,14},... | collective-permute-start | bytes 3145736 | tf_op jit(solution)/shard_map/ppermute | solution.py:82
  89.8 22.3 %collective-permute-start.16 = (bf16[128,1024]{1,0:T(8,128)(2,1)S(1)}, bf16[128,1024]{1,0:T(8,128)(2,1)}, u32[]{:S(2)}, u32[]{:S(2)}) collective-permute-start(bf16[128,1024]{1,0:T(8,128)(2,1)S(1)} %add.105.refs_0_), channel_id=1, source_target_pairs={{0,1},{1,2},{2,3},{3,0},{4,5},{5,6},{6,7},{7,4},{8,9},{9,10},{10,1... | collective-permute-start | bytes 786440 | tf_op jit(solution)/shard_map/ppermute | solution.py:82
  90.7 21.4 %collective-permute-start.17 = (bf16[128,1024]{1,0:T(8,128)(2,1)S(1)}, bf16[128,1024]{1,0:T(8,128)(2,1)}, u32[]{:S(2)}, u32[]{:S(2)}) collective-permute-start(bf16[128,1024]{1,0:T(8,128)(2,1)S(1)} %add.105.refs_0_), channel_id=1, source_target_pairs={{0,2},{1,3},{2,0},{3,1},{4,6},{5,7},{6,4},{7,5},{8,10},{9,11},{10,... | collective-permute-start | bytes 786440 | tf_op jit(solution)/shard_map/ppermute | solution.py:82
  92.1 2.6 %copy-start.7 = (bf16[2,256,1024]{2,1,0:T(8,128)(2,1)}, bf16[2,256,1024]{2,1,0:T(8,128)(2,1)S(1)}, u32[]{:S(2)}) copy-start(bf16[2,256,1024]{2,1,0:T(8,128)(2,1)S(1)} %collective-permute-done.15.refs_7_) | copy-start | bytes 3145732
  92.1 20.0 %collective-permute-start.18 = (bf16[128,1024]{1,0:T(8,128)(2,1)S(1)}, bf16[128,1024]{1,0:T(8,128)(2,1)}, u32[]{:S(2)}, u32[]{:S(2)}) collective-permute-start(bf16[128,1024]{1,0:T(8,128)(2,1)S(1)} %add.105.refs_0_), channel_id=1, source_target_pairs={{0,3},{1,0},{2,1},{3,2},{4,7},{5,4},{6,5},{7,6},{8,11},{9,8},{10,9... | collective-permute-start | bytes 786440 | tf_op jit(solution)/shard_map/ppermute | solution.py:82
  112.8 2.3 %copy-start.6 = (bf16[1024,512]{1,0:T(8,128)(2,1)}, bf16[1024,512]{1,0:T(8,128)(2,1)S(1)}, u32[]{:S(2)}) copy-start(bf16[1024,512]{1,0:T(8,128)(2,1)S(1)} %collective-permute-done.23.refs_15_) | copy-start | bytes 3145732
  114.1 28.3 %collective-permute-start.30 = (bf16[512,1024]{1,0:T(8,128)(2,1)S(1)}, bf16[512,1024]{1,0:T(8,128)(2,1)}, u32[]{:S(2)}, u32[]{:S(2)}) collective-permute-start(bf16[512,1024]{1,0:T(8,128)(2,1)S(1)} %collective-permute-done.24.far_x), channel_id=1, source_target_pairs={{0,16},{16,0},{1,17},{17,1},{2,18},{18,2},{3,19},{19,3},{4,20},{20... | collective-permute-start | bytes 3145736 | tf_op jit(solution)/shard_map/ppermute | solution.py:82
  114.6 2.0 %collective-permute-start.19 = (bf16[128,1024]{1,0:T(8,128)(2,1)S(1)}, bf16[128,1024]{1,0:T(8,128)(2,1)}, u32[]{:S(2)}, u32[]{:S(2)}) collective-permute-start(bf16[128,1024]{1,0:T(8,128)(2,1)S(1)} %add.105.refs_0_), channel_id=1, source_target_pairs={{0,4},{4,0},{8,12},{12,8},{1,5},{5,1},{9,13},{13,9},{2,6},{6,2},{1... | collective-permute-start | bytes 786440 | tf_op jit(solution)/shard_map/ppermute | solution.py:82
  114.6 2.9 %collective-permute-start.20 = (bf16[128,1024]{1,0:T(8,128)(2,1)}, bf16[128,1024]{1,0:T(8,128)(2,1)}, u32[]{:S(2)}, u32[]{:S(2)}) collective-permute-start(bf16[128,1024]{1,0:T(8,128)(2,1)} %collective-permute-done.16.refs_1_), channel_id=1, source_target_pairs={{0,4},{4,0},{8,12},{12,8},{1,5},{5,1},{9,13},{13,9},{2,6},{6,2},{1... | collective-permute-start | bytes 786440 | tf_op jit(solution)/shard_map/ppermute | solution.py:82
  115.1 2.4 %collective-permute-start.21 = (bf16[128,1024]{1,0:T(8,128)(2,1)}, bf16[128,1024]{1,0:T(8,128)(2,1)}, u32[]{:S(2)}, u32[]{:S(2)}) collective-permute-start(bf16[128,1024]{1,0:T(8,128)(2,1)} %collective-permute-done.17.refs_2_), channel_id=1, source_target_pairs={{0,4},{4,0},{8,12},{12,8},{1,5},{5,1},{9,13},{13,9},{2,6},{6,2},{1... | collective-permute-start | bytes 786440 | tf_op jit(solution)/shard_map/ppermute | solution.py:82
  115.1 2.5 %collective-permute-start.22 = (bf16[128,1024]{1,0:T(8,128)(2,1)}, bf16[128,1024]{1,0:T(8,128)(2,1)}, u32[]{:S(2)}, u32[]{:S(2)}) collective-permute-start(bf16[128,1024]{1,0:T(8,128)(2,1)} %collective-permute-done.18.refs_3_), channel_id=1, source_target_pairs={{0,4},{4,0},{8,12},{12,8},{1,5},{5,1},{9,13},{13,9},{2,6},{6,2},{1... | collective-permute-start | bytes 786440 | tf_op jit(solution)/shard_map/ppermute | solution.py:82
  115.8 11.2 %copy-start.2 = (f32[2,4,128,128]{3,2,1,0:T(8,128)S(1)}, f32[2,4,128,128]{3,2,1,0:T(8,128)}, u32[]{:S(2)}) copy-start(f32[2,4,128,128]{3,2,1,0:T(8,128)} %get-tuple-element.122.states) | copy-start | bytes 1572868
  116.6 10.4 %collective-permute-start.25 = (bf16[2,4,128,128]{3,2,1,0:T(8,128)(2,1)}, bf16[2,4,128,128]{3,2,1,0:T(8,128)(2,1)S(1)}, u32[]{:S(2)}, u32[]{:S(2)}) collective-permute-start(bf16[2,4,128,128]{3,2,1,0:T(8,128)(2,1)} %get-tuple-element.123), channel_id=1, source_target_pairs={{0,8},{4,12},{8,0},{12,4},{1,9},{5,13},{9,1},{13,5},{2,10},{6,14},... | collective-permute-start | bytes 786440 | tf_op jit(solution)/shard_map/ppermute | solution.py:82
  127.0 1.2 copy-start.1
  128.2 33.5 %copy-start.3 = (bf16[32,4096]{1,0:T(8,128)(2,1)S(1)}, bf16[32,4096]{1,0:T(8,128)(2,1)}, u32[]{:S(2)}) copy-start(bf16[32,4096]{1,0:T(8,128)(2,1)} %get-tuple-element.115.residual) | copy-start | bytes 786436
  128.7 1.4 collective-permute-start.26
  133.1 9.3 %collective-permute-start.28 = (bf16[32,2048]{1,0:T(8,128)(2,1)S(1)}, bf16[32,2048]{1,0:T(8,128)(2,1)S(1)}, u32[]{:S(2)}, u32[]{:S(2)}) collective-permute-start(bf16[32,2048]{1,0:T(8,128)(2,1)S(1)} %get-tuple-element.129), channel_id=1, source_target_pairs={{0,2},{1,3},{2,0},{3,1},{4,6},{5,7},{6,4},{7,5},{8,10},{9,11},{10,... | collective-permute-start | bytes 393224 | tf_op jit(solution)/shard_map/ppermute | solution.py:82
  135.1 11.1 %collective-permute-start.31 = (bf16[512,1024]{1,0:T(8,128)(2,1)S(1)}, bf16[512,1024]{1,0:T(8,128)(2,1)S(1)}, u32[]{:S(2)}, u32[]{:S(2)}) collective-permute-start(bf16[512,1024]{1,0:T(8,128)(2,1)S(1)} %collective-permute-done.24.far_x), channel_id=1, source_target_pairs={{0,4},{4,0},{8,12},{12,8},{1,5},{5,1},{9,13},{13,9},{2,6},{6,2},{1... | collective-permute-start | bytes 3145736 | tf_op jit(solution)/shard_map/ppermute | solution.py:82
  142.4 3.8 %collective-permute-start.32 = (bf16[512,1024]{1,0:T(8,128)(2,1)}, bf16[512,1024]{1,0:T(8,128)(2,1)S(1)}, u32[]{:S(2)}, u32[]{:S(2)}) collective-permute-start(bf16[512,1024]{1,0:T(8,128)(2,1)} %collective-permute-done.30.far_y), channel_id=1, source_target_pairs={{0,4},{4,0},{8,12},{12,8},{1,5},{5,1},{9,13},{13,9},{2,6},{6,2},{1... | collective-permute-start | bytes 3145736 | tf_op jit(solution)/shard_map/ppermute | solution.py:82
  142.4 10.3 %collective-permute-start.27 = (bf16[32,2048]{1,0:T(8,128)(2,1)S(1)}, bf16[32,2048]{1,0:T(8,128)(2,1)S(1)}, u32[]{:S(2)}, u32[]{:S(2)}) collective-permute-start(bf16[32,2048]{1,0:T(8,128)(2,1)S(1)} %get-tuple-element.128), channel_id=1, source_target_pairs={{0,1},{1,2},{2,3},{3,0},{4,5},{5,6},{6,7},{7,4},{8,9},{9,10},{10,1... | collective-permute-start | bytes 393224 | tf_op jit(solution)/shard_map/ppermute | solution.py:82
  142.7 10.0 %collective-permute-start.29 = (bf16[32,2048]{1,0:T(8,128)(2,1)S(1)}, bf16[32,2048]{1,0:T(8,128)(2,1)S(1)}, u32[]{:S(2)}, u32[]{:S(2)}) collective-permute-start(bf16[32,2048]{1,0:T(8,128)(2,1)S(1)} %get-tuple-element.130), channel_id=1, source_target_pairs={{0,3},{1,0},{2,1},{3,2},{4,7},{5,4},{6,5},{7,6},{8,11},{9,8},{10,9... | collective-permute-start | bytes 393224 | tf_op jit(solution)/shard_map/ppermute | solution.py:82
  148.8 8.3 %collective-permute-start.33 = (bf16[32,2048]{1,0:T(8,128)(2,1)S(1)}, bf16[32,2048]{1,0:T(8,128)(2,1)S(1)}, u32[]{:S(2)}, u32[]{:S(2)}) collective-permute-start(bf16[32,2048]{1,0:T(8,128)(2,1)S(1)} %get-tuple-element.136), channel_id=1, source_target_pairs={{0,1},{1,2},{2,3},{3,0},{4,5},{5,6},{6,7},{7,4},{8,9},{9,10},{10,1... | collective-permute-start | bytes 393224 | tf_op jit(solution)/shard_map/ppermute | solution.py:82
  148.8 12.9 %collective-permute-start.34 = (bf16[32,2048]{1,0:T(8,128)(2,1)S(1)}, bf16[32,2048]{1,0:T(8,128)(2,1)S(1)}, u32[]{:S(2)}, u32[]{:S(2)}) collective-permute-start(bf16[32,2048]{1,0:T(8,128)(2,1)S(1)} %get-tuple-element.137), channel_id=1, source_target_pairs={{0,2},{1,3},{2,0},{3,1},{4,6},{5,7},{6,4},{7,5},{8,10},{9,11},{10,... | collective-permute-start | bytes 393224 | tf_op jit(solution)/shard_map/ppermute | solution.py:82
  151.3 10.4 %collective-permute-start.35 = (bf16[32,2048]{1,0:T(8,128)(2,1)S(1)}, bf16[32,2048]{1,0:T(8,128)(2,1)S(1)}, u32[]{:S(2)}, u32[]{:S(2)}) collective-permute-start(bf16[32,2048]{1,0:T(8,128)(2,1)S(1)} %get-tuple-element.138), channel_id=1, source_target_pairs={{0,3},{1,0},{2,1},{3,2},{4,7},{5,4},{6,5},{7,6},{8,11},{9,8},{10,9... | collective-permute-start | bytes 393224 | tf_op jit(solution)/shard_map/ppermute | solution.py:82
  162.5 6.7 %collective-permute-start.36 = (bf16[32,1024]{1,0:T(8,128)(2,1)S(1)}, bf16[32,1024]{1,0:T(8,128)(2,1)S(1)}, u32[]{:S(2)}, u32[]{:S(2)}) collective-permute-start(bf16[32,1024]{1,0:T(8,128)(2,1)S(1)} %get-tuple-element.140), channel_id=1, source_target_pairs={{0,1},{1,2},{2,3},{3,0},{4,5},{5,6},{6,7},{7,4},{8,9},{9,10},{10,1... | collective-permute-start | bytes 196616 | tf_op jit(solution)/shard_map/ppermute | solution.py:82
  165.2 6.4 %collective-permute-start.37 = (bf16[32,1024]{1,0:T(8,128)(2,1)S(1)}, bf16[32,1024]{1,0:T(8,128)(2,1)S(1)}, u32[]{:S(2)}, u32[]{:S(2)}) collective-permute-start(bf16[32,1024]{1,0:T(8,128)(2,1)S(1)} %get-tuple-element.141), channel_id=1, source_target_pairs={{0,2},{1,3},{2,0},{3,1},{4,6},{5,7},{6,4},{7,5},{8,10},{9,11},{10,... | collective-permute-start | bytes 196616 | tf_op jit(solution)/shard_map/ppermute | solution.py:82
  166.4 5.3 %collective-permute-start.38 = (bf16[32,1024]{1,0:T(8,128)(2,1)S(1)}, bf16[32,1024]{1,0:T(8,128)(2,1)S(1)}, u32[]{:S(2)}, u32[]{:S(2)}) collective-permute-start(bf16[32,1024]{1,0:T(8,128)(2,1)S(1)} %get-tuple-element.142), channel_id=1, source_target_pairs={{0,3},{1,0},{2,1},{3,2},{4,7},{5,4},{6,5},{7,6},{8,11},{9,8},{10,9... | collective-permute-start | bytes 196616 | tf_op jit(solution)/shard_map/ppermute | solution.py:82

commit v7 on v6

--- a/solution.py
+++ b/solution.py
@@ -459,9 +459,9 @@
 
     states, rounded, e = tie((states, rounded, e))
     sib_e = [sib(array) for array in e]
-    states, rounded, out_x, query_y, query_x = tie((states, rounded, out_x, query_y, query_x))
+    others = permute(rounded, "ctx", to_far)
+    states, out_x, query_y, query_x = tie((states, out_x, query_y, query_x))
     out_y = swap(out_x)
-    others = permute(rounded, "ctx", to_far)
 
     chip_rows = 2 * rows_local
     share = rows_local // nhead

time: 173 us -> 173 us (level)
  no operation moved by 1% of the time
where the time goes in v7:
time: 173 us
  waiting for transfers between devices  70.2 us (41%)
  starting transfers between devices  38.8 us (22%)
  Pallas kernels  34.8 us (20%)
  local copies, waits for them, and re-layouts  23.4 us (14%)
  other arithmetic  5.4 us (3%)
    ppermute x39, waiting for transfers between devices, permute(): return lax.ppermute(array, axis, pairs)  70.2 us
    ppermute x39, starting transfers between devices, permute(): return lax.ppermute(array, axis, pairs)  38.8 us
    pallas_call x1, Pallas kernels, permuted_plan(): pl.pallas_call(functools.partial(state_kernel, nblocks), out_shape=(jax.S...  17.4 us
    gather x1, local copies, waits for them, and re-layouts, lookup(): jnp.take(embed_table, jnp.clip(offset_ids, 0, embed_table.shape[0] - 1),...  11.4 us
    pallas_call x1, Pallas kernels, permuted_plan(): pl.pallas_call(functools.partial(project_kernel, nhead, steps), out_shape...  9.35 us
    pallas_call x4, Pallas kernels, small_call(): pl.pallas_call(kernel, out_shape=outs, grid_spec=pltpu.PrefetchScalarGrid...  7.51 us
    squeeze x3, local copies, waits for them, and re-layouts, fetched(): lax.dynamic_slice(weight, (k, 0, (core ^ grp) * cols), (1, block, cols))[0]  6.85 us
  transfers between devices with their start and end apart: 39, of which 16 were waited for; matrix products, arithmetic and copies ran while one was open for 15% of the time, Pallas kernels for 19%

profile of v7, /device:TPU:0, one launch (start us, length us, event | category | flops | bytes accessed | tf_op | source)
XLA Modules:
  0.0 172.9 jit_solution(14595700127794840525)
XLA Ops:
  0.0 2.3 %dynamic-slice_bitcast_fusion.2 = bf16[1024,512]{1,0:T(8,128)(2,1)} fusion(bf16[3,1024,1024]{2,1,0:T(8,128)(2,1)} %refs_10_.1, s32[]{:T(128)S(6)} %select_n.115), kind=kLoop, calls=%fused_computation.4 | loop fusion | bytes 2097156 | tf_op jit(solution)/shard_map/squeeze | solution.py:349
  2.8 3.0 %collective-permute-start = (bf16[2,256,1024]{2,1,0:T(8,128)(2,1)}, bf16[2,256,1024]{2,1,0:T(8,128)(2,1)}, u32[]{:S(2)}, u32[]{:S(2)}) collective-permute-start(bf16[2,256,1024]{2,1,0:T(8,128)(2,1)} %refs_0_), channel_id=1, source_target_pairs={{0,1},{1,2},{2,3},{3,0},{4,5},{5,6},{6,7},{7,4},{8,9},{9,10},{10,1... | collective-permute-start | bytes 3145736 | tf_op jit(solution)/shard_map/ppermute | solution.py:82
  5.9 1.5 collective-permute-start.1
  7.4 2.2 %dynamic-slice_bitcast_fusion.1 = bf16[1024,512]{1,0:T(8,128)(2,1)} fusion(bf16[3,1024,1024]{2,1,0:T(8,128)(2,1)} %refs_10_.1, s32[]{:T(128)S(6)} %select_n.115), kind=kLoop, calls=%fused_computation.3 | loop fusion | bytes 2097156 | tf_op jit(solution)/shard_map/squeeze | solution.py:349
  11.2 11.4 %gather_fusion = bf16[512,1024]{1,0:T(8,128)(2,1)} fusion(bf16[8192,1024]{1,0:T(8,128)(2,1)} %param.9, s32[1024]{0:T(1024)S(1)} %pad_clamp_fusion), kind=kCustom, calls=%fused_computation | custom fusion | bytes 2099200 | tf_op jit(solution)/shard_map/jit(_take)/gather | solution.py:326
  22.6 1.6 select_select_fusion
  24.2 0.9 constant_dynamic-slice_fusion.3
  25.1 0.9 copy.14
  27.0 2.3 %dynamic-slice_bitcast_fusion = bf16[1024,512]{1,0:T(8,128)(2,1)} fusion(bf16[3,1024,1024]{2,1,0:T(8,128)(2,1)} %refs_10_.1, s32[]{:T(128)S(6)} %select_n.115), kind=kLoop, calls=%fused_computation.1 | loop fusion | bytes 2097156 | tf_op jit(solution)/shard_map/squeeze | solution.py:349
  29.3 2.2 %collective-permute-done.refs_1_ = bf16[2,256,1024]{2,1,0:T(8,128)(2,1)} collective-permute-done((bf16[2,256,1024]{2,1,0:T(8,128)(2,1)}, bf16[2,256,1024]{2,1,0:T(8,128)(2,1)}, u32[]{:S(2)}, u32[]{:S(2)}) %collective-permute-start) | collective-permute-done | bytes 1048608 | tf_op jit(solution)/shard_map/ppermute | solution.py:82
  31.7 1.6 collective-permute-start.5
  33.2 1.6 collective-permute-start.6
  34.8 0.8 collective-permute-start.7
  36.2 3.2 %collective-permute-done.9 = bf16[4,2,32,1024]{3,2,0,1:T(8,128)(2,1)} collective-permute-done((bf16[4,2,32,1024]{3,2,0,1:T(8,128)(2,1)}, bf16[4,2,32,1024]{3,2,0,1:T(8,128)(2,1)}, u32[]{:S(2)}, u32[]{:S(2)}) %collective-permute-start.9) | collective-permute-done | bytes 524320 | tf_op jit(solution)/shard_map/ppermute | solution.py:82
  39.9 1.3 bitcast_add_fusion
  41.9 16.2 %collective-permute-done.5.refs_14_.refs_18_ = bf16[1024,512]{1,0:T(8,128)(2,1)} collective-permute-done((bf16[1024,512]{1,0:T(8,128)(2,1)}, bf16[1024,512]{1,0:T(8,128)(2,1)}, u32[]{:S(2)}, u32[]{:S(2)}) %collective-permute-start.5) | collective-permute-done | bytes 1048608 | tf_op jit(solution)/shard_map/ppermute | solution.py:82
  58.1 1.9 %collective-permute-done.6.refs_2_ = bf16[2,256,1024]{2,1,0:T(8,128)(2,1)} collective-permute-done((bf16[2,256,1024]{2,1,0:T(8,128)(2,1)}, bf16[2,256,1024]{2,1,0:T(8,128)(2,1)}, u32[]{:S(2)}, u32[]{:S(2)}) %collective-permute-start.6) | collective-permute-done | bytes 1048608 | tf_op jit(solution)/shard_map/ppermute | solution.py:82
  60.7 1.4 collective-permute-start.12
  62.8 22.3 %collective-permute-done.14 = bf16[128,1024]{1,0:T(8,128)(2,1)} collective-permute-done((bf16[128,1024]{1,0:T(8,128)(2,1)S(1)}, bf16[128,1024]{1,0:T(8,128)(2,1)}, u32[]{:S(2)}, u32[]{:S(2)}) %collective-permute-start.14) | collective-permute-done | bytes 262176 | tf_op jit(solution)/shard_map/ppermute | solution.py:82
  85.0 1.1 add.105.refs_0_
  86.3 2.6 %collective-permute-start.23 = (bf16[1024,512]{1,0:T(8,128)(2,1)}, bf16[1024,512]{1,0:T(8,128)(2,1)S(1)}, u32[]{:S(2)}, u32[]{:S(2)}) collective-permute-start(bf16[1024,512]{1,0:T(8,128)(2,1)} %collective-permute-done.11.refs_14_), channel_id=1, source_target_pairs={{0,16},{16,0},{1,17},{17,1},{2,18},{18,2},{3,19},{19,3},{4,20},{20... | collective-permute-start | bytes 3145736 | tf_op jit(solution)/shard_map/ppermute | solution.py:82
  88.9 0.9 collective-permute-start.24
  89.8 0.9 collective-permute-start.16
  90.7 1.4 collective-permute-start.17
  92.1 2.6 %collective-permute-start.18 = (bf16[128,1024]{1,0:T(8,128)(2,1)S(1)}, bf16[128,1024]{1,0:T(8,128)(2,1)}, u32[]{:S(2)}, u32[]{:S(2)}) collective-permute-start(bf16[128,1024]{1,0:T(8,128)(2,1)S(1)} %add.105.refs_0_), channel_id=1, source_target_pairs={{0,3},{1,0},{2,1},{3,2},{4,7},{5,4},{6,5},{7,6},{8,11},{9,8},{10,9... | collective-permute-start | bytes 786440 | tf_op jit(solution)/shard_map/ppermute | solution.py:82
  94.7 17.4 %prompt_state.1 = (f32[2,4,128,128]{3,2,1,0:T(8,128)}, bf16[2,4,128,128]{3,2,1,0:T(8,128)(2,1)}) custom-call(s32[7]{0:T(128)} %stack.74.meta, bf16[2,256,1024]{2,1,0:T(8,128)(2,1)} %refs_0_, bf16[2,256,1024]{2,1,0:T(8,128)(2,1)} %collective-permute-done.refs_1_, bf16[2,256,1024]{2,1,0:T(8,128)(2,1)} %collective-permute-done.6.refs_2_, ...), custom_call_target="tpu_custom_call" | custom-call | flops 8589934592 | bytes 16777216 | tf_op jit(solution)/shard_map/prompt_state/pallas_call | solution.py:425
  112.8 1.3 collective-permute-done.24.far_x
  115.8 0.8 collective-permute-done.19.refs_4_
  116.6 0.9 collective-permute-start.25
  117.6 9.4 %response_rows.1 = (f32[256,1024]{1,0:T(8,128)}, bf16[32,4096]{1,0:T(8,128)(2,1)}) custom-call(s32[7]{0:T(128)} %stack.74.meta, bf16[128,1024]{1,0:T(8,128)(2,1)} %copy-done.5, bf16[128,1024]{1,0:T(8,128)(2,1)} %collective-permute-done.16.refs_1_, bf16[128,1024]{1,0:T(8,128)(2,1)} %collective-permute-done.17.refs_2_, ...), custom_call_target="tpu_custom_call" | custom-call | flops 3221225472 | bytes 14680064 | tf_op jit(solution)/shard_map/response_rows/pallas_call | solution.py:470
  127.0 1.2 copy-done.1
  128.9 1.2 collective-permute-done.26.heads_sib
  130.2 2.9 %near_terms.1 = (f32[32,2048]{1,0:T(8,128)S(1)}, bf16[32,2048]{1,0:T(8,128)(2,1)S(1)}, bf16[32,2048]{1,0:T(8,128)(2,1)S(1)}, bf16[32,2048]{1,0:T(8,128)(2,1)S(1)}) custom-call(s32[6]{0:T(128)S(1)} %stack.79.meta, bf16[128,512]{1,0:T(8,128)(2,1)S(1)} %get-tuple-element.130.heads_own, bf16[128,512]{1,0:T(8,128)(2,1)S(1)} %collective-permute-done.26.heads_sib, ...), custom_call_target="tpu_custom_call" | custom-call | flops 536870912 | bytes 4194304 | tf_op jit(solution)/shard_map/near_terms/pallas_call | solution.py:290
  133.1 2.1 %collective-permute-start.28 = (bf16[32,2048]{1,0:T(8,128)(2,1)S(1)}, bf16[32,2048]{1,0:T(8,128)(2,1)S(1)}, u32[]{:S(2)}, u32[]{:S(2)}) collective-permute-start(bf16[32,2048]{1,0:T(8,128)(2,1)S(1)} %get-tuple-element.127), channel_id=1, source_target_pairs={{0,2},{1,3},{2,0},{3,1},{4,6},{5,7},{6,4},{7,5},{8,10},{9,11},{10,... | collective-permute-start | bytes 393224 | tf_op jit(solution)/shard_map/ppermute | solution.py:82
  135.1 7.2 %collective-permute-done.28.refs_2_ = bf16[32,2048]{1,0:T(8,128)(2,1)S(1)} collective-permute-done((bf16[32,2048]{1,0:T(8,128)(2,1)S(1)}, bf16[32,2048]{1,0:T(8,128)(2,1)S(1)}, u32[]{:S(2)}, u32[]{:S(2)}) %collective-permute-start.28) | collective-permute-done | bytes 131104 | tf_op jit(solution)/shard_map/ppermute | solution.py:82
  142.7 3.5 %collective-permute-start.29 = (bf16[32,2048]{1,0:T(8,128)(2,1)S(1)}, bf16[32,2048]{1,0:T(8,128)(2,1)S(1)}, u32[]{:S(2)}, u32[]{:S(2)}) collective-permute-start(bf16[32,2048]{1,0:T(8,128)(2,1)S(1)} %get-tuple-element.128), channel_id=1, source_target_pairs={{0,3},{1,0},{2,1},{3,2},{4,7},{5,4},{6,5},{7,6},{8,11},{9,8},{10,9... | collective-permute-start | bytes 393224 | tf_op jit(solution)/shard_map/ppermute | solution.py:82
  146.2 2.5 %far_terms.1 = (f32[32,2048]{1,0:T(8,128)S(1)}, bf16[32,2048]{1,0:T(8,128)(2,1)S(1)}, bf16[32,2048]{1,0:T(8,128)(2,1)S(1)}, bf16[32,2048]{1,0:T(8,128)(2,1)S(1)}) custom-call(s32[6]{0:T(128)S(1)} %stack.79.meta, bf16[128,512]{1,0:T(8,128)(2,1)S(1)} %get-tuple-element.130.heads_own, bf16[128,512]{1,0:T(8,128)(2,1)S(1)} %collective-permute-done.26.heads_sib, ...), custom_call_target="tpu_custom_call" | custom-call | flops 536870912 | bytes 4194304 | tf_op jit(solution)/shard_map/far_terms/pallas_call | solution.py:290
  148.8 2.5 %collective-permute-start.34 = (bf16[32,2048]{1,0:T(8,128)(2,1)S(1)}, bf16[32,2048]{1,0:T(8,128)(2,1)S(1)}, u32[]{:S(2)}, u32[]{:S(2)}) collective-permute-start(bf16[32,2048]{1,0:T(8,128)(2,1)S(1)} %get-tuple-element.135), channel_id=1, source_target_pairs={{0,2},{1,3},{2,0},{3,1},{4,6},{5,7},{6,4},{7,5},{8,10},{9,11},{10,... | collective-permute-start | bytes 393224 | tf_op jit(solution)/shard_map/ppermute | solution.py:82
  151.3 1.3 collective-permute-start.35
  152.7 4.4 %collective-permute-done.33.refs_5_ = bf16[32,2048]{1,0:T(8,128)(2,1)S(1)} collective-permute-done((bf16[32,2048]{1,0:T(8,128)(2,1)S(1)}, bf16[32,2048]{1,0:T(8,128)(2,1)S(1)}, u32[]{:S(2)}, u32[]{:S(2)}) %collective-permute-start.33) | collective-permute-done | bytes 131104 | tf_op jit(solution)/shard_map/ppermute | solution.py:82
  157.1 4.6 %collective-permute-done.34.refs_6_ = bf16[32,2048]{1,0:T(8,128)(2,1)S(1)} collective-permute-done((bf16[32,2048]{1,0:T(8,128)(2,1)S(1)}, bf16[32,2048]{1,0:T(8,128)(2,1)S(1)}, u32[]{:S(2)}, u32[]{:S(2)}) %collective-permute-start.34) | collective-permute-done | bytes 131104 | tf_op jit(solution)/shard_map/ppermute | solution.py:82
  161.7 0.8 final_norm.1
  162.5 2.7 %collective-permute-start.36 = (bf16[32,1024]{1,0:T(8,128)(2,1)S(1)}, bf16[32,1024]{1,0:T(8,128)(2,1)S(1)}, u32[]{:S(2)}, u32[]{:S(2)}) collective-permute-start(bf16[32,1024]{1,0:T(8,128)(2,1)S(1)} %get-tuple-element.138), channel_id=1, source_target_pairs={{0,1},{1,2},{2,3},{3,0},{4,5},{5,6},{6,7},{7,4},{8,9},{9,10},{10,1... | collective-permute-start | bytes 196616 | tf_op jit(solution)/shard_map/ppermute | solution.py:82
  165.2 1.1 collective-permute-start.37
  166.4 1.3 collective-permute-start.38
  167.7 1.5 collective-permute-done.36.refs_1_
  169.2 2.4 %collective-permute-done.37.refs_2_ = bf16[32,1024]{1,0:T(8,128)(2,1)S(1)} collective-permute-done((bf16[32,1024]{1,0:T(8,128)(2,1)S(1)}, bf16[32,1024]{1,0:T(8,128)(2,1)S(1)}, u32[]{:S(2)}, u32[]{:S(2)}) %collective-permute-start.37) | collective-permute-done | bytes 65568 | tf_op jit(solution)/shard_map/ppermute | solution.py:82
  171.6 1.3 place.1
  (81 shorter events, 10.1 us)
Async XLA Ops:
  2.3 29.3 %collective-permute-start.3 = (bf16[3,1024,1024]{2,1,0:T(8,128)(2,1)}, bf16[3,1024,1024]{2,1,0:T(8,128)(2,1)}, u32[]{:S(2)}, u32[]{:S(2)}) collective-permute-start(bf16[3,1024,1024]{2,1,0:T(8,128)(2,1)} %refs_10_.1), channel_id=1, source_target_pairs={{0,4},{4,0},{8,12},{12,8},{1,5},{5,1},{9,13},{13,9},{2,6},{6,2},{1... | collective-permute-start | bytes 18874376 | tf_op jit(solution)/shard_map/ppermute | solution.py:82
  2.8 28.9 %collective-permute-start.4 = (bf16[1024,1024]{1,0:T(8,128)(2,1)}, bf16[1024,1024]{1,0:T(8,128)(2,1)}, u32[]{:S(2)}, u32[]{:S(2)}) collective-permute-start(bf16[1024,1024]{1,0:T(8,128)(2,1)} %own.1), channel_id=1, source_target_pairs={{0,4},{4,0},{8,12},{12,8},{1,5},{5,1},{9,13},{13,9},{2,6},{6,2},{1... | collective-permute-start | bytes 6291464 | tf_op jit(solution)/shard_map/ppermute | solution.py:82
  2.8 28.7 %collective-permute-start = (bf16[2,256,1024]{2,1,0:T(8,128)(2,1)}, bf16[2,256,1024]{2,1,0:T(8,128)(2,1)}, u32[]{:S(2)}, u32[]{:S(2)}) collective-permute-start(bf16[2,256,1024]{2,1,0:T(8,128)(2,1)} %refs_0_), channel_id=1, source_target_pairs={{0,1},{1,2},{2,3},{3,0},{4,5},{5,6},{6,7},{7,4},{8,9},{9,10},{10,1... | collective-permute-start | bytes 3145736 | tf_op jit(solution)/shard_map/ppermute | solution.py:82
  5.9 25.8 %collective-permute-start.2 = (bf16[2,256,1024]{2,1,0:T(8,128)(2,1)}, bf16[2,256,1024]{2,1,0:T(8,128)(2,1)}, u32[]{:S(2)}, u32[]{:S(2)}) collective-permute-start(bf16[2,256,1024]{2,1,0:T(8,128)(2,1)} %refs_0_), channel_id=1, source_target_pairs={{0,4},{4,0},{8,12},{12,8},{1,5},{5,1},{9,13},{13,9},{2,6},{6,2},{1... | collective-permute-start | bytes 3145736 | tf_op jit(solution)/shard_map/ppermute | solution.py:82
  5.9 25.8 %collective-permute-start.1 = (bf16[1024,512]{1,0:T(8,128)(2,1)}, bf16[1024,512]{1,0:T(8,128)(2,1)S(1)}, u32[]{:S(2)}, u32[]{:S(2)}) collective-permute-start(bf16[1024,512]{1,0:T(8,128)(2,1)} %dynamic-slice_bitcast_fusion.2), channel_id=1, source_target_pairs={{0,8},{4,12},{8,0},{12,4},{16,28},{20,24},{24,20},{28,16},{1,9},{5... | collective-permute-start | bytes 3145736 | tf_op jit(solution)/shard_map/ppermute | solution.py:82
  11.2 14.8 %copy-start.8 = (s32[128]{0:T(128)S(1)}, s32[128]{0:T(128)}, u32[]{:S(2)}) copy-start(s32[128]{0:T(128)} %param.11) | copy-start | bytes 1540
  22.6 40.1 %copy-start = (bf16[1024,1024]{1,0:T(8,128)(2,1)S(1)}, bf16[1024,1024]{1,0:T(8,128)(2,1)}, u32[]{:S(2)}) copy-start(bf16[1024,1024]{1,0:T(8,128)(2,1)} %own.1) | copy-start | bytes 6291460
  31.7 54.6 %copy-start.4 = (bf16[1024,512]{1,0:T(8,128)(2,1)}, bf16[1024,512]{1,0:T(8,128)(2,1)S(1)}, u32[]{:S(2)}) copy-start(bf16[1024,512]{1,0:T(8,128)(2,1)S(1)} %collective-permute-done.1.refs_12_.refs_16_) | copy-start | bytes 3145732
  31.7 26.4 %collective-permute-start.5 = (bf16[1024,512]{1,0:T(8,128)(2,1)}, bf16[1024,512]{1,0:T(8,128)(2,1)}, u32[]{:S(2)}, u32[]{:S(2)}) collective-permute-start(bf16[1024,512]{1,0:T(8,128)(2,1)} %dynamic-slice_bitcast_fusion.1), channel_id=1, source_target_pairs={{0,8},{4,12},{8,0},{12,4},{16,28},{20,24},{24,20},{28,16},{1,9},{5... | collective-permute-start | bytes 3145736 | tf_op jit(solution)/shard_map/ppermute | solution.py:82
  33.2 26.7 %collective-permute-start.6 = (bf16[2,256,1024]{2,1,0:T(8,128)(2,1)}, bf16[2,256,1024]{2,1,0:T(8,128)(2,1)}, u32[]{:S(2)}, u32[]{:S(2)}) collective-permute-start(bf16[2,256,1024]{2,1,0:T(8,128)(2,1)} %collective-permute-done.refs_1_), channel_id=1, source_target_pairs={{0,1},{1,2},{2,3},{3,0},{4,5},{5,6},{6,7},{7,4},{8,9},{9,10},{10,1... | collective-permute-start | bytes 3145736 | tf_op jit(solution)/shard_map/ppermute | solution.py:82
  34.8 25.2 %collective-permute-start.7 = (bf16[1024,512]{1,0:T(8,128)(2,1)S(1)}, bf16[1024,512]{1,0:T(8,128)(2,1)}, u32[]{:S(2)}, u32[]{:S(2)}) collective-permute-start(bf16[1024,512]{1,0:T(8,128)(2,1)S(1)} %collective-permute-done.1.refs_12_.refs_16_), channel_id=1, source_target_pairs={{0,16},{16,0},{1,17},{17,1},{2,18},{18,2},{3,19},{19,3},{4,20},{20... | collective-permute-start | bytes 3145736 | tf_op jit(solution)/shard_map/ppermute | solution.py:82
  35.6 24.3 %collective-permute-start.8 = (bf16[2,256,1024]{2,1,0:T(8,128)(2,1)}, bf16[2,256,1024]{2,1,0:T(8,128)(2,1)}, u32[]{:S(2)}, u32[]{:S(2)}) collective-permute-start(bf16[2,256,1024]{2,1,0:T(8,128)(2,1)} %collective-permute-done.refs_1_), channel_id=1, source_target_pairs={{0,4},{4,0},{8,12},{12,8},{1,5},{5,1},{9,13},{13,9},{2,6},{6,2},{1... | collective-permute-start | bytes 3145736 | tf_op jit(solution)/shard_map/ppermute | solution.py:82
  35.6 3.7 %collective-permute-start.9 = (bf16[4,2,32,1024]{3,2,0,1:T(8,128)(2,1)}, bf16[4,2,32,1024]{3,2,0,1:T(8,128)(2,1)}, u32[]{:S(2)}, u32[]{:S(2)}) collective-permute-start(bf16[4,2,32,1024]{3,2,0,1:T(8,128)(2,1)} %bitcast.37), channel_id=1, source_target_pairs={{0,4},{4,0},{8,12},{12,8},{1,5},{5,1},{9,13},{13,9},{2,6},{6,2},{1... | collective-permute-start | bytes 1572872 | tf_op jit(solution)/shard_map/ppermute | solution.py:82
  39.4 46.8 %collective-permute-start.11 = (bf16[1024,512]{1,0:T(8,128)(2,1)}, bf16[1024,512]{1,0:T(8,128)(2,1)}, u32[]{:S(2)}, u32[]{:S(2)}) collective-permute-start(bf16[1024,512]{1,0:T(8,128)(2,1)} %dynamic-slice_bitcast_fusion), channel_id=1, source_target_pairs={{0,8},{4,12},{8,0},{12,4},{16,28},{20,24},{24,20},{28,16},{1,9},{5... | collective-permute-start | bytes 3145736 | tf_op jit(solution)/shard_map/ppermute | solution.py:82
  60.0 26.2 %collective-permute-start.10 = (bf16[2,256,1024]{2,1,0:T(8,128)(2,1)}, bf16[2,256,1024]{2,1,0:T(8,128)(2,1)}, u32[]{:S(2)}, u32[]{:S(2)}) collective-permute-start(bf16[2,256,1024]{2,1,0:T(8,128)(2,1)} %collective-permute-done.6.refs_2_), channel_id=1, source_target_pairs={{0,1},{1,2},{2,3},{3,0},{4,5},{5,6},{6,7},{7,4},{8,9},{9,10},{10,1... | collective-permute-start | bytes 3145736 | tf_op jit(solution)/shard_map/ppermute | solution.py:82
  60.7 25.4 %collective-permute-start.12 = (bf16[1024,512]{1,0:T(8,128)(2,1)}, bf16[1024,512]{1,0:T(8,128)(2,1)}, u32[]{:S(2)}, u32[]{:S(2)}) collective-permute-start(bf16[1024,512]{1,0:T(8,128)(2,1)} %collective-permute-done.5.refs_14_.refs_18_), channel_id=1, source_target_pairs={{0,16},{16,0},{1,17},{17,1},{2,18},{18,2},{3,19},{19,3},{4,20},{20... | collective-permute-start | bytes 3145736 | tf_op jit(solution)/shard_map/ppermute | solution.py:82
  62.2 24.0 %collective-permute-start.13 = (bf16[2,256,1024]{2,1,0:T(8,128)(2,1)}, bf16[2,256,1024]{2,1,0:T(8,128)(2,1)}, u32[]{:S(2)}, u32[]{:S(2)}) collective-permute-start(bf16[2,256,1024]{2,1,0:T(8,128)(2,1)} %collective-permute-done.6.refs_2_), channel_id=1, source_target_pairs={{0,4},{4,0},{8,12},{12,8},{1,5},{5,1},{9,13},{13,9},{2,6},{6,2},{1... | collective-permute-start | bytes 3145736 | tf_op jit(solution)/shard_map/ppermute | solution.py:82
  62.2 22.9 %collective-permute-start.14 = (bf16[128,1024]{1,0:T(8,128)(2,1)S(1)}, bf16[128,1024]{1,0:T(8,128)(2,1)}, u32[]{:S(2)}, u32[]{:S(2)}) collective-permute-start(bf16[128,1024]{1,0:T(8,128)(2,1)S(1)} %bitcast.38), channel_id=1, source_target_pairs={{0,8},{4,12},{8,0},{12,4},{1,9},{5,13},{9,1},{13,5},{2,10},{6,14},... | collective-permute-start | bytes 786440 | tf_op jit(solution)/shard_map/ppermute | solution.py:82
  86.1 28.5 %copy-start.5 = (bf16[128,1024]{1,0:T(8,128)(2,1)}, bf16[128,1024]{1,0:T(8,128)(2,1)S(1)}, u32[]{:S(2)}) copy-start(bf16[128,1024]{1,0:T(8,128)(2,1)S(1)} %add.105.refs_0_) | copy-start | bytes 786436
  86.2 5.9 %collective-permute-start.15 = (bf16[2,256,1024]{2,1,0:T(8,128)(2,1)}, bf16[2,256,1024]{2,1,0:T(8,128)(2,1)S(1)}, u32[]{:S(2)}, u32[]{:S(2)}) collective-permute-start(bf16[2,256,1024]{2,1,0:T(8,128)(2,1)} %collective-permute-done.10.refs_3_), channel_id=1, source_target_pairs={{0,4},{4,0},{8,12},{12,8},{1,5},{5,1},{9,13},{13,9},{2,6},{6,2},{1... | collective-permute-start | bytes 3145736 | tf_op jit(solution)/shard_map/ppermute | solution.py:82
  86.3 26.6 %collective-permute-start.23 = (bf16[1024,512]{1,0:T(8,128)(2,1)}, bf16[1024,512]{1,0:T(8,128)(2,1)S(1)}, u32[]{:S(2)}, u32[]{:S(2)}) collective-permute-start(bf16[1024,512]{1,0:T(8,128)(2,1)} %collective-permute-done.11.refs_14_), channel_id=1, source_target_pairs={{0,16},{16,0},{1,17},{17,1},{2,18},{18,2},{3,19},{19,3},{4,20},{20... | collective-permute-start | bytes 3145736 | tf_op jit(solution)/shard_map/ppermute | solution.py:82
  88.9 25.2 %collective-permute-start.24 = (bf16[512,1024]{1,0:T(8,128)(2,1)S(1)}, bf16[512,1024]{1,0:T(8,128)(2,1)S(1)}, u32[]{:S(2)}, u32[]{:S(2)}) collective-permute-start(bf16[512,1024]{1,0:T(8,128)(2,1)S(1)} %constant_dynamic-slice_fusion), channel_id=1, source_target_pairs={{0,8},{4,12},{8,0},{12,4},{1,9},{5,13},{9,1},{13,5},{2,10},{6,14},... | collective-permute-start | bytes 3145736 | tf_op jit(solution)/shard_map/ppermute | solution.py:82
  89.8 22.3 %collective-permute-start.16 = (bf16[128,1024]{1,0:T(8,128)(2,1)S(1)}, bf16[128,1024]{1,0:T(8,128)(2,1)}, u32[]{:S(2)}, u32[]{:S(2)}) collective-permute-start(bf16[128,1024]{1,0:T(8,128)(2,1)S(1)} %add.105.refs_0_), channel_id=1, source_target_pairs={{0,1},{1,2},{2,3},{3,0},{4,5},{5,6},{6,7},{7,4},{8,9},{9,10},{10,1... | collective-permute-start | bytes 786440 | tf_op jit(solution)/shard_map/ppermute | solution.py:82
  90.7 21.4 %collective-permute-start.17 = (bf16[128,1024]{1,0:T(8,128)(2,1)S(1)}, bf16[128,1024]{1,0:T(8,128)(2,1)}, u32[]{:S(2)}, u32[]{:S(2)}) collective-permute-start(bf16[128,1024]{1,0:T(8,128)(2,1)S(1)} %add.105.refs_0_), channel_id=1, source_target_pairs={{0,2},{1,3},{2,0},{3,1},{4,6},{5,7},{6,4},{7,5},{8,10},{9,11},{10,... | collective-permute-start | bytes 786440 | tf_op jit(solution)/shard_map/ppermute | solution.py:82
  92.1 2.6 %copy-start.7 = (bf16[2,256,1024]{2,1,0:T(8,128)(2,1)}, bf16[2,256,1024]{2,1,0:T(8,128)(2,1)S(1)}, u32[]{:S(2)}) copy-start(bf16[2,256,1024]{2,1,0:T(8,128)(2,1)S(1)} %collective-permute-done.15.refs_7_) | copy-start | bytes 3145732
  92.1 20.0 %collective-permute-start.18 = (bf16[128,1024]{1,0:T(8,128)(2,1)S(1)}, bf16[128,1024]{1,0:T(8,128)(2,1)}, u32[]{:S(2)}, u32[]{:S(2)}) collective-permute-start(bf16[128,1024]{1,0:T(8,128)(2,1)S(1)} %add.105.refs_0_), channel_id=1, source_target_pairs={{0,3},{1,0},{2,1},{3,2},{4,7},{5,4},{6,5},{7,6},{8,11},{9,8},{10,9... | collective-permute-start | bytes 786440 | tf_op jit(solution)/shard_map/ppermute | solution.py:82
  112.8 2.3 %copy-start.6 = (bf16[1024,512]{1,0:T(8,128)(2,1)}, bf16[1024,512]{1,0:T(8,128)(2,1)S(1)}, u32[]{:S(2)}) copy-start(bf16[1024,512]{1,0:T(8,128)(2,1)S(1)} %collective-permute-done.23.refs_15_) | copy-start | bytes 3145732
  114.1 28.3 %collective-permute-start.30 = (bf16[512,1024]{1,0:T(8,128)(2,1)S(1)}, bf16[512,1024]{1,0:T(8,128)(2,1)}, u32[]{:S(2)}, u32[]{:S(2)}) collective-permute-start(bf16[512,1024]{1,0:T(8,128)(2,1)S(1)} %collective-permute-done.24.far_x), channel_id=1, source_target_pairs={{0,16},{16,0},{1,17},{17,1},{2,18},{18,2},{3,19},{19,3},{4,20},{20... | collective-permute-start | bytes 3145736 | tf_op jit(solution)/shard_map/ppermute | solution.py:82
  114.6 2.0 %collective-permute-start.19 = (bf16[128,1024]{1,0:T(8,128)(2,1)S(1)}, bf16[128,1024]{1,0:T(8,128)(2,1)}, u32[]{:S(2)}, u32[]{:S(2)}) collective-permute-start(bf16[128,1024]{1,0:T(8,128)(2,1)S(1)} %add.105.refs_0_), channel_id=1, source_target_pairs={{0,4},{4,0},{8,12},{12,8},{1,5},{5,1},{9,13},{13,9},{2,6},{6,2},{1... | collective-permute-start | bytes 786440 | tf_op jit(solution)/shard_map/ppermute | solution.py:82
  114.6 2.9 %collective-permute-start.20 = (bf16[128,1024]{1,0:T(8,128)(2,1)}, bf16[128,1024]{1,0:T(8,128)(2,1)}, u32[]{:S(2)}, u32[]{:S(2)}) collective-permute-start(bf16[128,1024]{1,0:T(8,128)(2,1)} %collective-permute-done.16.refs_1_), channel_id=1, source_target_pairs={{0,4},{4,0},{8,12},{12,8},{1,5},{5,1},{9,13},{13,9},{2,6},{6,2},{1... | collective-permute-start | bytes 786440 | tf_op jit(solution)/shard_map/ppermute | solution.py:82
  115.1 2.4 %collective-permute-start.21 = (bf16[128,1024]{1,0:T(8,128)(2,1)}, bf16[128,1024]{1,0:T(8,128)(2,1)}, u32[]{:S(2)}, u32[]{:S(2)}) collective-permute-start(bf16[128,1024]{1,0:T(8,128)(2,1)} %collective-permute-done.17.refs_2_), channel_id=1, source_target_pairs={{0,4},{4,0},{8,12},{12,8},{1,5},{5,1},{9,13},{13,9},{2,6},{6,2},{1... | collective-permute-start | bytes 786440 | tf_op jit(solution)/shard_map/ppermute | solution.py:82
  115.1 2.5 %collective-permute-start.22 = (bf16[128,1024]{1,0:T(8,128)(2,1)}, bf16[128,1024]{1,0:T(8,128)(2,1)}, u32[]{:S(2)}, u32[]{:S(2)}) collective-permute-start(bf16[128,1024]{1,0:T(8,128)(2,1)} %collective-permute-done.18.refs_3_), channel_id=1, source_target_pairs={{0,4},{4,0},{8,12},{12,8},{1,5},{5,1},{9,13},{13,9},{2,6},{6,2},{1... | collective-permute-start | bytes 786440 | tf_op jit(solution)/shard_map/ppermute | solution.py:82
  115.8 11.2 %copy-start.2 = (f32[2,4,128,128]{3,2,1,0:T(8,128)S(1)}, f32[2,4,128,128]{3,2,1,0:T(8,128)}, u32[]{:S(2)}) copy-start(f32[2,4,128,128]{3,2,1,0:T(8,128)} %get-tuple-element.120.states) | copy-start | bytes 1572868
  116.6 10.4 %collective-permute-start.25 = (bf16[2,4,128,128]{3,2,1,0:T(8,128)(2,1)}, bf16[2,4,128,128]{3,2,1,0:T(8,128)(2,1)S(1)}, u32[]{:S(2)}, u32[]{:S(2)}) collective-permute-start(bf16[2,4,128,128]{3,2,1,0:T(8,128)(2,1)} %get-tuple-element.121), channel_id=1, source_target_pairs={{0,8},{4,12},{8,0},{12,4},{1,9},{5,13},{9,1},{13,5},{2,10},{6,14},... | collective-permute-start | bytes 786440 | tf_op jit(solution)/shard_map/ppermute | solution.py:82
  127.0 1.2 copy-start.1
  128.2 33.5 %copy-start.3 = (bf16[32,4096]{1,0:T(8,128)(2,1)S(1)}, bf16[32,4096]{1,0:T(8,128)(2,1)}, u32[]{:S(2)}) copy-start(bf16[32,4096]{1,0:T(8,128)(2,1)} %get-tuple-element.114.residual) | copy-start | bytes 786436
  128.7 1.4 collective-permute-start.26
  133.1 9.3 %collective-permute-start.28 = (bf16[32,2048]{1,0:T(8,128)(2,1)S(1)}, bf16[32,2048]{1,0:T(8,128)(2,1)S(1)}, u32[]{:S(2)}, u32[]{:S(2)}) collective-permute-start(bf16[32,2048]{1,0:T(8,128)(2,1)S(1)} %get-tuple-element.127), channel_id=1, source_target_pairs={{0,2},{1,3},{2,0},{3,1},{4,6},{5,7},{6,4},{7,5},{8,10},{9,11},{10,... | collective-permute-start | bytes 393224 | tf_op jit(solution)/shard_map/ppermute | solution.py:82
  135.1 11.1 %collective-permute-start.31 = (bf16[512,1024]{1,0:T(8,128)(2,1)S(1)}, bf16[512,1024]{1,0:T(8,128)(2,1)S(1)}, u32[]{:S(2)}, u32[]{:S(2)}) collective-permute-start(bf16[512,1024]{1,0:T(8,128)(2,1)S(1)} %collective-permute-done.24.far_x), channel_id=1, source_target_pairs={{0,4},{4,0},{8,12},{12,8},{1,5},{5,1},{9,13},{13,9},{2,6},{6,2},{1... | collective-permute-start | bytes 3145736 | tf_op jit(solution)/shard_map/ppermute | solution.py:82
  142.4 3.8 %collective-permute-start.32 = (bf16[512,1024]{1,0:T(8,128)(2,1)}, bf16[512,1024]{1,0:T(8,128)(2,1)S(1)}, u32[]{:S(2)}, u32[]{:S(2)}) collective-permute-start(bf16[512,1024]{1,0:T(8,128)(2,1)} %collective-permute-done.30.far_y), channel_id=1, source_target_pairs={{0,4},{4,0},{8,12},{12,8},{1,5},{5,1},{9,13},{13,9},{2,6},{6,2},{1... | collective-permute-start | bytes 3145736 | tf_op jit(solution)/shard_map/ppermute | solution.py:82
  142.4 10.3 %collective-permute-start.27 = (bf16[32,2048]{1,0:T(8,128)(2,1)S(1)}, bf16[32,2048]{1,0:T(8,128)(2,1)S(1)}, u32[]{:S(2)}, u32[]{:S(2)}) collective-permute-start(bf16[32,2048]{1,0:T(8,128)(2,1)S(1)} %get-tuple-element.126), channel_id=1, source_target_pairs={{0,1},{1,2},{2,3},{3,0},{4,5},{5,6},{6,7},{7,4},{8,9},{9,10},{10,1... | collective-permute-start | bytes 393224 | tf_op jit(solution)/shard_map/ppermute | solution.py:82
  142.7 10.0 %collective-permute-start.29 = (bf16[32,2048]{1,0:T(8,128)(2,1)S(1)}, bf16[32,2048]{1,0:T(8,128)(2,1)S(1)}, u32[]{:S(2)}, u32[]{:S(2)}) collective-permute-start(bf16[32,2048]{1,0:T(8,128)(2,1)S(1)} %get-tuple-element.128), channel_id=1, source_target_pairs={{0,3},{1,0},{2,1},{3,2},{4,7},{5,4},{6,5},{7,6},{8,11},{9,8},{10,9... | collective-permute-start | bytes 393224 | tf_op jit(solution)/shard_map/ppermute | solution.py:82
  148.8 8.3 %collective-permute-start.33 = (bf16[32,2048]{1,0:T(8,128)(2,1)S(1)}, bf16[32,2048]{1,0:T(8,128)(2,1)S(1)}, u32[]{:S(2)}, u32[]{:S(2)}) collective-permute-start(bf16[32,2048]{1,0:T(8,128)(2,1)S(1)} %get-tuple-element.134), channel_id=1, source_target_pairs={{0,1},{1,2},{2,3},{3,0},{4,5},{5,6},{6,7},{7,4},{8,9},{9,10},{10,1... | collective-permute-start | bytes 393224 | tf_op jit(solution)/shard_map/ppermute | solution.py:82
  148.8 12.9 %collective-permute-start.34 = (bf16[32,2048]{1,0:T(8,128)(2,1)S(1)}, bf16[32,2048]{1,0:T(8,128)(2,1)S(1)}, u32[]{:S(2)}, u32[]{:S(2)}) collective-permute-start(bf16[32,2048]{1,0:T(8,128)(2,1)S(1)} %get-tuple-element.135), channel_id=1, source_target_pairs={{0,2},{1,3},{2,0},{3,1},{4,6},{5,7},{6,4},{7,5},{8,10},{9,11},{10,... | collective-permute-start | bytes 393224 | tf_op jit(solution)/shard_map/ppermute | solution.py:82
  151.3 10.4 %collective-permute-start.35 = (bf16[32,2048]{1,0:T(8,128)(2,1)S(1)}, bf16[32,2048]{1,0:T(8,128)(2,1)S(1)}, u32[]{:S(2)}, u32[]{:S(2)}) collective-permute-start(bf16[32,2048]{1,0:T(8,128)(2,1)S(1)} %get-tuple-element.136), channel_id=1, source_target_pairs={{0,3},{1,0},{2,1},{3,2},{4,7},{5,4},{6,5},{7,6},{8,11},{9,8},{10,9... | collective-permute-start | bytes 393224 | tf_op jit(solution)/shard_map/ppermute | solution.py:82
  162.5 6.7 %collective-permute-start.36 = (bf16[32,1024]{1,0:T(8,128)(2,1)S(1)}, bf16[32,1024]{1,0:T(8,128)(2,1)S(1)}, u32[]{:S(2)}, u32[]{:S(2)}) collective-permute-start(bf16[32,1024]{1,0:T(8,128)(2,1)S(1)} %get-tuple-element.138), channel_id=1, source_target_pairs={{0,1},{1,2},{2,3},{3,0},{4,5},{5,6},{6,7},{7,4},{8,9},{9,10},{10,1... | collective-permute-start | bytes 196616 | tf_op jit(solution)/shard_map/ppermute | solution.py:82
  165.2 6.4 %collective-permute-start.37 = (bf16[32,1024]{1,0:T(8,128)(2,1)S(1)}, bf16[32,1024]{1,0:T(8,128)(2,1)S(1)}, u32[]{:S(2)}, u32[]{:S(2)}) collective-permute-start(bf16[32,1024]{1,0:T(8,128)(2,1)S(1)} %get-tuple-element.139), channel_id=1, source_target_pairs={{0,2},{1,3},{2,0},{3,1},{4,6},{5,7},{6,4},{7,5},{8,10},{9,11},{10,... | collective-permute-start | bytes 196616 | tf_op jit(solution)/shard_map/ppermute | solution.py:82
  166.4 5.3 %collective-permute-start.38 = (bf16[32,1024]{1,0:T(8,128)(2,1)S(1)}, bf16[32,1024]{1,0:T(8,128)(2,1)S(1)}, u32[]{:S(2)}, u32[]{:S(2)}) collective-permute-start(bf16[32,1024]{1,0:T(8,128)(2,1)S(1)} %get-tuple-element.140), channel_id=1, source_target_pairs={{0,3},{1,0},{2,1},{3,2},{4,7},{5,4},{6,5},{7,6},{8,11},{9,8},{10,9... | collective-permute-start | bytes 196616 | tf_op jit(solution)/shard_map/ppermute | solution.py:82
